TPU v7x, 32 devices: a whole 2x2x4 slice. The times are simulated.
32 devices in a mesh: seq: 8 (over z, y), rep: 4 (over x, core).
Axes of the slice: x: 2, y: 2, z: 4, core: 2. Of those that a mesh axis runs over, the one named last changes fastest.
Arguments:
- hidden: bfloat16 [2048, 4096], P('seq'), may hold values from -6 to 6
- seg_ids: int32 [2048], P('seq'), may hold values from 0 to 3, never falling along the last dimension, each value on 1 to 1024 neighbouring positions
- x_weight: bfloat16 [4096, 4096], P('seq', 'rep'), may hold values from -0.09375 to 0.09375
- bc_weight: bfloat16 [4096, 256], P('seq', 'rep'), may hold values from -0.02734375 to 0.02734375
- dt_weight: bfloat16 [4096, 32], P('seq', 'rep'), may hold values from -0.09375 to 0.09375
- dt_bias: float32 [32], P('rep'), may hold values from -3 to -1.5
- decay_rate: float32 [32], P('rep'), may hold values from 0.0001953125 to 0.5
- skip: float32 [32], P('rep'), may hold values from 0.5 to 1.5
Outputs:
- mixed: bfloat16 [2048, 4096], P('seq', 'rep')
Inputs may be any that keep to these rules, and one draw needn't show every extreme that they name: `seg_ids`: ids never fall; each id covers 1 to 1024 consecutive tokens and some id covers exactly 1024.
All inputs are finite; a program needn't handle non-finite values.
Results may differ from a plain program's by a relative error of at most 0.007.
Values may be sent and summed in bfloat16 or wider, within the bound.
No kernel may reach another device: no remote copies, remote signals or barrier semaphores. Data moves between devices by JAX's collectives and lax.ppermute only.
A program may use at most 192 MiB of HBM per device.

v0:
```python
import jax
import jax.numpy as jnp
from jax import lax
from jax.sharding import PartitionSpec as P

P_SIZE = 128
NS = 128
DOC_MAX = 1024


def passed_along(x, axis, by):
    peers = lax.axis_size(axis)
    pairs = [(i, i + by) for i in range(peers) if 0 <= i + by < peers]
    return lax.ppermute(x, axis, pairs)


def state_read(c_block, state):
    upper_part = state.astype(jnp.bfloat16)
    lower_part = (state - upper_part.astype(jnp.float32)).astype(jnp.bfloat16)
    first = jnp.einsum("tn,hnp->thp", c_block, upper_part, preferred_element_type=jnp.float32)
    second = jnp.einsum("tn,hnp->thp", c_block, lower_part, preferred_element_type=jnp.float32)
    return first + second


def block_step(state, prev_seg, x_block, b_block, c_block, dt_block, rate_block, seg_block):
    count = x_block.shape[0]
    cum = jnp.cumsum(rate_block, axis=0)
    order = jnp.arange(count)
    masked = (order[:, None] >= order[None, :]) & (seg_block[:, None] == seg_block[None, :])
    scores = jnp.dot(c_block, b_block.T, preferred_element_type=jnp.float32)
    cum_heads = cum.T
    gaps = cum_heads[:, :, None] - cum_heads[:, None, :]
    decay = jnp.where(masked[None], jnp.exp(jnp.where(masked[None], gaps, 0.0)), 0.0)
    mixing = (scores[None] * decay * dt_block.T[:, None, :]).astype(jnp.bfloat16)
    diag_part = jnp.einsum("htj,jhp->thp", mixing, x_block, preferred_element_type=jnp.float32)
    keep = (seg_block == prev_seg).astype(jnp.float32)
    factor = jnp.exp(cum) * keep[:, None]
    carried = state_read(c_block, state) * factor[:, :, None]
    last_seg = seg_block[count - 1]
    tail = (
        jnp.exp(cum[count - 1][None, :] - cum)
        * dt_block
        * (seg_block == last_seg).astype(jnp.float32)[:, None]
    )
    loaded = (tail.T[:, :, None] * b_block.astype(jnp.float32)[None]).astype(jnp.bfloat16)
    built = jnp.einsum("hjn,jhp->hnp", loaded, x_block, preferred_element_type=jnp.float32)
    through = jnp.exp(cum[count - 1]) * (last_seg == prev_seg).astype(jnp.float32)
    new_state = built + through[:, None, None] * state
    return (diag_part + carried, new_state, last_seg)


def combine(earlier, later):
    early_state, early_keep, early_first, early_last = earlier
    late_state, late_keep, late_first, late_last = later
    linked = ((early_last == late_first) | (early_last < 0) | (late_first < 0)).astype(jnp.float32)
    passing = late_keep * linked
    return (
        late_state + passing[:, None, None] * early_state,
        early_keep * passing,
        jnp.where(early_first < 0, late_first, early_first),
        jnp.where(late_last < 0, early_last, late_last),
    )


def shards(hidden, seg_ids, x_weight, bc_weight, dt_weight, dt_bias, decay_rate, skip):
    tok_rows = hidden.shape[0]
    heads = dt_bias.shape[0]
    width = x_weight.shape[1]
    x_rows, bc_rows, dt_rows = (
        lax.all_gather(x_weight, "seq", axis=0, tiled=True),
        lax.all_gather(bc_weight, "seq", axis=0, tiled=True),
        lax.all_gather(dt_weight, "seq", axis=0, tiled=True),
    )
    x_total = jnp.dot(hidden, x_rows, preferred_element_type=jnp.float32)
    bc_total = jnp.dot(hidden, bc_rows, preferred_element_type=jnp.float32)
    dt_total = jnp.dot(hidden, dt_rows, preferred_element_type=jnp.float32)
    inputs = x_total.astype(jnp.bfloat16).reshape(tok_rows, heads, P_SIZE)
    maps = lax.all_gather(bc_total.astype(jnp.bfloat16), "rep", axis=1, tiled=True)
    b_all = maps[:, :NS]
    c_all = maps[:, NS:]
    steps = jax.nn.softplus(dt_total + dt_bias)
    rates = -steps * decay_rate
    state = jnp.zeros((heads, NS, P_SIZE), jnp.float32)
    prev_seg = jnp.int32(-1)
    result, state, prev_seg = block_step(
        state, prev_seg, inputs, b_all, c_all, steps, rates, seg_ids
    )
    whole_keep = jnp.exp(jnp.sum(rates, axis=0)) * (seg_ids[0] == seg_ids[tok_rows - 1]).astype(
        jnp.float32
    )
    element = (state, whole_keep, seg_ids[:1], seg_ids[tok_rows - 1 :])
    reach = DOC_MAX // tok_rows + 1
    first_hop = passed_along((element[0], element[1], element[2], element[3]), "seq", 1)
    incoming = first_hop
    for hop in range(reach - 1):
        incoming = combine(
            passed_along((incoming[0], incoming[1], incoming[2], incoming[3]), "seq", 1), first_hop
        )
    state_in = incoming[0]
    tag_in = incoming[3]
    running = jnp.cumsum(rates, axis=0)
    factor = jnp.exp(running) * (seg_ids == tag_in[0]).astype(jnp.float32)[:, None]
    extra = state_read(c_all, state_in) * factor[:, :, None]
    total_out = result + extra + skip[None, :, None] * inputs.astype(jnp.float32)
    return total_out.astype(jnp.bfloat16).reshape(tok_rows, width)


def solution(mesh):
    placed = (
        P("seq", None),
        P("seq"),
        P("seq", "rep"),
        P("seq", "rep"),
        P("seq", "rep"),
        P("rep"),
        P("rep"),
        P("rep"),
    )
    return jax.shard_map(
        shards, mesh=mesh, in_specs=placed, out_specs=P("seq", "rep"), check_vma=False
    )
```

profile of v0, /device:TPU:16, one launch (start us, length us, event | category | flops | bytes accessed | tf_op | source)
XLA Modules:
  0.0 240.3 jit_solution(4764006685819561446)
XLA Ops:
  6.5 0.0 all-gather.2.cloned.1.call-start
  6.5 0.7 all-gather.2.cloned.1.call-update
  7.3 1.4 fusion.33
  8.6 3.4 %collective-permute-start.2 = (s32[1]{0:T(128)}, s32[1]{0:T(128)}, u32[]{:S(2)}, u32[]{:S(2)}) collective-permute-start(s32[1]{0:T(128)} %get-tuple-element.17), channel_id=1, source_target_pairs={{0,4},{4,8},{8,12},{12,16},{16,20},{20,24},{24,28},{1,5},{5,9},{9,... | collective-permute-start | bytes 20 | tf_op jit(solution)/shard_map/ppermute | solution.py:14
  12.7 26.7 %all_gather.15 = bf16[4096,8]{0,1:T(8,128)(2,1)S(1)} all-gather(bf16[512,8]{0,1:T(8,128)(2,1)} %param.12), channel_id=1, replica_groups=mesh['seq'=8,'rep'=4] {'seq'}, dimensions={0}, use_global_device_ids=true | all-gather | bytes 73728 | tf_op jit(solution)/shard_map/all_gather | solution.py:72
  39.4 0.0 copy-done
  39.4 1.5 fusion.26
  40.9 0.0 copy-start.5
  40.9 0.1 compare_select_fusion.1
  41.0 0.6 reduce-window.6
  41.5 0.2 slice_reduce_fusion
  41.7 35.6 %all_gather.13 = bf16[4096,64]{0,1:T(8,128)(2,1)S(1)} all-gather(bf16[512,64]{0,1:T(8,128)(2,1)S(1)} %copy-done.3), channel_id=1, replica_groups=mesh['seq'=8,'rep'=4] {'seq'}, dimensions={0}, use_global_device_ids=true | all-gather | bytes 589824 | tf_op jit(solution)/shard_map/all_gather | solution.py:71
  77.3 0.8 convolution_convert_fusion.1
  78.1 5.4 %all_gather.14 = bf16[256,256]{0,1:T(8,128)(2,1)S(1)} all-gather(bf16[256,64]{0,1:T(8,128)(2,1)S(1)} %convolution_convert_fusion.1), channel_id=1, replica_groups=mesh['seq'=8,'rep'=4] {'rep'}, dimensions={1}, use_global_device_ids=true | all-gather | bytes 163840 | tf_op jit(solution)/shard_map/all_gather | solution.py:78
  83.5 0.0 collective-permute-done.2
  83.5 1.9 collective-permute-start.3
  86.0 4.0 %collective-permute-done.3 = s32[1]{0:T(128)} collective-permute-done((s32[1]{0:T(128)}, s32[1]{0:T(128)}, u32[]{:S(2)}, u32[]{:S(2)}) %collective-permute-start.3) | collective-permute-done | bytes 36 | tf_op jit(solution)/shard_map/ppermute | solution.py:14
  91.2 3.2 %collective-permute-start.4 = (s32[1]{0:T(128)}, s32[1]{0:T(128)}, u32[]{:S(2)}, u32[]{:S(2)}) collective-permute-start(s32[1]{0:T(128)} %select_n.33), channel_id=1, source_target_pairs={{0,4},{4,8},{8,12},{12,16},{16,20},{20,24},{24,28},{1,5},{5,9},{9,... | collective-permute-start | bytes 20 | tf_op jit(solution)/shard_map/ppermute | solution.py:14
  94.4 4.8 %collective-permute-done.4 = s32[1]{0:T(128)} collective-permute-done((s32[1]{0:T(128)}, s32[1]{0:T(128)}, u32[]{:S(2)}, u32[]{:S(2)}) %collective-permute-start.4) | collective-permute-done | bytes 36 | tf_op jit(solution)/shard_map/ppermute | solution.py:14
  100.4 3.2 %collective-permute-start.5 = (s32[1]{0:T(128)}, s32[1]{0:T(128)}, u32[]{:S(2)}, u32[]{:S(2)}) collective-permute-start(s32[1]{0:T(128)} %select_n.34), channel_id=1, source_target_pairs={{0,4},{4,8},{8,12},{12,16},{16,20},{20,24},{24,28},{1,5},{5,9},{9,... | collective-permute-start | bytes 20 | tf_op jit(solution)/shard_map/ppermute | solution.py:14
  103.6 3.2 %collective-permute-done.5 = s32[1]{0:T(128)} collective-permute-done((s32[1]{0:T(128)}, s32[1]{0:T(128)}, u32[]{:S(2)}, u32[]{:S(2)}) %collective-permute-start.5) | collective-permute-done | bytes 36 | tf_op jit(solution)/shard_map/ppermute | solution.py:14
  108.0 3.2 %collective-permute-start.6 = (s32[1]{0:T(128)}, s32[1]{0:T(128)}, u32[]{:S(2)}, u32[]{:S(2)}) collective-permute-start(s32[1]{0:T(128)} %select_n.35), channel_id=1, source_target_pairs={{0,4},{4,8},{8,12},{12,16},{16,20},{20,24},{24,28},{1,5},{5,9},{9,... | collective-permute-start | bytes 20 | tf_op jit(solution)/shard_map/ppermute | solution.py:14
  111.2 3.2 %collective-permute-done.6 = s32[1]{0:T(128)} collective-permute-done((s32[1]{0:T(128)}, s32[1]{0:T(128)}, u32[]{:S(2)}, u32[]{:S(2)}) %collective-permute-start.6) | collective-permute-done | bytes 36 | tf_op jit(solution)/shard_map/ppermute | solution.py:14
  115.6 0.0 copy-done.5
  115.6 0.6 compare_convert_fusion
  116.3 0.7 exponential_multiply_fusion.1
  116.9 0.2 slice_reduce_fusion.1
  117.1 0.1 multiply_multiply_fusion
  117.2 22.6 %all-gather.2.cloned.1.call-done = bf16[4096,1024]{1,0:T(8,128)(2,1)} async-done(((bf16[512,1024]{1,0:T(8,128)(2,1)}), bf16[4096,1024]{1,0:T(8,128)(2,1)}) %all-gather.2.cloned.1.call-update) | async-done | bytes 8388624 | tf_op jit(solution)/shard_map/all_gather | solution.py:70
  139.8 5.7 %convolution_convert_fusion = bf16[256,1024]{1,0:T(8,128)(2,1)S(1)} fusion(bf16[256,4096]{1,0:T(8,128)(2,1)S(1)} %copy-done, bf16[4096,1024]{1,0:T(8,128)(2,1)} %all-gather.2.cloned.1.call-done), kind=kOutput, calls=%fused_computation.6 | convolution fusion | flops 2147745792 | bytes 11010048 | tf_op jit(solution)/shard_map/dot_general | solution.py:74
  145.6 0.2 copy.30
  145.8 0.3 convolution_add_fusion
  146.1 2.4 collective-permute-start
  148.4 13.9 %collective-permute-done = f32[8,128,128]{2,1,0:T(8,128)S(1)} collective-permute-done((f32[8,128,128]{2,1,0:T(8,128)S(1)}, f32[8,128,128]{2,1,0:T(8,128)S(1)}, u32[]{:S(2)}, u32[]{:S(2)}) %collective-permute-start) | collective-permute-done | bytes 524320 | tf_op jit(solution)/shard_map/ppermute | solution.py:14
  162.3 1.9 collective-permute-start.8
  164.2 4.0 %collective-permute-start.7 = (s32[1]{0:T(128)}, s32[1]{0:T(128)}, u32[]{:S(2)}, u32[]{:S(2)}) collective-permute-start(s32[1]{0:T(128)} %get-tuple-element.16), channel_id=1, source_target_pairs={{0,4},{4,8},{8,12},{12,16},{16,20},{20,24},{24,28},{1,5},{5,9},{9,... | collective-permute-start | bytes 20 | tf_op jit(solution)/shard_map/ppermute | solution.py:14
  169.6 1.9 collective-permute-start.1
  171.5 6.3 %collective-permute-done.7 = s32[1]{0:T(128)} collective-permute-done((s32[1]{0:T(128)}, s32[1]{0:T(128)}, u32[]{:S(2)}, u32[]{:S(2)}) %collective-permute-start.7) | collective-permute-done | bytes 36 | tf_op jit(solution)/shard_map/ppermute | solution.py:14
  185.9 0.0 collective-permute-done.1
  185.9 0.0 collective-permute-done.8
  185.9 1.2 multiply_add_fusion.3
  187.1 1.9 collective-permute-start.9
  189.0 12.5 %collective-permute-done.9 = f32[8,128,128]{2,1,0:T(8,128)S(1)} collective-permute-done((f32[8,128,128]{2,1,0:T(8,128)S(1)}, f32[8,128,128]{2,1,0:T(8,128)S(1)}, u32[]{:S(2)}, u32[]{:S(2)}) %collective-permute-start.9) | collective-permute-done | bytes 524320 | tf_op jit(solution)/shard_map/ppermute | solution.py:14
  201.5 0.1 multiply_add_fusion.2
  201.6 1.9 collective-permute-start.10
  203.6 0.9 fusion.16
  204.5 10.7 %collective-permute-done.10 = f32[8,128,128]{2,1,0:T(8,128)S(1)} collective-permute-done((f32[8,128,128]{2,1,0:T(8,128)S(1)}, f32[8,128,128]{2,1,0:T(8,128)S(1)}, u32[]{:S(2)}, u32[]{:S(2)}) %collective-permute-start.10) | collective-permute-done | bytes 524320 | tf_op jit(solution)/shard_map/ppermute | solution.py:14
  215.1 0.1 multiply_add_fusion.1
  215.3 1.9 collective-permute-start.11
  217.2 0.7 fusion.12
  217.9 1.3 fusion.13
  219.2 0.6 exponential_multiply_fusion
  219.8 8.1 %collective-permute-done.11 = f32[8,128,128]{2,1,0:T(8,128)S(1)} collective-permute-done((f32[8,128,128]{2,1,0:T(8,128)S(1)}, f32[8,128,128]{2,1,0:T(8,128)S(1)}, u32[]{:S(2)}, u32[]{:S(2)}) %collective-permute-start.11) | collective-permute-done | bytes 524320 | tf_op jit(solution)/shard_map/ppermute | solution.py:14
  227.8 0.9 subtract_convert_fusion
  228.7 1.1 copy.24
  229.9 0.2 copy.22
  230.1 0.0 copy-start.1
  230.1 0.0 copy-start.9
  230.1 0.3 fusion.19
  230.4 0.3 fusion.21
  230.7 0.6 copy-done.1
  231.3 0.0 copy-done.2
  231.3 1.1 fusion.3
  232.4 1.0 copy.26
  (19 shorter events, 0.1 us)
Async XLA Ops:
  6.5 32.9 %copy-start = (bf16[256,4096]{1,0:T(8,128)(2,1)S(1)}, bf16[256,4096]{1,0:T(8,128)(2,1)}, u32[]{:S(2)}) copy-start(bf16[256,4096]{1,0:T(8,128)(2,1)} %param.8) | copy-start | bytes 6291460
  6.5 34.4 %copy-start.8 = (f32[8]{0:T(128)S(1)}, f32[8]{0:T(128)}, u32[]{:S(2)}) copy-start(f32[8]{0:T(128)} %param.14) | copy-start | bytes 100
  6.5 35.2 %copy-start.3 = (bf16[512,64]{0,1:T(8,128)(2,1)S(1)}, bf16[512,64]{0,1:T(8,128)(2,1)}, u32[]{:S(2)}) copy-start(bf16[512,64]{0,1:T(8,128)(2,1)} %param.11) | copy-start | bytes 196612
  6.5 133.3 %all-gather.2.cloned.1.call-start = ((), (), s32[]{:S(2)}) async-start(), calls=%async_computation | async-start | bytes 9437184 | tf_op jit(solution)/shard_map/all_gather | solution.py:70
  8.6 74.9 %collective-permute-start.2 = (s32[1]{0:T(128)}, s32[1]{0:T(128)}, u32[]{:S(2)}, u32[]{:S(2)}) collective-permute-start(s32[1]{0:T(128)} %get-tuple-element.17), channel_id=1, source_target_pairs={{0,4},{4,8},{8,12},{12,16},{16,20},{20,24},{24,28},{1,5},{5,9},{9,... | collective-permute-start | bytes 20 | tf_op jit(solution)/shard_map/ppermute | solution.py:14
  40.9 74.7 %copy-start.5 = (s32[256]{0:T(256)S(1)}, s32[256]{0:T(256)}, u32[]{:S(2)}) copy-start(s32[256]{0:T(256)} %param.9) | copy-start | bytes 3076
  83.5 6.5 %collective-permute-start.3 = (s32[1]{0:T(128)}, s32[1]{0:T(128)}, u32[]{:S(2)}, u32[]{:S(2)}) collective-permute-start(s32[1]{0:T(128)} %collective-permute-done.2), channel_id=1, source_target_pairs={{0,4},{4,8},{8,12},{12,16},{16,20},{20,24},{24,28},{1,5},{5,9},{9,... | collective-permute-start | bytes 20 | tf_op jit(solution)/shard_map/ppermute | solution.py:14
  91.2 8.0 %collective-permute-start.4 = (s32[1]{0:T(128)}, s32[1]{0:T(128)}, u32[]{:S(2)}, u32[]{:S(2)}) collective-permute-start(s32[1]{0:T(128)} %select_n.33), channel_id=1, source_target_pairs={{0,4},{4,8},{8,12},{12,16},{16,20},{20,24},{24,28},{1,5},{5,9},{9,... | collective-permute-start | bytes 20 | tf_op jit(solution)/shard_map/ppermute | solution.py:14
  100.4 6.4 %collective-permute-start.5 = (s32[1]{0:T(128)}, s32[1]{0:T(128)}, u32[]{:S(2)}, u32[]{:S(2)}) collective-permute-start(s32[1]{0:T(128)} %select_n.34), channel_id=1, source_target_pairs={{0,4},{4,8},{8,12},{12,16},{16,20},{20,24},{24,28},{1,5},{5,9},{9,... | collective-permute-start | bytes 20 | tf_op jit(solution)/shard_map/ppermute | solution.py:14
  108.0 6.4 %collective-permute-start.6 = (s32[1]{0:T(128)}, s32[1]{0:T(128)}, u32[]{:S(2)}, u32[]{:S(2)}) collective-permute-start(s32[1]{0:T(128)} %select_n.35), channel_id=1, source_target_pairs={{0,4},{4,8},{8,12},{12,16},{16,20},{20,24},{24,28},{1,5},{5,9},{9,... | collective-permute-start | bytes 20 | tf_op jit(solution)/shard_map/ppermute | solution.py:14
  146.1 16.3 %collective-permute-start = (f32[8,128,128]{2,1,0:T(8,128)S(1)}, f32[8,128,128]{2,1,0:T(8,128)S(1)}, u32[]{:S(2)}, u32[]{:S(2)}) collective-permute-start(f32[8,128,128]{2,1,0:T(8,128)S(1)} %convolution_add_fusion), channel_id=1, source_target_pairs={{0,4},{4,8},{8,12},{12,16},{16,20},{20,24},{24,28},{1,5},{5,9},{9,... | collective-permute-start | bytes 1572872 | tf_op jit(solution)/shard_map/ppermute | solution.py:14
  162.3 23.6 %collective-permute-start.8 = (f32[8,128,128]{2,1,0:T(8,128)S(1)}, f32[8,128,128]{2,1,0:T(8,128)}, u32[]{:S(2)}, u32[]{:S(2)}) collective-permute-start(f32[8,128,128]{2,1,0:T(8,128)S(1)} %collective-permute-done), channel_id=1, source_target_pairs={{0,4},{4,8},{8,12},{12,16},{16,20},{20,24},{24,28},{1,5},{5,9},{9,... | collective-permute-start | bytes 1572872 | tf_op jit(solution)/shard_map/ppermute | solution.py:14
  164.2 13.5 %collective-permute-start.7 = (s32[1]{0:T(128)}, s32[1]{0:T(128)}, u32[]{:S(2)}, u32[]{:S(2)}) collective-permute-start(s32[1]{0:T(128)} %get-tuple-element.16), channel_id=1, source_target_pairs={{0,4},{4,8},{8,12},{12,16},{16,20},{20,24},{24,28},{1,5},{5,9},{9,... | collective-permute-start | bytes 20 | tf_op jit(solution)/shard_map/ppermute | solution.py:14
  169.6 16.4 %collective-permute-start.1 = (f32[8]{0:T(128)S(1)}, f32[8]{0:T(128)S(1)}, u32[]{:S(2)}, u32[]{:S(2)}) collective-permute-start(f32[8]{0:T(128)S(1)} %exponential_multiply_fusion.2), channel_id=1, source_target_pairs={{0,4},{4,8},{8,12},{12,16},{16,20},{20,24},{24,28},{1,5},{5,9},{9,... | collective-permute-start | bytes 104 | tf_op jit(solution)/shard_map/ppermute | solution.py:14
  187.1 14.4 %collective-permute-start.9 = (f32[8,128,128]{2,1,0:T(8,128)S(1)}, f32[8,128,128]{2,1,0:T(8,128)S(1)}, u32[]{:S(2)}, u32[]{:S(2)}) collective-permute-start(f32[8,128,128]{2,1,0:T(8,128)S(1)} %multiply_add_fusion.3), channel_id=1, source_target_pairs={{0,4},{4,8},{8,12},{12,16},{16,20},{20,24},{24,28},{1,5},{5,9},{9,... | collective-permute-start | bytes 1572872 | tf_op jit(solution)/shard_map/ppermute | solution.py:14
  201.6 13.5 %collective-permute-start.10 = (f32[8,128,128]{2,1,0:T(8,128)S(1)}, f32[8,128,128]{2,1,0:T(8,128)S(1)}, u32[]{:S(2)}, u32[]{:S(2)}) collective-permute-start(f32[8,128,128]{2,1,0:T(8,128)S(1)} %multiply_add_fusion.2), channel_id=1, source_target_pairs={{0,4},{4,8},{8,12},{12,16},{16,20},{20,24},{24,28},{1,5},{5,9},{9,... | collective-permute-start | bytes 1572872 | tf_op jit(solution)/shard_map/ppermute | solution.py:14
  215.3 12.6 %collective-permute-start.11 = (f32[8,128,128]{2,1,0:T(8,128)S(1)}, f32[8,128,128]{2,1,0:T(8,128)S(1)}, u32[]{:S(2)}, u32[]{:S(2)}) collective-permute-start(f32[8,128,128]{2,1,0:T(8,128)S(1)} %multiply_add_fusion.1), channel_id=1, source_target_pairs={{0,4},{4,8},{8,12},{12,16},{16,20},{20,24},{24,28},{1,5},{5,9},{9,... | collective-permute-start | bytes 1572872 | tf_op jit(solution)/shard_map/ppermute | solution.py:14
  230.1 1.2 copy-start.1
  230.1 1.3 copy-start.2
  230.1 1.3 copy-start.4
  230.1 1.2 copy-start.6
  230.1 1.2 copy-start.7
  230.1 1.2 copy-start.9
Sparse Core Ops, SparseCore 0:
  9.5 130.3 all-gather.1
where the time goes:
time: 241 us; the launch traced here: 240 us
  waiting for transfers between devices  90 us (37%)
  blocking collectives  67.7 us (28%)
  starting transfers between devices  30.9 us (13%)
  between operations  29 us (12%)
  matrix products  12 us (5%)
  other arithmetic  5.7 us (2%)
  local copies, waits for them, and re-layouts  4.9 us (2%)
    ppermute x12, waiting for transfers between devices, passed_along(): return lax.ppermute(x, axis, pairs)  66.7 us
    all_gather x1, blocking collectives, shards(): lax.all_gather(bc_weight, 'seq', axis=0, tiled=True)  35.6 us
    ppermute x12, starting transfers between devices, passed_along(): return lax.ppermute(x, axis, pairs)  30.9 us
    all_gather x1, blocking collectives, shards(): lax.all_gather(dt_weight, 'seq', axis=0, tiled=True)  26.7 us
    all_gather x1, waiting for transfers between devices, shards(): lax.all_gather(x_weight, 'seq', axis=0, tiled=True)  22.6 us
    dot_general x1, matrix products, shards(): x_total = jnp.dot(hidden, x_rows, preferred_element_type=jnp.float32)  5.7 us
    all_gather x1, blocking collectives, shards(): lax.all_gather(bc_total.astype(jnp.bfloat16), 'rep', axis=1, tiled=True)  5.42 us
  transfers between devices with their start and end apart: 13, of which 10 were waited for; matrix products, arithmetic and copies ran while one was open for 4% of the time, Pallas kernels for 0%

commit v1 on v0

--- a/solution.py
+++ b/solution.py
@@ -6,6 +6,8 @@
 P_SIZE = 128
 NS = 128
 DOC_MAX = 1024
+LANES = 2
+PLANES = 4
 
 
 def passed_along(x, axis, by):
@@ -62,7 +64,7 @@
     )
 
 
-def shards(hidden, seg_ids, x_weight, bc_weight, dt_weight, dt_bias, decay_rate, skip):
+def gathered_shards(hidden, seg_ids, x_weight, bc_weight, dt_weight, dt_bias, decay_rate, skip):
     tok_rows = hidden.shape[0]
     heads = dt_bias.shape[0]
     width = x_weight.shape[1]
@@ -105,6 +107,164 @@
     return total_out.astype(jnp.bfloat16).reshape(tok_rows, width)
 
 
+def pick(first, one, other):
+    return jnp.where(first, one, other)
+
+
+def split_hi_lo(value):
+    upper = lax.reduce_precision(value, 8, 7)
+    return upper.astype(jnp.bfloat16), (value - upper).astype(jnp.bfloat16)
+
+
+def plane_shards(hidden, seg_ids, x_weight, bc_weight, dt_weight, dt_bias, decay_rate, skip):
+    bf16, f32 = jnp.bfloat16, jnp.float32
+    me = lax.axis_index("seq")
+    lane, plane = me % LANES, me // LANES
+    even = lane == 0
+    core_even = lax.axis_index("rep") % 2 == 0
+    rows, depth = hidden.shape
+    k_rows, cols = x_weight.shape
+    half = cols // 2
+    heads = dt_bias.shape[0]
+    mine_heads = heads // 2
+    map_cols = bc_weight.shape[1]
+
+    def at(p, l):
+        return LANES * p + l
+
+    swap = [(i, i ^ 1) for i in range(LANES * PLANES)]
+    cores = [(i, i ^ 1) for i in range(lax.axis_size("rep"))]
+
+    def shift(by, sources):
+        return [(at(p, l), at(p + by, l)) for p in sources for l in range(LANES)]
+
+    def ring(by):
+        return [(at(p, l), at((p + by) % PLANES, l)) for p in range(PLANES) for l in range(LANES)]
+
+    def send(x, pairs, axis="seq"):
+        return lax.ppermute(x, axis, pairs)
+
+    own = pick(even, x_weight[:, :half], x_weight[:, half:])
+    other = send(pick(even, x_weight[:, half:], x_weight[:, :half]), swap)
+    up_one = [send(w, shift(1, (0, 1, 2))) for w in (own, other)]
+    down_one = [send(w, shift(-1, (1, 2, 3))) for w in (own, other)]
+
+    small = jnp.concatenate([bc_weight, dt_weight], axis=1).T
+    ids_row = jnp.pad(seg_ids.astype(bf16), (0, k_rows - rows))[None]
+    used = map_cols + heads
+    small = jnp.concatenate([small, ids_row, jnp.zeros((80 - used - 1, k_rows), bf16)], axis=0)
+    from_ring = [small] + [send(small, ring(by)) for by in (3, 2, 1)]
+    lane_small = jnp.stack(from_ring)
+    lane_small = lax.dynamic_slice_in_dim(
+        jnp.concatenate([lane_small, lane_small]), PLANES - plane, PLANES, 0
+    )
+    other_small = send(lane_small, swap)
+    all_small = pick(
+        even,
+        jnp.stack([lane_small, other_small], 1),
+        jnp.stack([other_small, lane_small], 1),
+    )
+    weights_small = all_small[:, :, :used].transpose(2, 0, 1, 3).reshape(used, depth)
+    ids = all_small[:, :, used, :rows].astype(jnp.int32)
+    totals = lax.dot_general(
+        hidden, weights_small, (((1,), (1,)), ((), ())), preferred_element_type=f32
+    )
+    dt_hi, dt_lo = split_hi_lo(totals[:, map_cols:])
+    pack = jnp.concatenate([totals[:, :map_cols].astype(bf16), dt_hi, dt_lo], axis=1)
+    pack_other = send(pack, swap)
+    both = pick(even, jnp.stack([pack, pack_other]), jnp.stack([pack_other, pack]))
+    maps = lax.all_gather(both[:, :, :map_cols], "rep", axis=2, tiled=True)
+    b_all, c_all = maps[:, :, :NS], maps[:, :, NS:]
+    dt_total = both[:, :, map_cols : map_cols + heads].astype(f32) + both[
+        :, :, map_cols + heads :
+    ].astype(f32)
+
+    def my_heads(x):
+        return pick(even, x[..., :mine_heads], x[..., mine_heads:])
+
+    steps = jax.nn.softplus(my_heads(dt_total) + my_heads(dt_bias))
+    rates = -steps * my_heads(decay_rate)
+    cum = jnp.cumsum(rates, axis=1)
+    seg = lax.dynamic_index_in_dim(ids, plane, 0, keepdims=False)
+    order = jnp.arange(rows)
+    masked = (order[None, :, None] >= order[None, None, :]) & (seg[:, :, None] == seg[:, None, :])
+    cum_heads = cum.transpose(0, 2, 1)
+    gaps = cum_heads[:, :, :, None] - cum_heads[:, :, None, :]
+    masked = masked[:, None]
+    decay = jnp.where(masked, jnp.exp(jnp.where(masked, gaps, 0.0)), 0.0)
+    scores = jnp.einsum("btn,bjn->btj", c_all, b_all, preferred_element_type=f32)
+    mixing = (scores[:, None] * decay * steps.transpose(0, 2, 1)[:, :, None, :]).astype(bf16)
+    last = seg[:, rows - 1]
+    end = cum[:, rows - 1]
+    tail = jnp.exp(end[:, None] - cum) * steps * (seg == last[:, None]).astype(f32)[:, :, None]
+    loaded = (tail[..., None] * b_all.astype(f32)[:, :, None]).astype(bf16)
+    link = jnp.exp(end[1]) * (last[1] == last[0]).astype(f32)
+    through_plane = jnp.exp(end[0] + end[1])
+    earlier_through = send(through_plane, shift(1, (0, 1, 2)))
+    ends = ids[:, LANES - 1, rows - 1]
+    tag = jnp.where(plane > 0, ends[jnp.maximum(plane - 1, 0)], -1)
+    tag_before = jnp.where(plane > 1, ends[jnp.maximum(plane - 2, 0)], -1)
+    earlier_link = earlier_through * (tag == tag_before).astype(f32)
+    enters = jnp.exp(end[0]) * (last[0] == tag).astype(f32)
+    factor0 = jnp.exp(cum[0]) * (seg[0] == tag).astype(f32)[:, None]
+    factor1 = jnp.exp(cum[1]) * (seg[1] == last[0]).astype(f32)[:, None]
+
+    near = send(pick(core_even, hidden[:, : depth // 2], hidden[:, depth // 2 :]), swap)
+    far = send(near, cores, "rep")
+    partner = pick(
+        core_even,
+        jnp.concatenate([near, far], axis=1),
+        jnp.concatenate([far, near], axis=1),
+    )
+    tokens = pick(
+        even,
+        jnp.concatenate([hidden, partner], axis=0),
+        jnp.concatenate([partner, hidden], axis=0),
+    )
+
+    def part(at_plane, weights):
+        total = None
+        for l, w in zip((lane, 1 - lane), weights):
+            block = lax.dynamic_slice_in_dim(tokens, (LANES * at_plane + l) * k_rows, k_rows, 1)
+            product = jnp.dot(block, w, preferred_element_type=f32)
+            total = product if total is None else total + product
+        return total
+
+    up_two = [send(w, shift(1, (1, 2))) for w in up_one]
+    down_two = [send(w, shift(-1, (1, 2))) for w in down_one]
+    two = [a + b for a, b in zip(up_two, down_two)]
+    three = [send(w, shift(1, (2,)) + shift(-1, (1,))) for w in two]
+    x_total = part(plane, (own, other))
+    x_total = x_total + part(jnp.maximum(plane - 1, 0), up_one)
+    x_total = x_total + part(jnp.minimum(plane + 1, PLANES - 1), down_one)
+    x_total = x_total + part((plane + 2) % PLANES, two)
+    x_total = x_total + part(jnp.where(plane == 0, PLANES - 1, 0), three)
+    inputs = x_total.astype(bf16).reshape(LANES, rows, mine_heads, P_SIZE)
+
+    built = jnp.einsum("bjhn,bjhp->bhnp", loaded, inputs, preferred_element_type=f32)
+    ready = (built[1] + link[:, None, None] * built[0]).astype(bf16)
+    from_one = send(ready, shift(1, (0, 1, 2)))
+    from_two = send(ready, shift(2, (0, 1)))
+    diag = jnp.einsum("bhtj,bjhp->bthp", mixing, inputs, preferred_element_type=f32)
+    local = diag + my_heads(skip)[None, None, :, None] * inputs.astype(f32)
+    carried = jnp.einsum("tn,hnp->thp", c_all[1], built[0].astype(bf16), preferred_element_type=f32)
+    incoming = from_one.astype(f32) + earlier_link[:, None, None] * from_two.astype(f32)
+    entering = incoming.astype(bf16)
+    carry0 = jnp.einsum("tn,hnp->thp", c_all[0], entering, preferred_element_type=f32)
+    carry1 = jnp.einsum("tn,hnp->thp", c_all[1], entering, preferred_element_type=f32)
+    out0 = local[0] + factor0[:, :, None] * carry0
+    out1 = local[1] + factor1[:, :, None] * (carried + enters[None, :, None] * carry1)
+    out0 = out0.astype(bf16).reshape(rows, half)
+    out1 = out1.astype(bf16).reshape(rows, half)
+    swapped = send(pick(even, out1, out0), swap)
+    kept = pick(even, out0, out1)
+    return pick(
+        even,
+        jnp.concatenate([kept, swapped], axis=1),
+        jnp.concatenate([swapped, kept], axis=1),
+    )
+
+
 def solution(mesh):
     placed = (
         P("seq", None),
@@ -116,6 +276,11 @@
         P("rep"),
         P("rep"),
     )
+    by_planes = mesh.shape["seq"] == LANES * PLANES and mesh.shape["rep"] % 2 == 0
     return jax.shard_map(
-        shards, mesh=mesh, in_specs=placed, out_specs=P("seq", "rep"), check_vma=False
-    )
+        plane_shards if by_planes else gathered_shards,
+        mesh=mesh,
+        in_specs=placed,
+        out_specs=P("seq", "rep"),
+        check_vma=False,
+    )

time: 241 us -> 175 us (0.73)
  blocking collectives: 67.7 us -> 6.01 us
  between operations: 29 us -> 3.69 us
  other arithmetic: 5.7 us -> 20.8 us
  starting transfers between devices: 30.9 us -> 44.8 us
  waiting for transfers between devices: 90 us -> 79.5 us
    all_gather x3 -> x1, blocking collectives: 67.7 us -> 6.01 us  [plane_shards(): maps = lax.all_gather(both[:, :, :map_cols], 'rep', axis=2, tiled=True)]
    all_gather x1 -> x0, waiting for transfers between devices: 22.6 us -> none  [shards(): lax.all_gather(x_weight, 'seq', axis=0, tiled=True)]
    ppermute x12 -> x22, starting transfers between devices: 30.9 us -> 44.8 us  [send(): return lax.ppermute(x, axis, pairs)]
    ppermute x12 -> x22, waiting for transfers between devices: 66.7 us -> 79.5 us  [send(): return lax.ppermute(x, axis, pairs)]
    select_n x1 -> x11, other arithmetic: 0.06 us -> 11 us  [pick(): return jnp.where(first, one, other)]
    dot_general x6 -> x14, matrix products: 10.2 us -> 13.5 us  [the longest x10 8.75 us: part(): product = jnp.dot(block, w, preferred_element_type=f32)]
  transfers between devices with their start and end apart: 13 -> 22, of which waited for: 10 -> 12; matrix products, arithmetic and copies ran while one was open for 4% -> 18% of each run, Pallas kernels for 0% -> 0%
where the time goes in v1:
time: 175 us; the launch traced here: 174 us
  waiting for transfers between devices  79.5 us (45%)
  starting transfers between devices  44.8 us (26%)
  other arithmetic  20.8 us (12%)
  matrix products  14.1 us (8%)
  blocking collectives  6.01 us (3%)
  local copies, waits for them, and re-layouts  5.1 us (3%)
  between operations  3.69 us (2%)
    ppermute x22, waiting for transfers between devices, send(): return lax.ppermute(x, axis, pairs)  79.5 us
    ppermute x22, starting transfers between devices, send(): return lax.ppermute(x, axis, pairs)  44.8 us
    select_n x11, other arithmetic, pick(): return jnp.where(first, one, other)  11 us
    dot_general x10, matrix products, part(): product = jnp.dot(block, w, preferred_element_type=f32)  8.75 us
    all_gather x1, blocking collectives, plane_shards(): maps = lax.all_gather(both[:, :, :map_cols], 'rep', axis=2, tiled=True)  6.01 us
  transfers between devices with their start and end apart: 22, of which 12 were waited for; matrix products, arithmetic and copies ran while one was open for 18% of the time, Pallas kernels for 0%

profile of v1, /device:TPU:16, one launch (start us, length us, event | category | flops | bytes accessed | tf_op | source)
XLA Modules:
  0.0 174.1 jit_solution(3875290797101911771)
XLA Ops:
  0.0 2.4 %broadcast_select_fusion.1 = (bf16[512,512]{1,0:T(8,128)(2,1)}, bf16[512,512]{1,0:T(8,128)(2,1)}) fusion(pred[]{:T(512)S(6)} %eq.75, bf16[512,1024]{1,0:T(8,128)(2,1)} %param.10), kind=kLoop, calls=%fused_computation.52 | loop fusion | flops 524288 | bytes 2097153 | tf_op jit(solution)/shard_map/jit(_where)/select_n | solution.py:111
  2.4 3.5 %collective-permute-start.3 = (bf16[512,512]{1,0:T(8,128)(2,1)}, bf16[512,512]{1,0:T(8,128)(2,1)}, u32[]{:S(2)}, u32[]{:S(2)}) collective-permute-start(bf16[512,512]{1,0:T(8,128)(2,1)} %get-tuple-element.13), channel_id=1, source_target_pairs={{0,8},{4,12},{8,16},{12,20},{16,24},{20,28},{1,9},{5,13},{9,17},{1... | collective-permute-start | bytes 1572872 | tf_op jit(solution)/shard_map/ppermute | solution.py:145
  5.9 2.4 %collective-permute-start.5 = (bf16[512,512]{1,0:T(8,128)(2,1)}, bf16[512,512]{1,0:T(8,128)(2,1)}, u32[]{:S(2)}, u32[]{:S(2)}) collective-permute-start(bf16[512,512]{1,0:T(8,128)(2,1)} %get-tuple-element.13), channel_id=1, source_target_pairs={{8,0},{12,4},{16,8},{20,12},{24,16},{28,20},{9,1},{13,5},{17,9},{2... | collective-permute-start | bytes 1572872 | tf_op jit(solution)/shard_map/ppermute | solution.py:145
  8.3 0.7 convert_element_type.100
  9.1 0.9 maximum_bitcast_fusion
  10.0 1.3 collective-permute-start.13
  11.3 3.5 %collective-permute-start.14 = (bf16[80,512]{1,0:T(8,128)(2,1)S(1)}, bf16[80,512]{1,0:T(8,128)(2,1)S(1)}, u32[]{:S(2)}, u32[]{:S(2)}) collective-permute-start(bf16[80,512]{1,0:T(8,128)(2,1)S(1)} %maximum_maximum_fusion), channel_id=1, source_target_pairs={{0,16},{4,20},{8,24},{12,28},{16,0},{20,4},{24,8},{28,12},{1,17},{... | collective-permute-start | bytes 245768 | tf_op jit(solution)/shard_map/ppermute | solution.py:145
  14.9 1.1 slice_select_fusion
  16.0 0.6 broadcast_select_fusion.4
  16.7 7.9 %collective-permute-done.13 = bf16[80,512]{1,0:T(8,128)(2,1)S(1)} collective-permute-done((bf16[80,512]{1,0:T(8,128)(2,1)S(1)}, bf16[80,512]{1,0:T(8,128)(2,1)S(1)}, u32[]{:S(2)}, u32[]{:S(2)}) %collective-permute-start.13) | collective-permute-done | bytes 81952 | tf_op jit(solution)/shard_map/ppermute | solution.py:145
  24.6 1.5 collective-permute-start.2
  26.4 1.5 collective-permute-start
  28.1 0.6 collective-permute-start.16
  28.7 0.6 broadcast_select_fusion.6
  29.3 36.1 %collective-permute-done.16 = bf16[4,80,512]{2,1,0:T(8,128)(2,1)S(1)} collective-permute-done((bf16[4,80,512]{2,1,0:T(8,128)(2,1)S(1)}, bf16[4,80,512]{2,1,0:T(8,128)(2,1)S(1)}, u32[]{:S(2)}, u32[]{:S(2)}) %collective-permute-start.16) | collective-permute-done | bytes 327712 | tf_op jit(solution)/shard_map/ppermute | solution.py:145
  65.6 0.6 copy.41
  66.2 1.3 reshape.197
  67.5 1.8 %convolution_bitcast_fusion.1 = f32[256,72]{0,1:T(8,128)S(1)} fusion(bf16[72,4096]{1,0:T(8,128)(2,1)} %reshape.197, bf16[256,4096]{1,0:T(8,128)(2,1)S(1)} %copy-done), kind=kOutput, calls=%fused_computation.13 | convolution fusion | flops 150994944 | bytes 2760704 | tf_op jit(solution)/shard_map/dot_general | solution.py:169
  69.6 0.7 fusion.63
  70.2 1.6 collective-permute-start.17
  72.1 0.6 constant_dynamic-slice_fusion
  73.3 0.6 compare_convert_fusion
  76.4 0.7 multiply_bitcast_fusion
  77.1 2.4 %reduce-window.6 = f32[2,4,2,128]{3,2,1,0:T(2,128)S(1)} reduce-window(f32[2,4,2,128]{3,2,1,0:T(2,128)S(1)} %reshape.198, f32[]{:T(128)} %constant.78.clone.1), window={size=1x1x1x128 pad=0_0x0_0x0_0x127_0}, to_apply=%region_0.1 | reduce-window | flops 260096 | bytes 16388 | tf_op jit(solution)/shard_map/reduce-window
  80.0 0.8 multiply_reduce_fusion
  80.8 1.9 %collective-permute-start.19 = (f32[4]{0:T(128)S(1)}, f32[4]{0:T(128)S(1)}, u32[]{:S(2)}, u32[]{:S(2)}) collective-permute-start(f32[4]{0:T(128)S(1)} %get-tuple-element.6), channel_id=1, source_target_pairs={{0,8},{4,12},{8,16},{12,20},{16,24},{20,28},{1,9},{5,13},{9,17},{1... | collective-permute-start | bytes 56 | tf_op jit(solution)/shard_map/ppermute | solution.py:145
  82.9 1.9 %collective-permute-start.4 = (bf16[512,512]{1,0:T(8,128)(2,1)}, bf16[512,512]{1,0:T(8,128)(2,1)S(1)}, u32[]{:S(2)}, u32[]{:S(2)}) collective-permute-start(bf16[512,512]{1,0:T(8,128)(2,1)} %collective-permute-done.2), channel_id=1, source_target_pairs={{0,8},{4,12},{8,16},{12,20},{16,24},{20,28},{1,9},{5,13},{9,17},{1... | collective-permute-start | bytes 1572872 | tf_op jit(solution)/shard_map/ppermute | solution.py:145
  84.8 1.5 collective-permute-done.19
  86.3 2.4 %collective-permute-start.6 = (bf16[512,512]{1,0:T(8,128)(2,1)}, bf16[512,512]{1,0:T(8,128)(2,1)S(1)}, u32[]{:S(2)}, u32[]{:S(2)}) collective-permute-start(bf16[512,512]{1,0:T(8,128)(2,1)} %collective-permute-done.2), channel_id=1, source_target_pairs={{8,0},{12,4},{16,8},{20,12},{24,16},{28,20},{9,1},{13,5},{17,9},{2... | collective-permute-start | bytes 1572872 | tf_op jit(solution)/shard_map/ppermute | solution.py:145
  88.9 6.0 %all_gather.3 = bf16[2,256,256]{1,2,0:T(8,128)(2,1)S(1)} all-gather(bf16[2,256,64]{1,2,0:T(8,128)(2,1)S(1)} %slice.187), channel_id=1, replica_groups=mesh['seq'=8,'rep'=4] {'rep'}, dimensions={2}, use_global_device_ids=true | all-gather | bytes 327680 | tf_op jit(solution)/shard_map/all_gather | solution.py:176
  95.0 3.4 %collective-permute-start.7 = (bf16[512,512]{1,0:T(8,128)(2,1)}, bf16[512,512]{1,0:T(8,128)(2,1)S(1)}, u32[]{:S(2)}, u32[]{:S(2)}) collective-permute-start(bf16[512,512]{1,0:T(8,128)(2,1)} %collective-permute-done.3), channel_id=1, source_target_pairs={{8,16},{12,20},{16,24},{20,28},{9,17},{13,21},{17,25},{21,29},{10,... | collective-permute-start | bytes 1572872 | tf_op jit(solution)/shard_map/ppermute | solution.py:145
  98.4 2.5 %collective-permute-start.8 = (bf16[512,512]{1,0:T(8,128)(2,1)}, bf16[512,512]{1,0:T(8,128)(2,1)S(1)}, u32[]{:S(2)}, u32[]{:S(2)}) collective-permute-start(bf16[512,512]{1,0:T(8,128)(2,1)} %collective-permute-done.5), channel_id=1, source_target_pairs={{8,0},{12,4},{16,8},{20,12},{9,1},{13,5},{17,9},{21,13},{10,2},{14... | collective-permute-start | bytes 1572872 | tf_op jit(solution)/shard_map/ppermute | solution.py:145
  100.9 1.9 %collective-permute-start.9 = (bf16[512,512]{1,0:T(8,128)(2,1)S(1)}, bf16[512,512]{1,0:T(8,128)(2,1)S(1)}, u32[]{:S(2)}, u32[]{:S(2)}) collective-permute-start(bf16[512,512]{1,0:T(8,128)(2,1)S(1)} %collective-permute-done.4), channel_id=1, source_target_pairs={{8,16},{12,20},{16,24},{20,28},{9,17},{13,21},{17,25},{21,29},{10,... | collective-permute-start | bytes 1572872 | tf_op jit(solution)/shard_map/ppermute | solution.py:145
  102.8 4.0 %collective-permute-start.10 = (bf16[512,512]{1,0:T(8,128)(2,1)S(1)}, bf16[512,512]{1,0:T(8,128)(2,1)S(1)}, u32[]{:S(2)}, u32[]{:S(2)}) collective-permute-start(bf16[512,512]{1,0:T(8,128)(2,1)S(1)} %collective-permute-done.6), channel_id=1, source_target_pairs={{8,0},{12,4},{16,8},{20,12},{9,1},{13,5},{17,9},{21,13},{10,2},{14... | collective-permute-start | bytes 1572872 | tf_op jit(solution)/shard_map/ppermute | solution.py:145
  106.8 0.6 fusion.46
  107.4 1.1 fusion.37
  108.5 0.6 broadcast_multiply_fusion
  109.1 2.7 %collective-permute-done.7 = bf16[512,512]{1,0:T(8,128)(2,1)S(1)} collective-permute-done((bf16[512,512]{1,0:T(8,128)(2,1)}, bf16[512,512]{1,0:T(8,128)(2,1)S(1)}, u32[]{:S(2)}, u32[]{:S(2)}) %collective-permute-start.7) | collective-permute-done | bytes 524320 | tf_op jit(solution)/shard_map/ppermute | solution.py:145
  111.8 1.6 collective-permute-done.8
  113.6 1.8 %collective-permute-start.11 = (bf16[512,512]{1,0:T(8,128)(2,1)S(1)}, bf16[512,512]{1,0:T(8,128)(2,1)S(1)}, u32[]{:S(2)}, u32[]{:S(2)}) collective-permute-start(bf16[512,512]{1,0:T(8,128)(2,1)S(1)} %add.185), channel_id=1, source_target_pairs={{16,24},{20,28},{8,0},{12,4},{17,25},{21,29},{9,1},{13,5},{18,26},... | collective-permute-start | bytes 1572872 | tf_op jit(solution)/shard_map/ppermute | solution.py:145
  115.4 7.1 %collective-permute-done.9 = bf16[512,512]{1,0:T(8,128)(2,1)S(1)} collective-permute-done((bf16[512,512]{1,0:T(8,128)(2,1)S(1)}, bf16[512,512]{1,0:T(8,128)(2,1)S(1)}, u32[]{:S(2)}, u32[]{:S(2)}) %collective-permute-start.9) | collective-permute-done | bytes 524320 | tf_op jit(solution)/shard_map/ppermute | solution.py:145
  122.5 1.2 collective-permute-done.10
  123.8 2.8 %collective-permute-start.12 = (bf16[512,512]{1,0:T(8,128)(2,1)S(1)}, bf16[512,512]{1,0:T(8,128)(2,1)S(1)}, u32[]{:S(2)}, u32[]{:S(2)}) collective-permute-start(bf16[512,512]{1,0:T(8,128)(2,1)S(1)} %add.188), channel_id=1, source_target_pairs={{16,24},{20,28},{8,0},{12,4},{17,25},{21,29},{9,1},{13,5},{18,26},... | collective-permute-start | bytes 1572872 | tf_op jit(solution)/shard_map/ppermute | solution.py:145
  126.7 2.4 %maximum_select_fusion.1 = bf16[256,4096]{1,0:T(8,128)(2,1)S(1)} fusion(bf16[256,2048]{1,0:T(8,128)(2,1)S(1)} %collective-permute-done.1, bf16[256,2048]{1,0:T(8,128)(2,1)} %collective-permute-done, pred[]{:T(512)S(6)} %eq.76), kind=kLoop, calls=%fused_computation.1 | loop fusion | flops 9437184 | bytes 4194305 | tf_op jit(solution)/shard_map/jit(_where)/select_n | solution.py:111
  129.1 1.8 %maximum_select_fusion = bf16[512,4096]{1,0:T(8,128)(2,1)S(1)} fusion(bf16[256,4096]{1,0:T(8,128)(2,1)S(1)} %maximum_select_fusion.1, bf16[256,4096]{1,0:T(8,128)(2,1)S(1)} %copy-done, pred[]{:T(512)S(6)} %eq.75), kind=kLoop, calls=%fused_computation | loop fusion | flops 18874368 | bytes 8388609 | tf_op jit(solution)/shard_map/jit(_where)/select_n | solution.py:111
  130.9 1.5 fusion.32
  132.9 1.5 fusion.25
  134.4 1.5 fusion.28
  135.9 1.5 fusion.30
  137.3 6.6 %collective-permute-done.12 = bf16[512,512]{1,0:T(8,128)(2,1)S(1)} collective-permute-done((bf16[512,512]{1,0:T(8,128)(2,1)S(1)}, bf16[512,512]{1,0:T(8,128)(2,1)S(1)}, u32[]{:S(2)}, u32[]{:S(2)}) %collective-permute-start.12) | collective-permute-done | bytes 524320 | tf_op jit(solution)/shard_map/ppermute | solution.py:145
  144.4 0.4 convolution_add_fusion.3
  145.3 0.5 fusion.2
  145.9 0.5 fusion.4
  147.1 0.8 fusion.35
  147.9 1.3 collective-permute-start.20
  149.2 4.4 %collective-permute-start.18 = (bf16[4,128,128]{2,1,0:T(8,128)(2,1)}, bf16[4,128,128]{2,1,0:T(8,128)(2,1)S(1)}, u32[]{:S(2)}, u32[]{:S(2)}) collective-permute-start(bf16[4,128,128]{2,1,0:T(8,128)(2,1)} %fusion.35), channel_id=1, source_target_pairs={{0,8},{4,12},{8,16},{12,20},{16,24},{20,28},{1,9},{5,13},{9,17},{1... | collective-permute-start | bytes 393224 | tf_op jit(solution)/shard_map/ppermute | solution.py:145
  153.7 1.5 fusion.3
  155.5 1.6 collective-permute-done.20
  157.0 5.4 %collective-permute-done.18 = bf16[4,128,128]{2,1,0:T(8,128)(2,1)S(1)} collective-permute-done((bf16[4,128,128]{2,1,0:T(8,128)(2,1)}, bf16[4,128,128]{2,1,0:T(8,128)(2,1)S(1)}, u32[]{:S(2)}, u32[]{:S(2)}) %collective-permute-start.18) | collective-permute-done | bytes 131104 | tf_op jit(solution)/shard_map/ppermute | solution.py:145
  162.5 0.8 add_convert_fusion
  163.8 0.9 broadcast_select_fusion.3
  165.0 0.6 collective-permute-start.21
  165.7 7.5 %collective-permute-done.21 = bf16[256,512]{1,0:T(8,128)(2,1)S(1)} collective-permute-done((bf16[256,512]{1,0:T(8,128)(2,1)S(1)}, bf16[256,512]{1,0:T(8,128)(2,1)S(1)}, u32[]{:S(2)}, u32[]{:S(2)}) %collective-permute-start.21) | collective-permute-done | bytes 262176 | tf_op jit(solution)/shard_map/ppermute | solution.py:145
  173.1 0.9 maximum_select_fusion.3
  (84 shorter events, 5.7 us)
Async XLA Ops:
  0.0 14.9 %copy-start = (bf16[256,4096]{1,0:T(8,128)(2,1)S(1)}, bf16[256,4096]{1,0:T(8,128)(2,1)}, u32[]{:S(2)}) copy-start(bf16[256,4096]{1,0:T(8,128)(2,1)} %param.8) | copy-start | bytes 6291460
  0.0 16.0 %copy-start.2 = (f32[8]{0:T(128)S(1)}, f32[8]{0:T(128)}, u32[]{:S(2)}) copy-start(f32[8]{0:T(128)} %param.15) | copy-start | bytes 100
  0.0 16.0 %copy-start.3 = (f32[8]{0:T(128)S(1)}, f32[8]{0:T(128)}, u32[]{:S(2)}) copy-start(f32[8]{0:T(128)} %param.14) | copy-start | bytes 100
  0.0 28.7 %copy-start.4 = (f32[8]{0:T(128)S(1)}, f32[8]{0:T(128)}, u32[]{:S(2)}) copy-start(f32[8]{0:T(128)} %param.13) | copy-start | bytes 100
  2.4 92.5 %collective-permute-start.3 = (bf16[512,512]{1,0:T(8,128)(2,1)}, bf16[512,512]{1,0:T(8,128)(2,1)}, u32[]{:S(2)}, u32[]{:S(2)}) collective-permute-start(bf16[512,512]{1,0:T(8,128)(2,1)} %get-tuple-element.13), channel_id=1, source_target_pairs={{0,8},{4,12},{8,16},{12,20},{16,24},{20,28},{1,9},{5,13},{9,17},{1... | collective-permute-start | bytes 1572872 | tf_op jit(solution)/shard_map/ppermute | solution.py:145
  5.9 92.5 %collective-permute-start.5 = (bf16[512,512]{1,0:T(8,128)(2,1)}, bf16[512,512]{1,0:T(8,128)(2,1)}, u32[]{:S(2)}, u32[]{:S(2)}) collective-permute-start(bf16[512,512]{1,0:T(8,128)(2,1)} %get-tuple-element.13), channel_id=1, source_target_pairs={{8,0},{12,4},{16,8},{20,12},{24,16},{28,20},{9,1},{13,5},{17,9},{2... | collective-permute-start | bytes 1572872 | tf_op jit(solution)/shard_map/ppermute | solution.py:145
  10.0 14.6 %collective-permute-start.13 = (bf16[80,512]{1,0:T(8,128)(2,1)S(1)}, bf16[80,512]{1,0:T(8,128)(2,1)S(1)}, u32[]{:S(2)}, u32[]{:S(2)}) collective-permute-start(bf16[80,512]{1,0:T(8,128)(2,1)S(1)} %maximum_maximum_fusion), channel_id=1, source_target_pairs={{0,24},{4,28},{8,0},{12,4},{16,8},{20,12},{24,16},{28,20},{1,25},{... | collective-permute-start | bytes 245768 | tf_op jit(solution)/shard_map/ppermute | solution.py:145
  11.3 15.1 %collective-permute-start.14 = (bf16[80,512]{1,0:T(8,128)(2,1)S(1)}, bf16[80,512]{1,0:T(8,128)(2,1)S(1)}, u32[]{:S(2)}, u32[]{:S(2)}) collective-permute-start(bf16[80,512]{1,0:T(8,128)(2,1)S(1)} %maximum_maximum_fusion), channel_id=1, source_target_pairs={{0,16},{4,20},{8,24},{12,28},{16,0},{20,4},{24,8},{28,12},{1,17},{... | collective-permute-start | bytes 245768 | tf_op jit(solution)/shard_map/ppermute | solution.py:145
  14.8 13.1 %collective-permute-start.15 = (bf16[80,512]{1,0:T(8,128)(2,1)S(1)}, bf16[80,512]{1,0:T(8,128)(2,1)S(1)}, u32[]{:S(2)}, u32[]{:S(2)}) collective-permute-start(bf16[80,512]{1,0:T(8,128)(2,1)S(1)} %maximum_maximum_fusion), channel_id=1, source_target_pairs={{0,8},{4,12},{8,16},{12,20},{16,24},{20,28},{24,0},{28,4},{1,9},{5... | collective-permute-start | bytes 245768 | tf_op jit(solution)/shard_map/ppermute | solution.py:145
  24.6 58.3 %collective-permute-start.2 = (bf16[512,512]{1,0:T(8,128)(2,1)}, bf16[512,512]{1,0:T(8,128)(2,1)}, u32[]{:S(2)}, u32[]{:S(2)}) collective-permute-start(bf16[512,512]{1,0:T(8,128)(2,1)} %get-tuple-element.14), channel_id=1, source_target_pairs={{0,4},{4,0},{8,12},{12,8},{16,20},{20,16},{24,28},{28,24},{1,5},{5... | collective-permute-start | bytes 1572872 | tf_op jit(solution)/shard_map/ppermute | solution.py:145
  26.4 62.4 %collective-permute-start = (bf16[256,2048]{1,0:T(8,128)(2,1)}, bf16[256,2048]{1,0:T(8,128)(2,1)}, u32[]{:S(2)}, u32[]{:S(2)}) collective-permute-start(bf16[256,2048]{1,0:T(8,128)(2,1)} %slice_select_fusion), channel_id=1, source_target_pairs={{0,4},{4,0},{8,12},{12,8},{16,20},{20,16},{24,28},{28,24},{1,5},{5... | collective-permute-start | bytes 3145736 | tf_op jit(solution)/shard_map/ppermute | solution.py:145
  28.1 37.3 %collective-permute-start.16 = (bf16[4,80,512]{2,1,0:T(8,128)(2,1)S(1)}, bf16[4,80,512]{2,1,0:T(8,128)(2,1)S(1)}, u32[]{:S(2)}, u32[]{:S(2)}) collective-permute-start(bf16[4,80,512]{2,1,0:T(8,128)(2,1)S(1)} %constant_dynamic-slice_fusion.3), channel_id=1, source_target_pairs={{0,4},{4,0},{8,12},{12,8},{16,20},{20,16},{24,28},{28,24},{1,5},{5... | collective-permute-start | bytes 983048 | tf_op jit(solution)/shard_map/ppermute | solution.py:145
  70.2 6.1 %collective-permute-start.17 = (bf16[256,80]{0,1:T(8,128)(2,1)S(1)}, bf16[256,80]{0,1:T(8,128)(2,1)S(1)}, u32[]{:S(2)}, u32[]{:S(2)}) collective-permute-start(bf16[256,80]{0,1:T(8,128)(2,1)S(1)} %get-tuple-element.18), channel_id=1, source_target_pairs={{0,4},{4,0},{8,12},{12,8},{16,20},{20,16},{24,28},{28,24},{1,5},{5... | collective-permute-start | bytes 122888 | tf_op jit(solution)/shard_map/ppermute | solution.py:145
  80.8 5.5 %collective-permute-start.19 = (f32[4]{0:T(128)S(1)}, f32[4]{0:T(128)S(1)}, u32[]{:S(2)}, u32[]{:S(2)}) collective-permute-start(f32[4]{0:T(128)S(1)} %get-tuple-element.6), channel_id=1, source_target_pairs={{0,8},{4,12},{8,16},{12,20},{16,24},{20,28},{1,9},{5,13},{9,17},{1... | collective-permute-start | bytes 56 | tf_op jit(solution)/shard_map/ppermute | solution.py:145
  82.9 18.0 %collective-permute-start.4 = (bf16[512,512]{1,0:T(8,128)(2,1)}, bf16[512,512]{1,0:T(8,128)(2,1)S(1)}, u32[]{:S(2)}, u32[]{:S(2)}) collective-permute-start(bf16[512,512]{1,0:T(8,128)(2,1)} %collective-permute-done.2), channel_id=1, source_target_pairs={{0,8},{4,12},{8,16},{12,20},{16,24},{20,28},{1,9},{5,13},{9,17},{1... | collective-permute-start | bytes 1572872 | tf_op jit(solution)/shard_map/ppermute | solution.py:145
  86.3 16.5 %collective-permute-start.6 = (bf16[512,512]{1,0:T(8,128)(2,1)}, bf16[512,512]{1,0:T(8,128)(2,1)S(1)}, u32[]{:S(2)}, u32[]{:S(2)}) collective-permute-start(bf16[512,512]{1,0:T(8,128)(2,1)} %collective-permute-done.2), channel_id=1, source_target_pairs={{8,0},{12,4},{16,8},{20,12},{24,16},{28,20},{9,1},{13,5},{17,9},{2... | collective-permute-start | bytes 1572872 | tf_op jit(solution)/shard_map/ppermute | solution.py:145
  88.7 37.9 %collective-permute-start.1 = (bf16[256,2048]{1,0:T(8,128)(2,1)}, bf16[256,2048]{1,0:T(8,128)(2,1)S(1)}, u32[]{:S(2)}, u32[]{:S(2)}) collective-permute-start(bf16[256,2048]{1,0:T(8,128)(2,1)} %collective-permute-done), channel_id=1, source_target_pairs={{0,1},{1,0},{2,3},{3,2},{4,5},{5,4},{6,7},{7,6},{8,9},{9,8},{10,11... | collective-permute-start | bytes 3145736 | tf_op jit(solution)/shard_map/ppermute | solution.py:145
  95.0 16.8 %collective-permute-start.7 = (bf16[512,512]{1,0:T(8,128)(2,1)}, bf16[512,512]{1,0:T(8,128)(2,1)S(1)}, u32[]{:S(2)}, u32[]{:S(2)}) collective-permute-start(bf16[512,512]{1,0:T(8,128)(2,1)} %collective-permute-done.3), channel_id=1, source_target_pairs={{8,16},{12,20},{16,24},{20,28},{9,17},{13,21},{17,25},{21,29},{10,... | collective-permute-start | bytes 1572872 | tf_op jit(solution)/shard_map/ppermute | solution.py:145
  98.4 15.0 %collective-permute-start.8 = (bf16[512,512]{1,0:T(8,128)(2,1)}, bf16[512,512]{1,0:T(8,128)(2,1)S(1)}, u32[]{:S(2)}, u32[]{:S(2)}) collective-permute-start(bf16[512,512]{1,0:T(8,128)(2,1)} %collective-permute-done.5), channel_id=1, source_target_pairs={{8,0},{12,4},{16,8},{20,12},{9,1},{13,5},{17,9},{21,13},{10,2},{14... | collective-permute-start | bytes 1572872 | tf_op jit(solution)/shard_map/ppermute | solution.py:145
  100.9 21.6 %collective-permute-start.9 = (bf16[512,512]{1,0:T(8,128)(2,1)S(1)}, bf16[512,512]{1,0:T(8,128)(2,1)S(1)}, u32[]{:S(2)}, u32[]{:S(2)}) collective-permute-start(bf16[512,512]{1,0:T(8,128)(2,1)S(1)} %collective-permute-done.4), channel_id=1, source_target_pairs={{8,16},{12,20},{16,24},{20,28},{9,17},{13,21},{17,25},{21,29},{10,... | collective-permute-start | bytes 1572872 | tf_op jit(solution)/shard_map/ppermute | solution.py:145
  102.8 20.9 %collective-permute-start.10 = (bf16[512,512]{1,0:T(8,128)(2,1)S(1)}, bf16[512,512]{1,0:T(8,128)(2,1)S(1)}, u32[]{:S(2)}, u32[]{:S(2)}) collective-permute-start(bf16[512,512]{1,0:T(8,128)(2,1)S(1)} %collective-permute-done.6), channel_id=1, source_target_pairs={{8,0},{12,4},{16,8},{20,12},{9,1},{13,5},{17,9},{21,13},{10,2},{14... | collective-permute-start | bytes 1572872 | tf_op jit(solution)/shard_map/ppermute | solution.py:145
  113.6 31.3 %collective-permute-start.11 = (bf16[512,512]{1,0:T(8,128)(2,1)S(1)}, bf16[512,512]{1,0:T(8,128)(2,1)S(1)}, u32[]{:S(2)}, u32[]{:S(2)}) collective-permute-start(bf16[512,512]{1,0:T(8,128)(2,1)S(1)} %add.185), channel_id=1, source_target_pairs={{16,24},{20,28},{8,0},{12,4},{17,25},{21,29},{9,1},{13,5},{18,26},... | collective-permute-start | bytes 1572872 | tf_op jit(solution)/shard_map/ppermute | solution.py:145
  123.8 20.1 %collective-permute-start.12 = (bf16[512,512]{1,0:T(8,128)(2,1)S(1)}, bf16[512,512]{1,0:T(8,128)(2,1)S(1)}, u32[]{:S(2)}, u32[]{:S(2)}) collective-permute-start(bf16[512,512]{1,0:T(8,128)(2,1)S(1)} %add.188), channel_id=1, source_target_pairs={{16,24},{20,28},{8,0},{12,4},{17,25},{21,29},{9,1},{13,5},{18,26},... | collective-permute-start | bytes 1572872 | tf_op jit(solution)/shard_map/ppermute | solution.py:145
  145.9 7.8 %copy-start.1 = (f32[2,256,256]{2,1,0:T(8,128)S(1)}, f32[2,256,256]{2,1,0:T(8,128)}, u32[]{:S(2)}) copy-start(f32[2,256,256]{2,1,0:T(8,128)} %fusion.37) | copy-start | bytes 1572868
  147.9 9.2 %collective-permute-start.20 = (bf16[4,128,128]{2,1,0:T(8,128)(2,1)}, bf16[4,128,128]{2,1,0:T(8,128)(2,1)S(1)}, u32[]{:S(2)}, u32[]{:S(2)}) collective-permute-start(bf16[4,128,128]{2,1,0:T(8,128)(2,1)} %fusion.35), channel_id=1, source_target_pairs={{0,16},{4,20},{8,24},{12,28},{1,17},{5,21},{9,25},{13,29},{2,18},{... | collective-permute-start | bytes 393224 | tf_op jit(solution)/shard_map/ppermute | solution.py:145
  149.2 13.3 %collective-permute-start.18 = (bf16[4,128,128]{2,1,0:T(8,128)(2,1)}, bf16[4,128,128]{2,1,0:T(8,128)(2,1)S(1)}, u32[]{:S(2)}, u32[]{:S(2)}) collective-permute-start(bf16[4,128,128]{2,1,0:T(8,128)(2,1)} %fusion.35), channel_id=1, source_target_pairs={{0,8},{4,12},{8,16},{12,20},{16,24},{20,28},{1,9},{5,13},{9,17},{1... | collective-permute-start | bytes 393224 | tf_op jit(solution)/shard_map/ppermute | solution.py:145
  165.0 8.2 %collective-permute-start.21 = (bf16[256,512]{1,0:T(8,128)(2,1)S(1)}, bf16[256,512]{1,0:T(8,128)(2,1)S(1)}, u32[]{:S(2)}, u32[]{:S(2)}) collective-permute-start(bf16[256,512]{1,0:T(8,128)(2,1)S(1)} %copy.55), channel_id=1, source_target_pairs={{0,4},{4,0},{8,12},{12,8},{16,20},{20,16},{24,28},{28,24},{1,5},{5... | collective-permute-start | bytes 786440 | tf_op jit(solution)/shard_map/ppermute | solution.py:145

commit v2 on v0

--- a/solution.py
+++ b/solution.py
@@ -1,11 +1,18 @@
+import functools
+import math
+
 import jax
 import jax.numpy as jnp
 from jax import lax
+from jax.experimental import pallas as pl
+from jax.experimental.pallas import tpu as pltpu
 from jax.sharding import PartitionSpec as P
 
 P_SIZE = 128
 NS = 128
 DOC_MAX = 1024
+LANES = 2
+PLANES = 4
 
 
 def passed_along(x, axis, by):
@@ -62,7 +69,7 @@
     )
 
 
-def shards(hidden, seg_ids, x_weight, bc_weight, dt_weight, dt_bias, decay_rate, skip):
+def gathered_shards(hidden, seg_ids, x_weight, bc_weight, dt_weight, dt_bias, decay_rate, skip):
     tok_rows = hidden.shape[0]
     heads = dt_bias.shape[0]
     width = x_weight.shape[1]
@@ -105,6 +112,375 @@
     return total_out.astype(jnp.bfloat16).reshape(tok_rows, width)
 
 
+def pick(first, one, other):
+    return jnp.where(first, one, other)
+
+
+def after(x, *earlier):
+    return lax.optimization_barrier((x, *earlier))[0]
+
+
+def call(body, outs, *operands, flops=0, scratch=()):
+    single = not isinstance(outs, list)
+    shapes = [outs] if single else outs
+    size = sum(math.prod(o.shape) * o.dtype.itemsize for o in (*operands, *shapes))
+    result = pl.pallas_call(
+        body,
+        out_shape=shapes,
+        in_specs=[pl.BlockSpec(memory_space=pltpu.SMEM)]
+        + [pl.BlockSpec(memory_space=pltpu.VMEM)] * (len(operands) - 1),
+        out_specs=[pl.BlockSpec(memory_space=pltpu.VMEM)] * len(shapes),
+        scratch_shapes=list(scratch),
+        compiler_params=pltpu.CompilerParams(vmem_limit_bytes=40 * 2**20),
+        cost_estimate=pl.CostEstimate(flops=flops, bytes_accessed=size, transcendentals=0),
+    )(*operands)
+    return result[0] if single else result
+
+
+def contract_last(a, b):
+    return lax.dot_general(a, b, (((1,), (1,)), ((), ())), preferred_element_type=jnp.float32)
+
+
+def mul(a, b):
+    return jnp.dot(a, b, preferred_element_type=jnp.float32)
+
+
+def depth_blocks(place, token_refs, at, size):
+    hidden_ref, near_ref, far_ref = token_refs
+    own = hidden_ref[:, pl.ds(pl.multiple_of(at * size, size), size)]
+    blocks = near_ref.shape[1] // size
+    inside = pl.ds(pl.multiple_of((at % blocks) * size, size), size)
+    is_near = (at // blocks) == place[2]
+    return own, jnp.where(is_near, near_ref[:, inside], far_ref[:, inside])
+
+
+def share_kernel(used, place, hidden, near, far, s0, s1, s2, s3, out):
+    plane, lane = place[0], place[1]
+    rows = hidden.shape[0]
+    size = s0.shape[1]
+    totals = [None, None]
+    for back, s in enumerate((s0, s1, s2, s3)):
+        at = LANES * ((plane + PLANES - back) % PLANES) + lane
+        weights = s[...]
+        for r, tokens in enumerate(depth_blocks(place, (hidden, near, far), at, size)):
+            product = contract_last(weights, tokens)
+            totals[r] = product if totals[r] is None else totals[r] + product
+    row = lax.broadcasted_iota(jnp.int32, (s0.shape[0] - used, rows), 0)
+    ids = s0[used:, :rows].astype(jnp.float32)
+    ends = [s[used:, :rows].astype(jnp.float32)[0:1, rows - 1 : rows] for s in (s1, s2)]
+    notes = jnp.where(row == 1, ends[0], jnp.where(row == 2, ends[1], ids))
+    out[:used, :rows] = totals[0][:used]
+    out[:used, rows:] = totals[1][:used]
+    out[used:, :rows] = notes
+    out[used:, rows:] = jnp.zeros_like(notes)
+
+
+def decay_kernel(
+    map_cols, place, maps, total, bias, rate_of, mixing, loaded, c_out, fac, meta
+):
+    f32, bf16 = jnp.float32, jnp.bfloat16
+    plane, lane = place[0], place[1]
+    heads = bias.shape[0]
+    mine = heads // 2
+    rows = total.shape[1] // 2
+    even = lane == 0
+    pre = total[map_cols : map_cols + heads, :] + bias[...]
+    steps = jnp.maximum(pre, 0.0) + jnp.log1p(jnp.exp(-jnp.abs(pre)))
+    rates = -steps * rate_of[...]
+    steps = jnp.where(even, steps[:mine], steps[mine:])
+    rates = jnp.where(even, rates[:mine], rates[mine:])
+    notes = total[map_cols + heads :, :]
+    tri_row = lax.broadcasted_iota(jnp.int32, (rows, rows), 0)
+    tri_col = lax.broadcasted_iota(jnp.int32, (rows, rows), 1)
+    upper = (tri_row <= tri_col).astype(f32)
+    causal = tri_row >= tri_col
+    pad = jnp.zeros((8 - mine, rows), f32)
+    cums, lasts = [], []
+    for r in range(2):
+        cut = slice(r * rows, (r + 1) * rows)
+        cums.append(
+            lax.dot_general(
+                jnp.concatenate([rates[:, cut], pad], axis=0),
+                upper,
+                (((1,), (0,)), ((), ())),
+                precision=lax.Precision.HIGHEST,
+                preferred_element_type=f32,
+            )
+        )
+        lasts.append(notes[0:1, (r + 1) * rows - 1 : (r + 1) * rows])
+    end = [c[:mine, rows - 1 : rows] for c in cums]
+    end0, end1 = pick(even, end[0], end[1]), pick(even, end[1], end[0])
+    last0, last1 = pick(even, lasts[0], lasts[1]), pick(even, lasts[1], lasts[0])
+    final = pick(even, notes[:, 2 * rows - 1 :], notes[:, rows - 1 : rows])
+    tag = jnp.where(plane > 0, final[1:2], -1.0)
+    tag_before = jnp.where(plane > 1, final[2:3], -1.0)
+    link = jnp.exp(end1) * (last1 == last0).astype(f32)
+    enters = jnp.exp(end0) * (last0 == tag).astype(f32)
+    through = jnp.exp(end0 + end1)
+    passes = (tag == tag_before).astype(f32)
+    width = meta.shape[1] // mine
+    meta[...] = jnp.zeros_like(meta)
+    for h in range(mine):
+        cut = slice(h * width, (h + 1) * width)
+        meta[0:1, cut] = jnp.broadcast_to(link[h : h + 1], (1, width))
+        meta[1:2, cut] = jnp.broadcast_to(enters[h : h + 1], (1, width))
+        meta[2:3, cut] = jnp.broadcast_to(through[h : h + 1], (1, width))
+        meta[3:4, cut] = jnp.broadcast_to(passes, (1, width))
+    for r in range(2):
+        b = lane if r == 0 else 1 - lane
+        cut = slice(r * rows, (r + 1) * rows)
+        seg, cum, dt = notes[0:1, cut], cums[r], steps[:, cut]
+        source = jnp.where(b == 0, tag, last0)
+        factor = jnp.exp(cum) * (seg == source).astype(f32)
+        fac[b] = factor.T
+        cols = jnp.concatenate([cum[:mine], jnp.broadcast_to(seg, (8 - mine, rows))], axis=0).T
+        keep = causal & (cols[:, mine : mine + 1] == seg)
+        b_t, c_t = maps[:NS, cut], maps[NS:, cut]
+        c_rows = c_t.astype(f32).T.astype(bf16)
+        c_out[b] = c_rows
+        scores = mul(c_rows, b_t)
+        tail = jnp.exp(end[r] - cum[:mine]) * dt * (seg == lasts[r]).astype(f32)
+        wide = b_t.astype(f32)
+        for h in range(mine):
+            gap = cols[:, h : h + 1] - cum[h : h + 1]
+            decay = jnp.where(keep, jnp.exp(jnp.where(keep, gap, 0.0)), 0.0)
+            mixing[b, h] = (scores * decay * dt[h : h + 1]).astype(bf16)
+            loaded[b, h] = (wide * tail[h : h + 1]).astype(bf16)
+
+
+def early_kernel(place, hidden, near, far, own, other, uo, up, do, dp, two, out):
+    plane, lane = place[0], place[1]
+    size = own.shape[0]
+    sources = (
+        (plane, own, other),
+        (jnp.maximum(plane - 1, 0), uo, up),
+        (jnp.minimum(plane + 1, PLANES - 1), do, dp),
+        ((plane + 2) % PLANES, two.at[:size], two.at[size:]),
+    )
+    totals = [None, None]
+    for at_plane, w_lane, w_other in sources:
+        for l, w in ((lane, w_lane), (1 - lane, w_other)):
+            weights = w[...]
+            blocks = depth_blocks(place, (hidden, near, far), LANES * at_plane + l, size)
+            for r, tokens in enumerate(blocks):
+                product = mul(tokens, weights)
+                totals[r] = product if totals[r] is None else totals[r] + product
+    out[0] = totals[0]
+    out[1] = totals[1]
+
+
+def input_kernel(place, hidden, near, far, acc, three, loaded, meta, x_out, ready, built_out):
+    f32, bf16 = jnp.float32, jnp.bfloat16
+    plane, lane = place[0], place[1]
+    size = three.shape[0] // 2
+    at_plane = jnp.where(plane == 0, PLANES - 1, 0)
+    totals = [acc[0], acc[1]]
+    for l, w in ((lane, three.at[:size]), (1 - lane, three.at[size:])):
+        weights = w[...]
+        blocks = depth_blocks(place, (hidden, near, far), LANES * at_plane + l, size)
+        for r, tokens in enumerate(blocks):
+            totals[r] = totals[r] + mul(tokens, weights)
+    x_out[lane] = totals[0].astype(bf16)
+    x_out[1 - lane] = totals[1].astype(bf16)
+    mine = loaded.shape[1]
+    width = meta.shape[1] // mine
+    for h in range(mine):
+        cut = slice(h * width, (h + 1) * width)
+        first = mul(loaded[0, h], x_out[0, :, cut])
+        second = mul(loaded[1, h], x_out[1, :, cut])
+        ready[:NS, cut] = (second + meta[0:1, cut] * first).astype(bf16)
+        built_out[:, cut] = first.astype(bf16)
+    through = meta[2:3, :]
+    upper = through.astype(bf16)
+    lower = (through - upper.astype(f32)).astype(bf16)
+    row = lax.broadcasted_iota(jnp.int32, (ready.shape[0] - NS, ready.shape[1]), 0)
+    ready[NS:, :] = jnp.where(
+        row == 0, upper.astype(f32), jnp.where(row == 1, lower.astype(f32), 0.0)
+    ).astype(bf16)
+
+
+def local_kernel(place, x, mixing, skip, c_rows, built, fac, out):
+    lane = place[1]
+    mine = mixing.shape[1]
+    width = x.shape[2] // mine
+    carried = mul(c_rows[1], built[...])
+    gains = jnp.where(lane == 0, skip[:, :mine], skip[:, mine:])
+    for h in range(mine):
+        cut = slice(h * width, (h + 1) * width)
+        for b in range(2):
+            xs = x[b, :, cut]
+            local = mul(mixing[b, h], xs) + gains[:, h : h + 1] * xs.astype(jnp.float32)
+            if b == 1:
+                local = local + fac[1, :, h : h + 1] * carried[:, cut]
+            out[b, :, cut] = local
+
+
+def final_kernel(partner, mine, place, local, c_rows, fac, meta, one, two, out):
+    f32, bf16 = jnp.float32, jnp.bfloat16
+    lane = place[1]
+    b = 1 - lane if partner else lane
+    through = one[NS : NS + 1, :].astype(f32) + one[NS + 1 : NS + 2, :].astype(f32)
+    incoming = one[:NS, :].astype(f32) + (through * meta[3:4, :]) * two[:NS, :].astype(f32)
+    entering = (incoming * jnp.where(b == 1, meta[1:2, :], 1.0)).astype(bf16)
+    carried = mul(c_rows[b], entering)
+    factor = fac[b]
+    width = out.shape[1] // mine
+    for h in range(mine):
+        cut = slice(h * width, (h + 1) * width)
+        out[:, cut] = (local[b, :, cut] + factor[:, h : h + 1] * carried[:, cut]).astype(bf16)
+
+
+def plane_shards(hidden, seg_ids, x_weight, bc_weight, dt_weight, dt_bias, decay_rate, skip):
+    bf16, f32 = jnp.bfloat16, jnp.float32
+    me = lax.axis_index("seq")
+    lane, plane = me % LANES, me // LANES
+    even = lane == 0
+    core = lax.axis_index("rep") % 2
+    place = jnp.stack([plane, lane, core]).astype(jnp.int32)
+    rows, depth = hidden.shape
+    k_rows, cols = x_weight.shape
+    half = cols // 2
+    heads = dt_bias.shape[0]
+    mine = heads // 2
+    map_cols = bc_weight.shape[1]
+    used = map_cols + heads
+
+    def shaped(dtype, *shape):
+        return jax.ShapeDtypeStruct(shape, dtype)
+
+    def at(p, l):
+        return LANES * p + l
+
+    swap = [(i, i ^ 1) for i in range(LANES * PLANES)]
+    cores = [(i, i ^ 1) for i in range(lax.axis_size("rep"))]
+
+    def shift(by, sources):
+        return [(at(p, l), at(p + by, l)) for p in sources for l in range(LANES)]
+
+    def ring(by):
+        return [(at(p, l), at((p + by) % PLANES, l)) for p in range(PLANES) for l in range(LANES)]
+
+    def send(x, pairs, axis="seq"):
+        return lax.ppermute(x, axis, pairs)
+
+    own = pick(even, x_weight[:, :half], x_weight[:, half:])
+    other = send(pick(even, x_weight[:, half:], x_weight[:, :half]), swap)
+    up_own, down_own = send(own, shift(1, (0, 1, 2))), send(own, shift(-1, (1, 2, 3)))
+    up_other, down_other = send(other, shift(1, (0, 1, 2))), send(other, shift(-1, (1, 2, 3)))
+    up_two = send(jnp.concatenate([up_own, up_other]), shift(1, (1, 2)))
+    down_two = send(jnp.concatenate([down_own, down_other]), shift(-1, (1, 2)))
+    two = up_two + down_two
+    three = send(two, shift(1, (2,)) + shift(-1, (1,)))
+
+    near = pick(core == 0, hidden[:, : depth // 2], hidden[:, depth // 2 :])
+    near = send(after(near, other), swap)
+    far = send(near, cores, "rep")
+
+    ids_row = jnp.pad(seg_ids.astype(bf16), (0, k_rows - rows))[None]
+    small = jnp.concatenate(
+        [bc_weight.T, dt_weight.T, ids_row, jnp.zeros((7, k_rows), bf16)], axis=0
+    )
+    from_ring = [small] + [send(small, ring(by)) for by in (1, 2, 3)]
+    share = call(
+        functools.partial(share_kernel, used),
+        shaped(f32, used + 8, LANES * rows),
+        place,
+        hidden,
+        near,
+        far,
+        *from_ring,
+        flops=4 * rows * depth * used,
+    )
+    share_other = send(share, swap)
+    total = share + jnp.concatenate([share_other[:, rows:], share_other[:, :rows]], axis=1)
+    maps = lax.all_gather(total[:map_cols].astype(bf16), "rep", axis=0, tiled=True)
+    mixing, loaded, c_rows, fac, meta = call(
+        functools.partial(decay_kernel, map_cols),
+        [
+            shaped(bf16, LANES, mine, rows, rows),
+            shaped(bf16, LANES, mine, NS, rows),
+            shaped(bf16, LANES, rows, NS),
+            shaped(f32, LANES, rows, 8),
+            shaped(f32, 8, half),
+        ],
+        place,
+        maps,
+        total,
+        dt_bias[:, None],
+        decay_rate[:, None],
+        flops=100 * mine * rows * rows,
+    )
+    early = call(
+        early_kernel,
+        shaped(f32, LANES, rows, half),
+        place,
+        hidden,
+        near,
+        far,
+        own,
+        other,
+        up_own,
+        up_other,
+        down_own,
+        down_other,
+        two,
+        flops=4 * rows * depth * half,
+    )
+    inputs, ready, built = call(
+        input_kernel,
+        [
+            shaped(bf16, LANES, rows, half),
+            shaped(bf16, NS + 16, half),
+            shaped(bf16, NS, half),
+        ],
+        place,
+        hidden,
+        near,
+        far,
+        early,
+        three,
+        loaded,
+        meta,
+        flops=rows * depth * half,
+    )
+    from_one = send(ready, shift(1, (0, 1, 2)))
+    from_two = send(ready, shift(2, (0, 1)))
+    local = call(
+        local_kernel,
+        shaped(f32, LANES, rows, half),
+        place,
+        inputs,
+        mixing,
+        skip[None],
+        c_rows,
+        built,
+        fac,
+        flops=4 * rows * rows * half,
+    )
+
+    def finish(partner):
+        return call(
+            functools.partial(final_kernel, partner, mine),
+            shaped(bf16, rows, half),
+            place,
+            local,
+            c_rows,
+            fac,
+            meta,
+            from_one,
+            from_two,
+            flops=2 * rows * NS * half,
+        )
+
+    swapped = send(finish(True), swap)
+    kept = finish(False)
+    return pick(
+        even,
+        jnp.concatenate([kept, swapped], axis=1),
+        jnp.concatenate([swapped, kept], axis=1),
+    )
+
+
 def solution(mesh):
     placed = (
         P("seq", None),
@@ -116,6 +492,11 @@
         P("rep"),
         P("rep"),
     )
+    by_planes = mesh.shape["seq"] == LANES * PLANES and mesh.shape["rep"] % 2 == 0
     return jax.shard_map(
-        shards, mesh=mesh, in_specs=placed, out_specs=P("seq", "rep"), check_vma=False
-    )
+        plane_shards if by_planes else gathered_shards,
+        mesh=mesh,
+        in_specs=placed,
+        out_specs=P("seq", "rep"),
+        check_vma=False,
+    )

time: 241 us -> 141 us (0.59)
  blocking collectives: 67.7 us -> 5.79 us
  between operations: 29 us -> 0.35 us
  waiting for transfers between devices: 90 us -> 76.6 us
  Pallas kernels: 0 us -> 13.4 us
  matrix products: 12 us -> 0 us
  starting transfers between devices: 30.9 us -> 35.7 us
  local copies, waits for them, and re-layouts: 4.9 us -> 0.34 us
    all_gather x3 -> x1, blocking collectives: 67.7 us -> 5.79 us  [plane_shards(): lax.all_gather(total[:map_cols].astype(bf16), 'rep', axis=0, tiled=True)]
    all_gather x1 -> x0, waiting for transfers between devices: 22.6 us -> none  [shards(): lax.all_gather(x_weight, 'seq', axis=0, tiled=True)]
    pallas_call x0 -> x7, Pallas kernels: none -> 13.4 us  [call(): pl.pallas_call(body, out_shape=shapes, in_specs=[pl.BlockSpec(memory_spac...]
    dot_general x6 -> x0, matrix products: 10.2 us -> none  [the longest x1 5.7 us: shards(): x_total = jnp.dot(hidden, x_rows, preferred_element_type=jnp.float32)]
    ppermute x12 -> x17, waiting for transfers between devices: 66.7 us -> 76.6 us  [send(): return lax.ppermute(x, axis, pairs)]
    ppermute x12 -> x17, starting transfers between devices: 30.9 us -> 35.7 us  [send(): return lax.ppermute(x, axis, pairs)]
    select_n x1 -> x3, other arithmetic: 0.06 us -> 3.26 us  [pick(): return jnp.where(first, one, other)]
  transfers between devices with their start and end apart: 13 -> 17, of which waited for: 10 -> 11; matrix products, arithmetic and copies ran while one was open for 4% -> 2% of each run, Pallas kernels for 0% -> 7%
where the time goes in v2:
time: 141 us; the launch traced here: 138 us
  waiting for transfers between devices  76.6 us (54%)
  starting transfers between devices  35.7 us (25%)
  Pallas kernels  13.4 us (10%)
  other arithmetic  6.11 us (4%)
  blocking collectives  5.79 us (4%)
    ppermute x17, waiting for transfers between devices, send(): return lax.ppermute(x, axis, pairs)  76.6 us
    ppermute x17, starting transfers between devices, send(): return lax.ppermute(x, axis, pairs)  35.7 us
    pallas_call x7, Pallas kernels, call(): pl.pallas_call(body, out_shape=shapes, in_specs=[pl.BlockSpec(memory_spac...  13.4 us
    all_gather x1, blocking collectives, plane_shards(): lax.all_gather(total[:map_cols].astype(bf16), 'rep', axis=0, tiled=True)  5.79 us
    select_n x3, other arithmetic, pick(): return jnp.where(first, one, other)  3.26 us
  transfers between devices with their start and end apart: 17, of which 11 were waited for; matrix products, arithmetic and copies ran while one was open for 2% of the time, Pallas kernels for 7%

profile of v2, /device:TPU:16, one launch (start us, length us, event | category | flops | bytes accessed | tf_op | source)
XLA Modules:
  0.0 138.2 jit_solution(10464621089862081576)
XLA Ops:
  0.0 2.2 %broadcast_select_fusion = (bf16[512,512]{1,0:T(8,128)(2,1)}, bf16[512,512]{1,0:T(8,128)(2,1)S(1)}) fusion(pred[]{:T(512)S(6)} %eq.9, bf16[512,1024]{1,0:T(8,128)(2,1)} %param.10), kind=kLoop, calls=%fused_computation.4 | loop fusion | flops 524288 | bytes 2097153 | tf_op jit(solution)/shard_map/jit(_where)/select_n | solution.py:116
  2.2 1.5 %collective-permute-start = (bf16[512,512]{1,0:T(8,128)(2,1)S(1)}, bf16[512,512]{1,0:T(8,128)(2,1)}, u32[]{:S(2)}, u32[]{:S(2)}) collective-permute-start(bf16[512,512]{1,0:T(8,128)(2,1)S(1)} %get-tuple-element.24), channel_id=1, source_target_pairs={{0,4},{4,0},{8,12},{12,8},{16,20},{20,16},{24,28},{28,24},{1,5},{5... | collective-permute-start | bytes 1572872 | tf_op jit(solution)/shard_map/ppermute | solution.py:364
  3.7 3.5 %collective-permute-start.3 = (bf16[512,512]{1,0:T(8,128)(2,1)}, bf16[512,512]{1,0:T(8,128)(2,1)}, u32[]{:S(2)}, u32[]{:S(2)}) collective-permute-start(bf16[512,512]{1,0:T(8,128)(2,1)} %get-tuple-element.23.own), channel_id=1, source_target_pairs={{0,8},{4,12},{8,16},{12,20},{16,24},{20,28},{1,9},{5,13},{9,17},{1... | collective-permute-start | bytes 1572872 | tf_op jit(solution)/shard_map/ppermute | solution.py:364
  7.2 8.8 %collective-permute-done.other = bf16[512,512]{1,0:T(8,128)(2,1)} collective-permute-done((bf16[512,512]{1,0:T(8,128)(2,1)S(1)}, bf16[512,512]{1,0:T(8,128)(2,1)}, u32[]{:S(2)}, u32[]{:S(2)}) %collective-permute-start) | collective-permute-done | bytes 524320 | tf_op jit(solution)/shard_map/ppermute | solution.py:364
  16.0 3.5 %collective-permute-start.4 = (bf16[512,512]{1,0:T(8,128)(2,1)}, bf16[512,512]{1,0:T(8,128)(2,1)S(1)}, u32[]{:S(2)}, u32[]{:S(2)}) collective-permute-start(bf16[512,512]{1,0:T(8,128)(2,1)} %collective-permute-done.other), channel_id=1, source_target_pairs={{0,8},{4,12},{8,16},{12,20},{16,24},{20,28},{1,9},{5,13},{9,17},{1... | collective-permute-start | bytes 1572872 | tf_op jit(solution)/shard_map/ppermute | solution.py:364
  19.5 0.0 copy-done
  19.5 0.1 slice_select_fusion
  19.6 0.0 copy-start.12
  19.6 1.6 %collective-permute-start.1 = (bf16[256,2048]{1,0:T(8,128)(2,1)S(1)}, bf16[256,2048]{1,0:T(8,128)(2,1)S(1)}, u32[]{:S(2)}, u32[]{:S(2)}) collective-permute-start(bf16[256,2048]{1,0:T(8,128)(2,1)S(1)} %slice_select_fusion), channel_id=1, source_target_pairs={{0,4},{4,0},{8,12},{12,8},{16,20},{20,16},{24,28},{28,24},{1,5},{5... | collective-permute-start | bytes 3145736 | tf_op jit(solution)/shard_map/ppermute | solution.py:364
  21.2 2.3 %collective-permute-start.5 = (bf16[512,512]{1,0:T(8,128)(2,1)}, bf16[512,512]{1,0:T(8,128)(2,1)S(1)}, u32[]{:S(2)}, u32[]{:S(2)}) collective-permute-start(bf16[512,512]{1,0:T(8,128)(2,1)} %get-tuple-element.23.own), channel_id=1, source_target_pairs={{8,0},{12,4},{16,8},{20,12},{24,16},{28,20},{9,1},{13,5},{17,9},{2... | collective-permute-start | bytes 1572872 | tf_op jit(solution)/shard_map/ppermute | solution.py:364
  23.5 2.4 %collective-permute-start.6 = (bf16[512,512]{1,0:T(8,128)(2,1)}, bf16[512,512]{1,0:T(8,128)(2,1)S(1)}, u32[]{:S(2)}, u32[]{:S(2)}) collective-permute-start(bf16[512,512]{1,0:T(8,128)(2,1)} %collective-permute-done.other), channel_id=1, source_target_pairs={{8,0},{12,4},{16,8},{20,12},{24,16},{28,20},{9,1},{13,5},{17,9},{2... | collective-permute-start | bytes 1572872 | tf_op jit(solution)/shard_map/ppermute | solution.py:364
  25.9 0.0 collective-permute-done.3.uo
  25.9 4.9 %collective-permute-done.4.up = bf16[512,512]{1,0:T(8,128)(2,1)S(1)} collective-permute-done((bf16[512,512]{1,0:T(8,128)(2,1)}, bf16[512,512]{1,0:T(8,128)(2,1)S(1)}, u32[]{:S(2)}, u32[]{:S(2)}) %collective-permute-start.4) | collective-permute-done | bytes 524320 | tf_op jit(solution)/shard_map/ppermute | solution.py:364
  30.9 1.3 pad_maximum_fusion
  32.2 3.5 %collective-permute-start.7 = (bf16[1024,512]{1,0:T(8,128)(2,1)S(1)}, bf16[1024,512]{1,0:T(8,128)(2,1)S(1)}, u32[]{:S(2)}, u32[]{:S(2)}) collective-permute-start(bf16[1024,512]{1,0:T(8,128)(2,1)S(1)} %pad_maximum_fusion), channel_id=1, source_target_pairs={{8,16},{12,20},{16,24},{20,28},{9,17},{13,21},{17,25},{21,29},{10,... | collective-permute-start | bytes 3145736 | tf_op jit(solution)/shard_map/ppermute | solution.py:364
  35.7 2.5 %collective-permute-done.5.do = bf16[512,512]{1,0:T(8,128)(2,1)S(1)} collective-permute-done((bf16[512,512]{1,0:T(8,128)(2,1)}, bf16[512,512]{1,0:T(8,128)(2,1)S(1)}, u32[]{:S(2)}, u32[]{:S(2)}) %collective-permute-start.5) | collective-permute-done | bytes 524320 | tf_op jit(solution)/shard_map/ppermute | solution.py:364
  38.1 8.6 %collective-permute-done.6.dp = bf16[512,512]{1,0:T(8,128)(2,1)S(1)} collective-permute-done((bf16[512,512]{1,0:T(8,128)(2,1)}, bf16[512,512]{1,0:T(8,128)(2,1)S(1)}, u32[]{:S(2)}, u32[]{:S(2)}) %collective-permute-start.6) | collective-permute-done | bytes 524320 | tf_op jit(solution)/shard_map/ppermute | solution.py:364
  46.8 0.1 pad_maximum_fusion.1
  46.8 0.0 copy-start.8
  46.8 0.0 copy-start.9
  46.8 0.0 copy-start.10
  46.9 0.0 copy-start.11
  46.9 2.6 %collective-permute-start.8 = (bf16[1024,512]{1,0:T(8,128)(2,1)S(1)}, bf16[1024,512]{1,0:T(8,128)(2,1)S(1)}, u32[]{:S(2)}, u32[]{:S(2)}) collective-permute-start(bf16[1024,512]{1,0:T(8,128)(2,1)S(1)} %pad_maximum_fusion.1), channel_id=1, source_target_pairs={{8,0},{12,4},{16,8},{20,12},{9,1},{13,5},{17,9},{21,13},{10,2},{14... | collective-permute-start | bytes 3145736 | tf_op jit(solution)/shard_map/ppermute | solution.py:364
  49.4 0.0 collective-permute-done.1.near
  49.4 0.1 collective-permute-start.2
  49.5 0.0 copy-done.12
  49.5 0.0 copy-done.1
  49.6 0.1 pad.14.clone
  49.7 7.5 %collective-permute-done.7 = bf16[1024,512]{1,0:T(8,128)(2,1)S(1)} collective-permute-done((bf16[1024,512]{1,0:T(8,128)(2,1)S(1)}, bf16[1024,512]{1,0:T(8,128)(2,1)S(1)}, u32[]{:S(2)}, u32[]{:S(2)}) %collective-permute-start.7) | collective-permute-done | bytes 1048608 | tf_op jit(solution)/shard_map/ppermute | solution.py:364
  57.2 12.2 %collective-permute-done.8 = bf16[1024,512]{1,0:T(8,128)(2,1)S(1)} collective-permute-done((bf16[1024,512]{1,0:T(8,128)(2,1)S(1)}, bf16[1024,512]{1,0:T(8,128)(2,1)S(1)}, u32[]{:S(2)}, u32[]{:S(2)}) %collective-permute-start.8) | collective-permute-done | bytes 1048608 | tf_op jit(solution)/shard_map/ppermute | solution.py:364
  69.4 1.3 add.18.two
  70.7 2.3 %collective-permute-start.9 = (bf16[1024,512]{1,0:T(8,128)(2,1)}, bf16[1024,512]{1,0:T(8,128)(2,1)}, u32[]{:S(2)}, u32[]{:S(2)}) collective-permute-start(bf16[1024,512]{1,0:T(8,128)(2,1)} %add.18.two), channel_id=1, source_target_pairs={{16,24},{20,28},{8,0},{12,4},{17,25},{21,29},{9,1},{13,5},{18,26},... | collective-permute-start | bytes 3145736 | tf_op jit(solution)/shard_map/ppermute | solution.py:364
  73.0 0.1 maximum_maximum_fusion.s0
  73.1 0.1 collective-permute-start.10
  73.1 5.0 %collective-permute-start.11 = (bf16[80,512]{1,0:T(8,128)(2,1)S(1)}, bf16[80,512]{1,0:T(8,128)(2,1)S(1)}, u32[]{:S(2)}, u32[]{:S(2)}) collective-permute-start(bf16[80,512]{1,0:T(8,128)(2,1)S(1)} %maximum_maximum_fusion.s0), channel_id=1, source_target_pairs={{0,16},{4,20},{8,24},{12,28},{16,0},{20,4},{24,8},{28,12},{1,17},{... | collective-permute-start | bytes 245768 | tf_op jit(solution)/shard_map/ppermute | solution.py:364
  78.2 0.0 collective-permute-start.12
  78.2 0.0 copy-done.10
  78.2 0.1 copy.9.bias
  78.2 0.1 copy.10.rate_of
  78.3 0.1 pad_add_fusion.place
  78.4 18.5 %collective-permute-done.10.s1 = bf16[80,512]{1,0:T(8,128)(2,1)S(1)} collective-permute-done((bf16[80,512]{1,0:T(8,128)(2,1)S(1)}, bf16[80,512]{1,0:T(8,128)(2,1)S(1)}, u32[]{:S(2)}, u32[]{:S(2)}) %collective-permute-start.10) | collective-permute-done | bytes 81952 | tf_op jit(solution)/shard_map/ppermute | solution.py:364
  96.9 0.0 collective-permute-done.11.s2
  96.9 0.0 collective-permute-done.12.s3
  96.9 0.0 collective-permute-done.2.far
  96.9 2.0 %shard_map.83 = f32[80,512]{1,0:T(8,128)S(1)} custom-call(s32[3]{0:T(128)S(1)} %pad_add_fusion.place, bf16[256,4096]{1,0:T(8,128)(2,1)S(1)} %copy-done, bf16[256,2048]{1,0:T(8,128)(2,1)S(1)} %collective-permute-done.1.near, bf16[256,2048]{1,0:T(8,128)(2,1)} %collective-permute-done.2.far, bf16[80,512]{1,0:T(8,128)(2,1)S(1)} %maximum_maximum_fusion.s0, ...), custom_call_target="tpu_custom_call" | custom-call | flops 301989888 | bytes 4685836 | tf_op jit(solution)/shard_map/pallas_call | solution.py:127
  98.9 0.6 collective-permute-start.13
  99.5 0.0 copy-done.6
  99.5 4.4 %shard_map.82.acc = f32[2,256,512]{2,1,0:T(8,128)S(1)} custom-call(s32[3]{0:T(128)S(1)} %pad_add_fusion.place, bf16[256,4096]{1,0:T(8,128)(2,1)S(1)} %copy-done, bf16[256,2048]{1,0:T(8,128)(2,1)S(1)} %collective-permute-done.1.near, bf16[256,2048]{1,0:T(8,128)(2,1)} %collective-permute-done.2.far, bf16[512,512]{1,0:T(8,128)(2,1)} %get-tuple-element.23.own, ...), custom_call_target="tpu_custom_call" | custom-call | flops 2147483648 | bytes 9437196 | tf_op jit(solution)/shard_map/pallas_call | solution.py:127
  103.9 0.4 collective-permute-done.13
  104.4 5.8 %all_gather.3.maps = bf16[256,512]{1,0:T(8,128)(2,1)S(1)} all-gather(bf16[64,512]{1,0:T(8,128)(2,1)S(1)} %slice.41), channel_id=1, replica_groups=mesh['seq'=8,'rep'=4] {'rep'}, dimensions={0}, use_global_device_ids=true | all-gather | bytes 327680 | tf_op jit(solution)/shard_map/all_gather | solution.py:396
  110.1 1.8 %shard_map.84 = (bf16[2,4,256,256]{3,2,1,0:T(8,128)(2,1)S(1)}, bf16[2,4,128,256]{3,2,1,0:T(8,128)(2,1)S(1)}, bf16[2,256,128]{2,1,0:T(8,128)(2,1)S(1)}, f32[2,256,8]{2,1,0:T(8,128)S(1)}, f32[8,512]{1,0:T(8,128)S(1)}) custom-call(s32[3]{0:T(128)S(1)} %pad_add_fusion.place, bf16[256,512]{1,0:T(8,128)(2,1)S(1)} %all_gather.3.maps, ...), custom_call_target="tpu_custom_call" | custom-call | flops 26214400 | bytes 2162764 | tf_op jit(solution)/shard_map/pallas_call | solution.py:127
  111.9 0.0 collective-permute-done.9.three
  111.9 0.0 copy-start.7
  111.9 2.6 %shard_map.85 = (bf16[2,256,512]{2,1,0:T(8,128)(2,1)S(1)}, bf16[144,512]{1,0:T(8,128)(2,1)S(1)}, bf16[128,512]{1,0:T(8,128)(2,1)S(1)}) custom-call(s32[3]{0:T(128)S(1)} %pad_add_fusion.place, bf16[256,4096]{1,0:T(8,128)(2,1)S(1)} %copy-done, bf16[256,2048]{1,0:T(8,128)(2,1)S(1)} %collective-permute-done.1.near, ...), custom_call_target="tpu_custom_call" | custom-call | flops 536870912 | bytes 7634956 | tf_op jit(solution)/shard_map/pallas_call | solution.py:127
  114.5 4.4 %collective-permute-start.14 = (bf16[144,512]{1,0:T(8,128)(2,1)S(1)}, bf16[144,512]{1,0:T(8,128)(2,1)S(1)}, u32[]{:S(2)}, u32[]{:S(2)}) collective-permute-start(bf16[144,512]{1,0:T(8,128)(2,1)S(1)} %get-tuple-element.22), channel_id=1, source_target_pairs={{0,8},{4,12},{8,16},{12,20},{16,24},{20,28},{1,9},{5,13},{9,17},{1... | collective-permute-start | bytes 442376 | tf_op jit(solution)/shard_map/ppermute | solution.py:364
  118.9 1.3 collective-permute-start.15
  120.2 1.0 shard_map.86.local
  121.3 3.0 %collective-permute-done.14.one = bf16[144,512]{1,0:T(8,128)(2,1)S(1)} collective-permute-done((bf16[144,512]{1,0:T(8,128)(2,1)S(1)}, bf16[144,512]{1,0:T(8,128)(2,1)S(1)}, u32[]{:S(2)}, u32[]{:S(2)}) %collective-permute-start.14) | collective-permute-done | bytes 147488 | tf_op jit(solution)/shard_map/ppermute | solution.py:364
  124.3 4.3 %collective-permute-done.15.two = bf16[144,512]{1,0:T(8,128)(2,1)S(1)} collective-permute-done((bf16[144,512]{1,0:T(8,128)(2,1)S(1)}, bf16[144,512]{1,0:T(8,128)(2,1)S(1)}, u32[]{:S(2)}, u32[]{:S(2)}) %collective-permute-start.15) | collective-permute-done | bytes 147488 | tf_op jit(solution)/shard_map/ppermute | solution.py:364
  128.6 0.8 shard_map.88
  129.4 1.2 collective-permute-start.16
  130.6 0.8 shard_map.87
  131.4 5.9 %collective-permute-done.16 = bf16[256,512]{1,0:T(8,128)(2,1)S(1)} collective-permute-done((bf16[256,512]{1,0:T(8,128)(2,1)S(1)}, bf16[256,512]{1,0:T(8,128)(2,1)S(1)}, u32[]{:S(2)}, u32[]{:S(2)}) %collective-permute-start.16) | collective-permute-done | bytes 262176 | tf_op jit(solution)/shard_map/ppermute | solution.py:364
  137.3 0.9 maximum_select_fusion
  (22 shorter events, 0.1 us)
Async XLA Ops:
  0.0 19.5 %copy-start = (bf16[256,4096]{1,0:T(8,128)(2,1)S(1)}, bf16[256,4096]{1,0:T(8,128)(2,1)}, u32[]{:S(2)}) copy-start(bf16[256,4096]{1,0:T(8,128)(2,1)} %hidden.5) | copy-start | bytes 6291460
  2.2 13.8 %collective-permute-start = (bf16[512,512]{1,0:T(8,128)(2,1)S(1)}, bf16[512,512]{1,0:T(8,128)(2,1)}, u32[]{:S(2)}, u32[]{:S(2)}) collective-permute-start(bf16[512,512]{1,0:T(8,128)(2,1)S(1)} %get-tuple-element.24), channel_id=1, source_target_pairs={{0,4},{4,0},{8,12},{12,8},{16,20},{20,16},{24,28},{28,24},{1,5},{5... | collective-permute-start | bytes 1572872 | tf_op jit(solution)/shard_map/ppermute | solution.py:364
  3.7 22.2 %collective-permute-start.3 = (bf16[512,512]{1,0:T(8,128)(2,1)}, bf16[512,512]{1,0:T(8,128)(2,1)}, u32[]{:S(2)}, u32[]{:S(2)}) collective-permute-start(bf16[512,512]{1,0:T(8,128)(2,1)} %get-tuple-element.23.own), channel_id=1, source_target_pairs={{0,8},{4,12},{8,16},{12,20},{16,24},{20,28},{1,9},{5,13},{9,17},{1... | collective-permute-start | bytes 1572872 | tf_op jit(solution)/shard_map/ppermute | solution.py:364
  16.0 14.9 %collective-permute-start.4 = (bf16[512,512]{1,0:T(8,128)(2,1)}, bf16[512,512]{1,0:T(8,128)(2,1)S(1)}, u32[]{:S(2)}, u32[]{:S(2)}) collective-permute-start(bf16[512,512]{1,0:T(8,128)(2,1)} %collective-permute-done.other), channel_id=1, source_target_pairs={{0,8},{4,12},{8,16},{12,20},{16,24},{20,28},{1,9},{5,13},{9,17},{1... | collective-permute-start | bytes 1572872 | tf_op jit(solution)/shard_map/ppermute | solution.py:364
  19.6 29.9 %copy-start.12 = (s32[256]{0:T(256)S(1)}, s32[256]{0:T(256)}, u32[]{:S(2)}) copy-start(s32[256]{0:T(256)} %param.9) | copy-start | bytes 3076
  19.6 29.8 %collective-permute-start.1 = (bf16[256,2048]{1,0:T(8,128)(2,1)S(1)}, bf16[256,2048]{1,0:T(8,128)(2,1)S(1)}, u32[]{:S(2)}, u32[]{:S(2)}) collective-permute-start(bf16[256,2048]{1,0:T(8,128)(2,1)S(1)} %slice_select_fusion), channel_id=1, source_target_pairs={{0,4},{4,0},{8,12},{12,8},{16,20},{20,16},{24,28},{28,24},{1,5},{5... | collective-permute-start | bytes 3145736 | tf_op jit(solution)/shard_map/ppermute | solution.py:364
  21.2 17.0 %collective-permute-start.5 = (bf16[512,512]{1,0:T(8,128)(2,1)}, bf16[512,512]{1,0:T(8,128)(2,1)S(1)}, u32[]{:S(2)}, u32[]{:S(2)}) collective-permute-start(bf16[512,512]{1,0:T(8,128)(2,1)} %get-tuple-element.23.own), channel_id=1, source_target_pairs={{8,0},{12,4},{16,8},{20,12},{24,16},{28,20},{9,1},{13,5},{17,9},{2... | collective-permute-start | bytes 1572872 | tf_op jit(solution)/shard_map/ppermute | solution.py:364
  23.5 23.2 %collective-permute-start.6 = (bf16[512,512]{1,0:T(8,128)(2,1)}, bf16[512,512]{1,0:T(8,128)(2,1)S(1)}, u32[]{:S(2)}, u32[]{:S(2)}) collective-permute-start(bf16[512,512]{1,0:T(8,128)(2,1)} %collective-permute-done.other), channel_id=1, source_target_pairs={{8,0},{12,4},{16,8},{20,12},{24,16},{28,20},{9,1},{13,5},{17,9},{2... | collective-permute-start | bytes 1572872 | tf_op jit(solution)/shard_map/ppermute | solution.py:364
  30.9 18.7 %copy-start.1 = (bf16[512,512]{1,0:T(8,128)(2,1)}, bf16[512,512]{1,0:T(8,128)(2,1)S(1)}, u32[]{:S(2)}) copy-start(bf16[512,512]{1,0:T(8,128)(2,1)S(1)} %collective-permute-done.4.up) | copy-start | bytes 1572868
  32.2 25.0 %collective-permute-start.7 = (bf16[1024,512]{1,0:T(8,128)(2,1)S(1)}, bf16[1024,512]{1,0:T(8,128)(2,1)S(1)}, u32[]{:S(2)}, u32[]{:S(2)}) collective-permute-start(bf16[1024,512]{1,0:T(8,128)(2,1)S(1)} %pad_maximum_fusion), channel_id=1, source_target_pairs={{8,16},{12,20},{16,24},{20,28},{9,17},{13,21},{17,25},{21,29},{10,... | collective-permute-start | bytes 3145736 | tf_op jit(solution)/shard_map/ppermute | solution.py:364
  38.1 11.4 %copy-start.3 = (bf16[512,512]{1,0:T(8,128)(2,1)}, bf16[512,512]{1,0:T(8,128)(2,1)S(1)}, u32[]{:S(2)}) copy-start(bf16[512,512]{1,0:T(8,128)(2,1)S(1)} %collective-permute-done.5.do) | copy-start | bytes 1572868
  46.8 2.8 %copy-start.5 = (bf16[512,512]{1,0:T(8,128)(2,1)}, bf16[512,512]{1,0:T(8,128)(2,1)S(1)}, u32[]{:S(2)}) copy-start(bf16[512,512]{1,0:T(8,128)(2,1)S(1)} %collective-permute-done.6.dp) | copy-start | bytes 1572868
  46.8 26.2 %copy-start.8 = (bf16[512,64]{0,1:T(8,128)(2,1)S(1)}, bf16[512,64]{0,1:T(8,128)(2,1)}, u32[]{:S(2)}) copy-start(bf16[512,64]{0,1:T(8,128)(2,1)} %param.11) | copy-start | bytes 196612
  46.8 26.1 %copy-start.9 = (bf16[512,8]{0,1:T(8,128)(2,1)S(1)}, bf16[512,8]{0,1:T(8,128)(2,1)}, u32[]{:S(2)}) copy-start(bf16[512,8]{0,1:T(8,128)(2,1)} %param.12) | copy-start | bytes 24580
  46.8 31.3 %copy-start.10 = (f32[8]{0:T(128)S(1)}, f32[8]{0:T(128)}, u32[]{:S(2)}) copy-start(f32[8]{0:T(128)} %param.13) | copy-start | bytes 100
  46.9 31.4 %copy-start.11 = (f32[8]{0:T(128)S(1)}, f32[8]{0:T(128)}, u32[]{:S(2)}) copy-start(f32[8]{0:T(128)} %param.14) | copy-start | bytes 100
  46.9 22.5 %collective-permute-start.8 = (bf16[1024,512]{1,0:T(8,128)(2,1)S(1)}, bf16[1024,512]{1,0:T(8,128)(2,1)S(1)}, u32[]{:S(2)}, u32[]{:S(2)}) collective-permute-start(bf16[1024,512]{1,0:T(8,128)(2,1)S(1)} %pad_maximum_fusion.1), channel_id=1, source_target_pairs={{8,0},{12,4},{16,8},{20,12},{9,1},{13,5},{17,9},{21,13},{10,2},{14... | collective-permute-start | bytes 3145736 | tf_op jit(solution)/shard_map/ppermute | solution.py:364
  49.4 47.5 %collective-permute-start.2 = (bf16[256,2048]{1,0:T(8,128)(2,1)S(1)}, bf16[256,2048]{1,0:T(8,128)(2,1)}, u32[]{:S(2)}, u32[]{:S(2)}) collective-permute-start(bf16[256,2048]{1,0:T(8,128)(2,1)S(1)} %collective-permute-done.1.near), channel_id=1, source_target_pairs={{0,1},{1,0},{2,3},{3,2},{4,5},{5,4},{6,7},{7,6},{8,9},{9,8},{10,11... | collective-permute-start | bytes 3145736 | tf_op jit(solution)/shard_map/ppermute | solution.py:364
  70.7 41.2 %collective-permute-start.9 = (bf16[1024,512]{1,0:T(8,128)(2,1)}, bf16[1024,512]{1,0:T(8,128)(2,1)}, u32[]{:S(2)}, u32[]{:S(2)}) collective-permute-start(bf16[1024,512]{1,0:T(8,128)(2,1)} %add.18.two), channel_id=1, source_target_pairs={{16,24},{20,28},{8,0},{12,4},{17,25},{21,29},{9,1},{13,5},{18,26},... | collective-permute-start | bytes 3145736 | tf_op jit(solution)/shard_map/ppermute | solution.py:364
  73.1 23.8 %collective-permute-start.10 = (bf16[80,512]{1,0:T(8,128)(2,1)S(1)}, bf16[80,512]{1,0:T(8,128)(2,1)S(1)}, u32[]{:S(2)}, u32[]{:S(2)}) collective-permute-start(bf16[80,512]{1,0:T(8,128)(2,1)S(1)} %maximum_maximum_fusion.s0), channel_id=1, source_target_pairs={{0,8},{4,12},{8,16},{12,20},{16,24},{20,28},{24,0},{28,4},{1,9},{5... | collective-permute-start | bytes 245768 | tf_op jit(solution)/shard_map/ppermute | solution.py:364
  73.1 23.8 %collective-permute-start.11 = (bf16[80,512]{1,0:T(8,128)(2,1)S(1)}, bf16[80,512]{1,0:T(8,128)(2,1)S(1)}, u32[]{:S(2)}, u32[]{:S(2)}) collective-permute-start(bf16[80,512]{1,0:T(8,128)(2,1)S(1)} %maximum_maximum_fusion.s0), channel_id=1, source_target_pairs={{0,16},{4,20},{8,24},{12,28},{16,0},{20,4},{24,8},{28,12},{1,17},{... | collective-permute-start | bytes 245768 | tf_op jit(solution)/shard_map/ppermute | solution.py:364
  78.2 18.7 %collective-permute-start.12 = (bf16[80,512]{1,0:T(8,128)(2,1)S(1)}, bf16[80,512]{1,0:T(8,128)(2,1)S(1)}, u32[]{:S(2)}, u32[]{:S(2)}) collective-permute-start(bf16[80,512]{1,0:T(8,128)(2,1)S(1)} %maximum_maximum_fusion.s0), channel_id=1, source_target_pairs={{0,24},{4,28},{8,0},{12,4},{16,8},{20,12},{24,16},{28,20},{1,25},{... | collective-permute-start | bytes 245768 | tf_op jit(solution)/shard_map/ppermute | solution.py:364
  78.4 21.1 %copy-start.2 = (bf16[512,512]{1,0:T(8,128)(2,1)S(1)}, bf16[512,512]{1,0:T(8,128)(2,1)}, u32[]{:S(2)}) copy-start(bf16[512,512]{1,0:T(8,128)(2,1)} %copy-done.1) | copy-start | bytes 1572868
  78.4 21.1 %copy-start.4 = (bf16[512,512]{1,0:T(8,128)(2,1)S(1)}, bf16[512,512]{1,0:T(8,128)(2,1)}, u32[]{:S(2)}) copy-start(bf16[512,512]{1,0:T(8,128)(2,1)} %copy-done.3) | copy-start | bytes 1572868
  78.4 21.1 %copy-start.6 = (bf16[512,512]{1,0:T(8,128)(2,1)S(1)}, bf16[512,512]{1,0:T(8,128)(2,1)}, u32[]{:S(2)}) copy-start(bf16[512,512]{1,0:T(8,128)(2,1)} %copy-done.5) | copy-start | bytes 1572868
  98.9 5.4 %collective-permute-start.13 = (f32[80,512]{1,0:T(8,128)S(1)}, f32[80,512]{1,0:T(8,128)S(1)}, u32[]{:S(2)}, u32[]{:S(2)}) collective-permute-start(f32[80,512]{1,0:T(8,128)S(1)} %shard_map.83), channel_id=1, source_target_pairs={{0,4},{4,0},{8,12},{12,8},{16,20},{20,16},{24,28},{28,24},{1,5},{5... | collective-permute-start | bytes 491528 | tf_op jit(solution)/shard_map/ppermute | solution.py:364
  111.9 8.3 %copy-start.7 = (f32[8]{0:T(128)S(1)}, f32[8]{0:T(128)}, u32[]{:S(2)}) copy-start(f32[8]{0:T(128)} %param.15) | copy-start | bytes 100
  114.5 9.8 %collective-permute-start.14 = (bf16[144,512]{1,0:T(8,128)(2,1)S(1)}, bf16[144,512]{1,0:T(8,128)(2,1)S(1)}, u32[]{:S(2)}, u32[]{:S(2)}) collective-permute-start(bf16[144,512]{1,0:T(8,128)(2,1)S(1)} %get-tuple-element.22), channel_id=1, source_target_pairs={{0,8},{4,12},{8,16},{12,20},{16,24},{20,28},{1,9},{5,13},{9,17},{1... | collective-permute-start | bytes 442376 | tf_op jit(solution)/shard_map/ppermute | solution.py:364
  118.9 9.7 %collective-permute-start.15 = (bf16[144,512]{1,0:T(8,128)(2,1)S(1)}, bf16[144,512]{1,0:T(8,128)(2,1)S(1)}, u32[]{:S(2)}, u32[]{:S(2)}) collective-permute-start(bf16[144,512]{1,0:T(8,128)(2,1)S(1)} %get-tuple-element.22), channel_id=1, source_target_pairs={{0,16},{4,20},{8,24},{12,28},{1,17},{5,21},{9,25},{13,29},{2,18},{... | collective-permute-start | bytes 442376 | tf_op jit(solution)/shard_map/ppermute | solution.py:364
  129.4 7.9 %collective-permute-start.16 = (bf16[256,512]{1,0:T(8,128)(2,1)S(1)}, bf16[256,512]{1,0:T(8,128)(2,1)S(1)}, u32[]{:S(2)}, u32[]{:S(2)}) collective-permute-start(bf16[256,512]{1,0:T(8,128)(2,1)S(1)} %shard_map.88), channel_id=1, source_target_pairs={{0,4},{4,0},{8,12},{12,8},{16,20},{20,16},{24,28},{28,24},{1,5},{5... | collective-permute-start | bytes 786440 | tf_op jit(solution)/shard_map/ppermute | solution.py:364

commit v3 on v2

--- a/solution.py
+++ b/solution.py
@@ -114,10 +114,6 @@
 
 def pick(first, one, other):
     return jnp.where(first, one, other)
-
-
-def after(x, *earlier):
-    return lax.optimization_barrier((x, *earlier))[0]
 
 
 def call(body, outs, *operands, flops=0, scratch=()):
@@ -248,38 +244,33 @@
             loaded[b, h] = (wide * tail[h : h + 1]).astype(bf16)
 
 
-def early_kernel(place, hidden, near, far, own, other, uo, up, do, dp, two, out):
+def add_products(place, token_refs, backs, weight_refs, totals):
     plane, lane = place[0], place[1]
-    size = own.shape[0]
-    sources = (
-        (plane, own, other),
-        (jnp.maximum(plane - 1, 0), uo, up),
-        (jnp.minimum(plane + 1, PLANES - 1), do, dp),
-        ((plane + 2) % PLANES, two.at[:size], two.at[size:]),
-    )
+    for (back, is_own), w in zip(backs, weight_refs):
+        at = LANES * ((plane + PLANES - back) % PLANES) + (lane if is_own else 1 - lane)
+        weights = w[...]
+        for r, tokens in enumerate(depth_blocks(place, token_refs, at, w.shape[0])):
+            product = mul(tokens, weights)
+            totals[r] = product if totals[r] is None else totals[r] + product
+
+
+def early_kernel(backs, place, hidden, near, far, *refs):
+    *weights, out = refs
     totals = [None, None]
-    for at_plane, w_lane, w_other in sources:
-        for l, w in ((lane, w_lane), (1 - lane, w_other)):
-            weights = w[...]
-            blocks = depth_blocks(place, (hidden, near, far), LANES * at_plane + l, size)
-            for r, tokens in enumerate(blocks):
-                product = mul(tokens, weights)
-                totals[r] = product if totals[r] is None else totals[r] + product
+    if len(weights) > len(backs):
+        totals = [weights[0][0], weights[0][1]]
+        weights = weights[1:]
+    add_products(place, (hidden, near, far), backs, weights, totals)
     out[0] = totals[0]
     out[1] = totals[1]
 
 
-def input_kernel(place, hidden, near, far, acc, three, loaded, meta, x_out, ready, built_out):
+def input_kernel(place, hidden, near, far, acc, last_own, last_other, loaded, meta, x_out, ready, built_out):
     f32, bf16 = jnp.float32, jnp.bfloat16
-    plane, lane = place[0], place[1]
-    size = three.shape[0] // 2
-    at_plane = jnp.where(plane == 0, PLANES - 1, 0)
+    lane = place[1]
     totals = [acc[0], acc[1]]
-    for l, w in ((lane, three.at[:size]), (1 - lane, three.at[size:])):
-        weights = w[...]
-        blocks = depth_blocks(place, (hidden, near, far), LANES * at_plane + l, size)
-        for r, tokens in enumerate(blocks):
-            totals[r] = totals[r] + mul(tokens, weights)
+    backs = ((PLANES - 1, True), (PLANES - 1, False))
+    add_products(place, (hidden, near, far), backs, (last_own, last_other), totals)
     x_out[lane] = totals[0].astype(bf16)
     x_out[1 - lane] = totals[1].astype(bf16)
     mine = loaded.shape[1]
@@ -363,24 +354,40 @@
     def send(x, pairs, axis="seq"):
         return lax.ppermute(x, axis, pairs)
 
+    together = lax.optimization_barrier
+    along = ring(1)
+
+    def add_early(backs, *operands):
+        return call(
+            functools.partial(early_kernel, backs),
+            shaped(f32, LANES, rows, half),
+            place,
+            hidden,
+            near,
+            far,
+            *operands,
+            flops=4 * rows * k_rows * half * len(backs),
+        )
+
     own = pick(even, x_weight[:, :half], x_weight[:, half:])
     other = send(pick(even, x_weight[:, half:], x_weight[:, :half]), swap)
-    up_own, down_own = send(own, shift(1, (0, 1, 2))), send(own, shift(-1, (1, 2, 3)))
-    up_other, down_other = send(other, shift(1, (0, 1, 2))), send(other, shift(-1, (1, 2, 3)))
-    up_two = send(jnp.concatenate([up_own, up_other]), shift(1, (1, 2)))
-    down_two = send(jnp.concatenate([down_own, down_other]), shift(-1, (1, 2)))
-    two = up_two + down_two
-    three = send(two, shift(1, (2,)) + shift(-1, (1,)))
-
-    near = pick(core == 0, hidden[:, : depth // 2], hidden[:, depth // 2 :])
-    near = send(after(near, other), swap)
-    far = send(near, cores, "rep")
+    own_one = send(own, along)
+    other_one = send(other, along)
+    own_two = send(own_one, along)
+    other_two = send(other_one, along)
+    own_three = send(own_two, along)
+    other_three = send(other_two, along)
 
     ids_row = jnp.pad(seg_ids.astype(bf16), (0, k_rows - rows))[None]
     small = jnp.concatenate(
         [bc_weight.T, dt_weight.T, ids_row, jnp.zeros((7, k_rows), bf16)], axis=0
     )
-    from_ring = [small] + [send(small, ring(by)) for by in (1, 2, 3)]
+    near = pick(core == 0, hidden[:, : depth // 2], hidden[:, depth // 2 :])
+    from_ring = [send(small, ring(by)) for by in (1, 2, 3)]
+    near, from_ring, _ = together((near, from_ring, (other, own_one)))
+    near = send(near, swap)
+    near, from_ring, _ = together((near, from_ring, (own_two, other_one)))
+    far = send(near, cores, "rep")
     share = call(
         functools.partial(share_kernel, used),
         shaped(f32, used + 8, LANES * rows),
@@ -388,11 +395,16 @@
         hidden,
         near,
         far,
+        small,
         *from_ring,
         flops=4 * rows * depth * used,
     )
+    early = add_early(
+        ((0, True), (0, False), (1, True), (1, False)), own, other, own_one, other_one
+    )
     share_other = send(share, swap)
     total = share + jnp.concatenate([share_other[:, rows:], share_other[:, :rows]], axis=1)
+    total, _ = together((total, own_three))
     maps = lax.all_gather(total[:map_cols].astype(bf16), "rep", axis=0, tiled=True)
     mixing, loaded, c_rows, fac, meta = call(
         functools.partial(decay_kernel, map_cols),
@@ -410,22 +422,7 @@
         decay_rate[:, None],
         flops=100 * mine * rows * rows,
     )
-    early = call(
-        early_kernel,
-        shaped(f32, LANES, rows, half),
-        place,
-        hidden,
-        near,
-        far,
-        own,
-        other,
-        up_own,
-        up_other,
-        down_own,
-        down_other,
-        two,
-        flops=4 * rows * depth * half,
-    )
+    early = add_early(((2, True), (2, False)), early, own_two, other_two)
     inputs, ready, built = call(
         input_kernel,
         [
@@ -438,7 +435,8 @@
         near,
         far,
         early,
-        three,
+        own_three,
+        other_three,
         loaded,
         meta,
         flops=rows * depth * half,

time: 141 us -> 114 us (0.81)
  waiting for transfers between devices: 76.6 us -> 60.9 us
  starting transfers between devices: 35.7 us -> 21.4 us
  local copies, waits for them, and re-layouts: 0.34 us -> 6.61 us
  other arithmetic: 6.11 us -> 3.45 us
    ppermute x17 -> x16, waiting for transfers between devices: 76.6 us -> 60.9 us  [send(): return lax.ppermute(x, axis, pairs)]
    ppermute x17 -> x16, starting transfers between devices: 35.7 us -> 21.4 us  [send(): return lax.ppermute(x, axis, pairs)]
    unnamed x26 -> x32, local copies, waits for them, and re-layouts: 0.06 us -> 5.03 us
    pallas_call x7 -> x8, Pallas kernels: 13.4 us -> 13.6 us  [call(): pl.pallas_call(body, out_shape=shapes, in_specs=[pl.BlockSpec(memory_spac...]
  transfers between devices with their start and end apart: 17 -> 16, of which waited for: 11 -> 10; matrix products, arithmetic and copies ran while one was open for 2% -> 2% of each run, Pallas kernels for 7% -> 9%
where the time goes in v3:
time: 114 us; the launch traced here: 112 us
  waiting for transfers between devices  60.9 us (53%)
  starting transfers between devices  21.4 us (19%)
  Pallas kernels  13.6 us (12%)
  local copies, waits for them, and re-layouts  6.61 us (6%)
  blocking collectives  5.79 us (5%)
  other arithmetic  3.45 us (3%)
    ppermute x16, waiting for transfers between devices, send(): return lax.ppermute(x, axis, pairs)  60.9 us
    ppermute x16, starting transfers between devices, send(): return lax.ppermute(x, axis, pairs)  21.4 us
    pallas_call x8, Pallas kernels, call(): pl.pallas_call(body, out_shape=shapes, in_specs=[pl.BlockSpec(memory_spac...  13.6 us
    all_gather x1, blocking collectives, plane_shards(): lax.all_gather(total[:map_cols].astype(bf16), 'rep', axis=0, tiled=True)  5.79 us
    unnamed x32, local copies, waits for them, and re-layouts  5.03 us
    select_n x3, other arithmetic, pick(): return jnp.where(first, one, other)  3.26 us
  transfers between devices with their start and end apart: 16, of which 10 were waited for; matrix products, arithmetic and copies ran while one was open for 2% of the time, Pallas kernels for 9%

profile of v3, /device:TPU:16, one launch (start us, length us, event | category | flops | bytes accessed | tf_op | source)
XLA Modules:
  0.0 112.0 jit_solution(5468823765756239300)
XLA Ops:
  0.0 0.0 copy-start
  0.0 2.2 %broadcast_select_fusion = (bf16[512,512]{1,0:T(8,128)(2,1)S(1)}, bf16[512,512]{1,0:T(8,128)(2,1)}) fusion(pred[]{:T(512)S(6)} %eq.9, bf16[512,1024]{1,0:T(8,128)(2,1)} %param.10), kind=kLoop, calls=%fused_computation.2 | loop fusion | flops 524288 | bytes 2097153 | tf_op jit(solution)/shard_map/jit(_where)/select_n | solution.py:116
  2.3 1.5 %collective-permute-start.3 = (bf16[512,512]{1,0:T(8,128)(2,1)}, bf16[512,512]{1,0:T(8,128)(2,1)S(1)}, u32[]{:S(2)}, u32[]{:S(2)}) collective-permute-start(bf16[512,512]{1,0:T(8,128)(2,1)} %get-tuple-element.40), channel_id=1, source_target_pairs={{0,4},{4,0},{8,12},{12,8},{16,20},{20,16},{24,28},{28,24},{1,5},{5... | collective-permute-start | bytes 1572872 | tf_op jit(solution)/shard_map/ppermute | solution.py:355
  3.8 1.6 %collective-permute-start.4 = (bf16[512,512]{1,0:T(8,128)(2,1)S(1)}, bf16[512,512]{1,0:T(8,128)(2,1)}, u32[]{:S(2)}, u32[]{:S(2)}) collective-permute-start(bf16[512,512]{1,0:T(8,128)(2,1)S(1)} %get-tuple-element.39.refs_0_), channel_id=1, source_target_pairs={{0,8},{4,12},{8,16},{12,20},{16,24},{20,28},{24,0},{28,4},{1,9},{5... | collective-permute-start | bytes 1572872 | tf_op jit(solution)/shard_map/ppermute | solution.py:355
  5.4 0.0 copy-done.15
  5.4 0.1 pad.14.clone
  5.5 0.0 copy-done.14
  5.5 0.0 copy-done.13
  5.5 0.1 maximum_maximum_fusion.s0
  5.6 0.3 collective-permute-start
  5.8 1.7 %collective-permute-start.1 = (bf16[80,512]{1,0:T(8,128)(2,1)S(1)}, bf16[80,512]{1,0:T(8,128)(2,1)S(1)}, u32[]{:S(2)}, u32[]{:S(2)}) collective-permute-start(bf16[80,512]{1,0:T(8,128)(2,1)S(1)} %maximum_maximum_fusion.s0), channel_id=1, source_target_pairs={{0,16},{4,20},{8,24},{12,28},{16,0},{20,4},{24,8},{28,12},{1,17},{... | collective-permute-start | bytes 245768 | tf_op jit(solution)/shard_map/ppermute | solution.py:355
  7.5 1.3 %collective-permute-start.2 = (bf16[80,512]{1,0:T(8,128)(2,1)S(1)}, bf16[80,512]{1,0:T(8,128)(2,1)S(1)}, u32[]{:S(2)}, u32[]{:S(2)}) collective-permute-start(bf16[80,512]{1,0:T(8,128)(2,1)S(1)} %maximum_maximum_fusion.s0), channel_id=1, source_target_pairs={{0,24},{4,28},{8,0},{12,4},{16,8},{20,12},{24,16},{28,20},{1,25},{... | collective-permute-start | bytes 245768 | tf_op jit(solution)/shard_map/ppermute | solution.py:355
  8.9 0.0 copy-done
  8.9 0.1 slice_select_fusion
  9.0 14.3 %collective-permute-done.s1 = bf16[80,512]{1,0:T(8,128)(2,1)S(1)} collective-permute-done((bf16[80,512]{1,0:T(8,128)(2,1)S(1)}, bf16[80,512]{1,0:T(8,128)(2,1)S(1)}, u32[]{:S(2)}, u32[]{:S(2)}) %collective-permute-start) | collective-permute-done | bytes 81952 | tf_op jit(solution)/shard_map/ppermute | solution.py:355
  23.3 0.0 collective-permute-done.1.s2
  23.3 0.0 collective-permute-done.2.s3
  23.3 0.6 copy-done.7
  23.9 0.0 collective-permute-done.3.refs_1_
  23.9 0.0 copy-done.1
  23.9 0.8 copy-done.3
  24.7 0.0 collective-permute-done.4.refs_2_
  24.7 0.5 collective-permute-start.5
  25.2 2.3 %collective-permute-start.6 = (bf16[512,512]{1,0:T(8,128)(2,1)}, bf16[512,512]{1,0:T(8,128)(2,1)S(1)}, u32[]{:S(2)}, u32[]{:S(2)}) collective-permute-start(bf16[512,512]{1,0:T(8,128)(2,1)} %collective-permute-done.4.refs_2_), channel_id=1, source_target_pairs={{0,8},{4,12},{8,16},{12,20},{16,24},{20,28},{24,0},{28,4},{1,9},{5... | collective-permute-start | bytes 1572872 | tf_op jit(solution)/shard_map/ppermute | solution.py:355
  27.6 0.6 collective-permute-start.7
  28.2 12.3 %collective-permute-done.6.refs_1_ = bf16[512,512]{1,0:T(8,128)(2,1)S(1)} collective-permute-done((bf16[512,512]{1,0:T(8,128)(2,1)}, bf16[512,512]{1,0:T(8,128)(2,1)S(1)}, u32[]{:S(2)}, u32[]{:S(2)}) %collective-permute-start.6) | collective-permute-done | bytes 524320 | tf_op jit(solution)/shard_map/ppermute | solution.py:355
  40.4 10.4 %collective-permute-done.7.refs_3_ = bf16[512,512]{1,0:T(8,128)(2,1)} collective-permute-done((bf16[512,512]{1,0:T(8,128)(2,1)}, bf16[512,512]{1,0:T(8,128)(2,1)}, u32[]{:S(2)}, u32[]{:S(2)}) %collective-permute-start.7) | collective-permute-done | bytes 524320 | tf_op jit(solution)/shard_map/ppermute | solution.py:355
  50.8 0.0 collective-permute-done.5.near
  50.8 0.0 copy-done.5
  50.8 0.0 collective-permute-start.8
  50.8 0.3 collective-permute-start.9
  51.1 0.1 pad_add_fusion.place
  51.2 2.4 %collective-permute-done.8.far = bf16[256,2048]{1,0:T(8,128)(2,1)} collective-permute-done((bf16[256,2048]{1,0:T(8,128)(2,1)S(1)}, bf16[256,2048]{1,0:T(8,128)(2,1)}, u32[]{:S(2)}, u32[]{:S(2)}) %collective-permute-start.8) | collective-permute-done | bytes 1048608 | tf_op jit(solution)/shard_map/ppermute | solution.py:355
  53.6 0.9 copy-done.8
  54.5 2.0 %shard_map.84 = f32[80,512]{1,0:T(8,128)S(1)} custom-call(s32[3]{0:T(128)S(1)} %pad_add_fusion.place, bf16[256,4096]{1,0:T(8,128)(2,1)S(1)} %copy-done, bf16[256,2048]{1,0:T(8,128)(2,1)S(1)} %collective-permute-done.5.near, bf16[256,2048]{1,0:T(8,128)(2,1)} %collective-permute-done.8.far, bf16[80,512]{1,0:T(8,128)(2,1)S(1)} %maximum_maximum_fusion.s0, ...), custom_call_target="tpu_custom_call" | custom-call | flops 301989888 | bytes 4685836 | tf_op jit(solution)/shard_map/pallas_call | solution.py:123
  56.5 0.0 copy-done.9
  56.5 1.6 %collective-permute-start.12 = (f32[80,512]{1,0:T(8,128)S(1)}, f32[80,512]{1,0:T(8,128)S(1)}, u32[]{:S(2)}, u32[]{:S(2)}) collective-permute-start(f32[80,512]{1,0:T(8,128)S(1)} %shard_map.84), channel_id=1, source_target_pairs={{0,4},{4,0},{8,12},{12,8},{16,20},{20,16},{24,28},{28,24},{1,5},{5... | collective-permute-start | bytes 491528 | tf_op jit(solution)/shard_map/ppermute | solution.py:355
  58.1 0.7 copy.9.bias
  58.8 0.7 copy.10.rate_of
  59.6 1.5 %collective-permute-start.10 = (bf16[512,512]{1,0:T(8,128)(2,1)}, bf16[512,512]{1,0:T(8,128)(2,1)S(1)}, u32[]{:S(2)}, u32[]{:S(2)}) collective-permute-start(bf16[512,512]{1,0:T(8,128)(2,1)} %copy-done.5), channel_id=1, source_target_pairs={{0,8},{4,12},{8,16},{12,20},{16,24},{20,28},{24,0},{28,4},{1,9},{5... | collective-permute-start | bytes 1572872 | tf_op jit(solution)/shard_map/ppermute | solution.py:355
  61.1 4.9 %collective-permute-done.9.refs_2_ = bf16[512,512]{1,0:T(8,128)(2,1)} collective-permute-done((bf16[512,512]{1,0:T(8,128)(2,1)}, bf16[512,512]{1,0:T(8,128)(2,1)}, u32[]{:S(2)}, u32[]{:S(2)}) %collective-permute-start.9) | collective-permute-done | bytes 524320 | tf_op jit(solution)/shard_map/ppermute | solution.py:355
  65.9 1.7 %collective-permute-start.11 = (bf16[512,512]{1,0:T(8,128)(2,1)}, bf16[512,512]{1,0:T(8,128)(2,1)S(1)}, u32[]{:S(2)}, u32[]{:S(2)}) collective-permute-start(bf16[512,512]{1,0:T(8,128)(2,1)} %collective-permute-done.9.refs_2_), channel_id=1, source_target_pairs={{0,8},{4,12},{8,16},{12,20},{16,24},{20,28},{24,0},{28,4},{1,9},{5... | collective-permute-start | bytes 1572872 | tf_op jit(solution)/shard_map/ppermute | solution.py:355
  67.6 1.0 copy-done.2
  68.7 1.0 copy-done.4
  69.7 0.6 copy-done.10
  70.3 2.9 %shard_map.82.refs_0_ = f32[2,256,512]{2,1,0:T(8,128)S(1)} custom-call(s32[3]{0:T(128)S(1)} %copy-done.10, bf16[256,4096]{1,0:T(8,128)(2,1)S(1)} %copy-done, bf16[256,2048]{1,0:T(8,128)(2,1)S(1)} %collective-permute-done.5.near, bf16[256,2048]{1,0:T(8,128)(2,1)} %collective-permute-done.8.far, bf16[512,512]{1,0:T(8,128)(2,1)S(1)} %copy-done.2, ...), custom_call_target="tpu_custom_call" | custom-call | flops 1073741824 | bytes 7340044 | tf_op jit(solution)/shard_map/pallas_call | solution.py:123
  73.2 0.0 copy-done.6
  73.2 2.1 %shard_map.83.acc = f32[2,256,512]{2,1,0:T(8,128)S(1)} custom-call(s32[3]{0:T(128)S(1)} %copy-done.10, bf16[256,4096]{1,0:T(8,128)(2,1)S(1)} %copy-done, bf16[256,2048]{1,0:T(8,128)(2,1)S(1)} %collective-permute-done.5.near, bf16[256,2048]{1,0:T(8,128)(2,1)} %collective-permute-done.8.far, f32[2,256,512]{2,1,0:T(8,128)S(1)} %shard_map.82.refs_0_, ...), custom_call_target="tpu_custom_call" | custom-call | flops 536870912 | bytes 7340044 | tf_op jit(solution)/shard_map/pallas_call | solution.py:123
  75.3 0.0 collective-permute-done.12
  75.3 1.7 %collective-permute-done.10.last_own = bf16[512,512]{1,0:T(8,128)(2,1)S(1)} collective-permute-done((bf16[512,512]{1,0:T(8,128)(2,1)}, bf16[512,512]{1,0:T(8,128)(2,1)S(1)}, u32[]{:S(2)}, u32[]{:S(2)}) %collective-permute-start.10) | collective-permute-done | bytes 524320 | tf_op jit(solution)/shard_map/ppermute | solution.py:355
  77.1 5.8 %all_gather.3.maps = bf16[256,512]{1,0:T(8,128)(2,1)S(1)} all-gather(bf16[64,512]{1,0:T(8,128)(2,1)S(1)} %slice.41), channel_id=1, replica_groups=mesh['seq'=8,'rep'=4] {'rep'}, dimensions={0}, use_global_device_ids=true | all-gather | bytes 327680 | tf_op jit(solution)/shard_map/all_gather | solution.py:408
  82.9 1.8 %shard_map.85 = (bf16[2,4,256,256]{3,2,1,0:T(8,128)(2,1)S(1)}, bf16[2,4,128,256]{3,2,1,0:T(8,128)(2,1)S(1)}, bf16[2,256,128]{2,1,0:T(8,128)(2,1)S(1)}, f32[2,256,8]{2,1,0:T(8,128)S(1)}, f32[8,512]{1,0:T(8,128)S(1)}) custom-call(s32[3]{0:T(128)S(1)} %copy-done.11, bf16[256,512]{1,0:T(8,128)(2,1)S(1)} %all_gather.3.maps, f32[80,512]{1,0:T(8,128)S(1)} %maximum_add_fusion.total, ...), custom_call_target="tpu_custom_call" | custom-call | flops 26214400 | bytes 2162764 | tf_op jit(solution)/shard_map/pallas_call | solution.py:123
  84.6 3.2 %collective-permute-done.11.last_other = bf16[512,512]{1,0:T(8,128)(2,1)S(1)} collective-permute-done((bf16[512,512]{1,0:T(8,128)(2,1)}, bf16[512,512]{1,0:T(8,128)(2,1)S(1)}, u32[]{:S(2)}, u32[]{:S(2)}) %collective-permute-start.11) | collective-permute-done | bytes 524320 | tf_op jit(solution)/shard_map/ppermute | solution.py:355
  87.9 2.3 %shard_map.86 = (bf16[2,256,512]{2,1,0:T(8,128)(2,1)S(1)}, bf16[144,512]{1,0:T(8,128)(2,1)S(1)}, bf16[128,512]{1,0:T(8,128)(2,1)S(1)}) custom-call(s32[3]{0:T(128)S(1)} %copy-done.11, bf16[256,4096]{1,0:T(8,128)(2,1)S(1)} %copy-done, bf16[256,2048]{1,0:T(8,128)(2,1)S(1)} %collective-permute-done.5.near, bf16[256,2048]{1,0:T(8,128)(2,1)} %collective-permute-done.8.far, ...), custom_call_target="tpu_custom_call" | custom-call | flops 536870912 | bytes 7634956 | tf_op jit(solution)/shard_map/pallas_call | solution.py:123
  90.1 3.7 %collective-permute-start.13 = (bf16[144,512]{1,0:T(8,128)(2,1)S(1)}, bf16[144,512]{1,0:T(8,128)(2,1)S(1)}, u32[]{:S(2)}, u32[]{:S(2)}) collective-permute-start(bf16[144,512]{1,0:T(8,128)(2,1)S(1)} %get-tuple-element.38), channel_id=1, source_target_pairs={{0,8},{4,12},{8,16},{12,20},{16,24},{20,28},{1,9},{5,13},{9,17},{1... | collective-permute-start | bytes 442376 | tf_op jit(solution)/shard_map/ppermute | solution.py:355
  93.8 1.3 %collective-permute-start.14 = (bf16[144,512]{1,0:T(8,128)(2,1)S(1)}, bf16[144,512]{1,0:T(8,128)(2,1)S(1)}, u32[]{:S(2)}, u32[]{:S(2)}) collective-permute-start(bf16[144,512]{1,0:T(8,128)(2,1)S(1)} %get-tuple-element.38), channel_id=1, source_target_pairs={{0,16},{4,20},{8,24},{12,28},{1,17},{5,21},{9,25},{13,29},{2,18},{... | collective-permute-start | bytes 442376 | tf_op jit(solution)/shard_map/ppermute | solution.py:355
  95.1 1.0 shard_map.87.local
  96.2 1.9 %collective-permute-done.13.one = bf16[144,512]{1,0:T(8,128)(2,1)S(1)} collective-permute-done((bf16[144,512]{1,0:T(8,128)(2,1)S(1)}, bf16[144,512]{1,0:T(8,128)(2,1)S(1)}, u32[]{:S(2)}, u32[]{:S(2)}) %collective-permute-start.13) | collective-permute-done | bytes 147488 | tf_op jit(solution)/shard_map/ppermute | solution.py:355
  98.1 4.8 %collective-permute-done.14.two = bf16[144,512]{1,0:T(8,128)(2,1)S(1)} collective-permute-done((bf16[144,512]{1,0:T(8,128)(2,1)S(1)}, bf16[144,512]{1,0:T(8,128)(2,1)S(1)}, u32[]{:S(2)}, u32[]{:S(2)}) %collective-permute-start.14) | collective-permute-done | bytes 147488 | tf_op jit(solution)/shard_map/ppermute | solution.py:355
  102.8 0.8 shard_map.89
  103.7 1.6 %collective-permute-start.15 = (bf16[256,512]{1,0:T(8,128)(2,1)S(1)}, bf16[256,512]{1,0:T(8,128)(2,1)S(1)}, u32[]{:S(2)}, u32[]{:S(2)}) collective-permute-start(bf16[256,512]{1,0:T(8,128)(2,1)S(1)} %shard_map.89), channel_id=1, source_target_pairs={{0,4},{4,0},{8,12},{12,8},{16,20},{20,16},{24,28},{28,24},{1,5},{5... | collective-permute-start | bytes 786440 | tf_op jit(solution)/shard_map/ppermute | solution.py:355
  105.2 0.8 shard_map.88
  106.0 5.0 %collective-permute-done.15 = bf16[256,512]{1,0:T(8,128)(2,1)S(1)} collective-permute-done((bf16[256,512]{1,0:T(8,128)(2,1)S(1)}, bf16[256,512]{1,0:T(8,128)(2,1)S(1)}, u32[]{:S(2)}, u32[]{:S(2)}) %collective-permute-start.15) | collective-permute-done | bytes 262176 | tf_op jit(solution)/shard_map/ppermute | solution.py:355
  111.0 0.9 maximum_select_fusion
  (24 shorter events, 0.1 us)
Async XLA Ops:
  0.0 5.4 %copy-start.15 = (s32[256]{0:T(256)S(1)}, s32[256]{0:T(256)}, u32[]{:S(2)}) copy-start(s32[256]{0:T(256)} %param.9) | copy-start | bytes 3076
  0.0 5.5 %copy-start.14 = (bf16[512,8]{0,1:T(8,128)(2,1)S(1)}, bf16[512,8]{0,1:T(8,128)(2,1)}, u32[]{:S(2)}) copy-start(bf16[512,8]{0,1:T(8,128)(2,1)} %param.12) | copy-start | bytes 24580
  0.0 5.5 %copy-start.13 = (bf16[512,64]{0,1:T(8,128)(2,1)S(1)}, bf16[512,64]{0,1:T(8,128)(2,1)}, u32[]{:S(2)}) copy-start(bf16[512,64]{0,1:T(8,128)(2,1)} %param.11) | copy-start | bytes 196612
  0.0 8.9 %copy-start = (bf16[256,4096]{1,0:T(8,128)(2,1)S(1)}, bf16[256,4096]{1,0:T(8,128)(2,1)}, u32[]{:S(2)}) copy-start(bf16[256,4096]{1,0:T(8,128)(2,1)} %hidden.7) | copy-start | bytes 6291460
  2.3 21.7 %copy-start.1 = (bf16[512,512]{1,0:T(8,128)(2,1)}, bf16[512,512]{1,0:T(8,128)(2,1)S(1)}, u32[]{:S(2)}) copy-start(bf16[512,512]{1,0:T(8,128)(2,1)S(1)} %get-tuple-element.39.refs_0_) | copy-start | bytes 1572868
  2.3 21.7 %collective-permute-start.3 = (bf16[512,512]{1,0:T(8,128)(2,1)}, bf16[512,512]{1,0:T(8,128)(2,1)S(1)}, u32[]{:S(2)}, u32[]{:S(2)}) collective-permute-start(bf16[512,512]{1,0:T(8,128)(2,1)} %get-tuple-element.40), channel_id=1, source_target_pairs={{0,4},{4,0},{8,12},{12,8},{16,20},{20,16},{24,28},{28,24},{1,5},{5... | collective-permute-start | bytes 1572872 | tf_op jit(solution)/shard_map/ppermute | solution.py:355
  3.8 21.0 %collective-permute-start.4 = (bf16[512,512]{1,0:T(8,128)(2,1)S(1)}, bf16[512,512]{1,0:T(8,128)(2,1)}, u32[]{:S(2)}, u32[]{:S(2)}) collective-permute-start(bf16[512,512]{1,0:T(8,128)(2,1)S(1)} %get-tuple-element.39.refs_0_), channel_id=1, source_target_pairs={{0,8},{4,12},{8,16},{12,20},{16,24},{20,28},{24,0},{28,4},{1,9},{5... | collective-permute-start | bytes 1572872 | tf_op jit(solution)/shard_map/ppermute | solution.py:355
  5.6 17.7 %collective-permute-start = (bf16[80,512]{1,0:T(8,128)(2,1)S(1)}, bf16[80,512]{1,0:T(8,128)(2,1)S(1)}, u32[]{:S(2)}, u32[]{:S(2)}) collective-permute-start(bf16[80,512]{1,0:T(8,128)(2,1)S(1)} %maximum_maximum_fusion.s0), channel_id=1, source_target_pairs={{0,8},{4,12},{8,16},{12,20},{16,24},{20,28},{24,0},{28,4},{1,9},{5... | collective-permute-start | bytes 245768 | tf_op jit(solution)/shard_map/ppermute | solution.py:355
  5.8 17.5 %collective-permute-start.1 = (bf16[80,512]{1,0:T(8,128)(2,1)S(1)}, bf16[80,512]{1,0:T(8,128)(2,1)S(1)}, u32[]{:S(2)}, u32[]{:S(2)}) collective-permute-start(bf16[80,512]{1,0:T(8,128)(2,1)S(1)} %maximum_maximum_fusion.s0), channel_id=1, source_target_pairs={{0,16},{4,20},{8,24},{12,28},{16,0},{20,4},{24,8},{28,12},{1,17},{... | collective-permute-start | bytes 245768 | tf_op jit(solution)/shard_map/ppermute | solution.py:355
  7.5 15.8 %collective-permute-start.2 = (bf16[80,512]{1,0:T(8,128)(2,1)S(1)}, bf16[80,512]{1,0:T(8,128)(2,1)S(1)}, u32[]{:S(2)}, u32[]{:S(2)}) collective-permute-start(bf16[80,512]{1,0:T(8,128)(2,1)S(1)} %maximum_maximum_fusion.s0), channel_id=1, source_target_pairs={{0,24},{4,28},{8,0},{12,4},{16,8},{20,12},{24,16},{28,20},{1,25},{... | collective-permute-start | bytes 245768 | tf_op jit(solution)/shard_map/ppermute | solution.py:355
  23.3 0.6 copy-start.7
  23.9 0.8 copy-start.3
  24.7 26.1 %collective-permute-start.5 = (bf16[256,2048]{1,0:T(8,128)(2,1)S(1)}, bf16[256,2048]{1,0:T(8,128)(2,1)S(1)}, u32[]{:S(2)}, u32[]{:S(2)}) collective-permute-start(bf16[256,2048]{1,0:T(8,128)(2,1)S(1)} %slice_select_fusion), channel_id=1, source_target_pairs={{0,4},{4,0},{8,12},{12,8},{16,20},{20,16},{24,28},{28,24},{1,5},{5... | collective-permute-start | bytes 3145736 | tf_op jit(solution)/shard_map/ppermute | solution.py:355
  25.2 15.2 %collective-permute-start.6 = (bf16[512,512]{1,0:T(8,128)(2,1)}, bf16[512,512]{1,0:T(8,128)(2,1)S(1)}, u32[]{:S(2)}, u32[]{:S(2)}) collective-permute-start(bf16[512,512]{1,0:T(8,128)(2,1)} %collective-permute-done.4.refs_2_), channel_id=1, source_target_pairs={{0,8},{4,12},{8,16},{12,20},{16,24},{20,28},{24,0},{28,4},{1,9},{5... | collective-permute-start | bytes 1572872 | tf_op jit(solution)/shard_map/ppermute | solution.py:355
  27.6 23.2 %collective-permute-start.7 = (bf16[512,512]{1,0:T(8,128)(2,1)}, bf16[512,512]{1,0:T(8,128)(2,1)}, u32[]{:S(2)}, u32[]{:S(2)}) collective-permute-start(bf16[512,512]{1,0:T(8,128)(2,1)} %copy-done.3), channel_id=1, source_target_pairs={{0,8},{4,12},{8,16},{12,20},{16,24},{20,28},{24,0},{28,4},{1,9},{5... | collective-permute-start | bytes 1572872 | tf_op jit(solution)/shard_map/ppermute | solution.py:355
  40.4 10.4 %copy-start.5 = (bf16[512,512]{1,0:T(8,128)(2,1)}, bf16[512,512]{1,0:T(8,128)(2,1)S(1)}, u32[]{:S(2)}) copy-start(bf16[512,512]{1,0:T(8,128)(2,1)S(1)} %collective-permute-done.6.refs_1_) | copy-start | bytes 1572868
  50.8 2.8 %collective-permute-start.8 = (bf16[256,2048]{1,0:T(8,128)(2,1)S(1)}, bf16[256,2048]{1,0:T(8,128)(2,1)}, u32[]{:S(2)}, u32[]{:S(2)}) collective-permute-start(bf16[256,2048]{1,0:T(8,128)(2,1)S(1)} %collective-permute-done.5.near), channel_id=1, source_target_pairs={{0,1},{1,0},{2,3},{3,2},{4,5},{5,4},{6,7},{7,6},{8,9},{9,8},{10,11... | collective-permute-start | bytes 3145736 | tf_op jit(solution)/shard_map/ppermute | solution.py:355
  50.8 15.1 %collective-permute-start.9 = (bf16[512,512]{1,0:T(8,128)(2,1)}, bf16[512,512]{1,0:T(8,128)(2,1)}, u32[]{:S(2)}, u32[]{:S(2)}) collective-permute-start(bf16[512,512]{1,0:T(8,128)(2,1)} %collective-permute-done.7.refs_3_), channel_id=1, source_target_pairs={{0,8},{4,12},{8,16},{12,20},{16,24},{20,28},{24,0},{28,4},{1,9},{5... | collective-permute-start | bytes 1572872 | tf_op jit(solution)/shard_map/ppermute | solution.py:355
  51.2 5.3 %copy-start.9 = (s32[3]{0:T(128)}, s32[3]{0:T(128)S(1)}, u32[]{:S(2)}) copy-start(s32[3]{0:T(128)S(1)} %pad_add_fusion.place) | copy-start | bytes 40
  53.6 0.9 copy-start.8
  56.5 18.8 %collective-permute-start.12 = (f32[80,512]{1,0:T(8,128)S(1)}, f32[80,512]{1,0:T(8,128)S(1)}, u32[]{:S(2)}, u32[]{:S(2)}) collective-permute-start(f32[80,512]{1,0:T(8,128)S(1)} %shard_map.84), channel_id=1, source_target_pairs={{0,4},{4,0},{8,12},{12,8},{16,20},{20,16},{24,28},{28,24},{1,5},{5... | collective-permute-start | bytes 491528 | tf_op jit(solution)/shard_map/ppermute | solution.py:355
  59.6 17.5 %collective-permute-start.10 = (bf16[512,512]{1,0:T(8,128)(2,1)}, bf16[512,512]{1,0:T(8,128)(2,1)S(1)}, u32[]{:S(2)}, u32[]{:S(2)}) collective-permute-start(bf16[512,512]{1,0:T(8,128)(2,1)} %copy-done.5), channel_id=1, source_target_pairs={{0,8},{4,12},{8,16},{12,20},{16,24},{20,28},{24,0},{28,4},{1,9},{5... | collective-permute-start | bytes 1572872 | tf_op jit(solution)/shard_map/ppermute | solution.py:355
  65.9 21.9 %collective-permute-start.11 = (bf16[512,512]{1,0:T(8,128)(2,1)}, bf16[512,512]{1,0:T(8,128)(2,1)S(1)}, u32[]{:S(2)}, u32[]{:S(2)}) collective-permute-start(bf16[512,512]{1,0:T(8,128)(2,1)} %collective-permute-done.9.refs_2_), channel_id=1, source_target_pairs={{0,8},{4,12},{8,16},{12,20},{16,24},{20,28},{24,0},{28,4},{1,9},{5... | collective-permute-start | bytes 1572872 | tf_op jit(solution)/shard_map/ppermute | solution.py:355
  67.6 1.0 copy-start.2
  68.6 1.0 copy-start.4
  69.7 0.6 copy-start.10
  70.3 2.9 %copy-start.6 = (bf16[512,512]{1,0:T(8,128)(2,1)S(1)}, bf16[512,512]{1,0:T(8,128)(2,1)}, u32[]{:S(2)}) copy-start(bf16[512,512]{1,0:T(8,128)(2,1)} %copy-done.5) | copy-start | bytes 1572868
  73.2 9.7 %copy-start.11 = (s32[3]{0:T(128)S(1)}, s32[3]{0:T(128)}, u32[]{:S(2)}) copy-start(s32[3]{0:T(128)} %copy-done.9) | copy-start | bytes 40
  87.9 7.3 %copy-start.12 = (f32[8]{0:T(128)S(1)}, f32[8]{0:T(128)}, u32[]{:S(2)}) copy-start(f32[8]{0:T(128)} %param.15) | copy-start | bytes 100
  90.1 7.9 %collective-permute-start.13 = (bf16[144,512]{1,0:T(8,128)(2,1)S(1)}, bf16[144,512]{1,0:T(8,128)(2,1)S(1)}, u32[]{:S(2)}, u32[]{:S(2)}) collective-permute-start(bf16[144,512]{1,0:T(8,128)(2,1)S(1)} %get-tuple-element.38), channel_id=1, source_target_pairs={{0,8},{4,12},{8,16},{12,20},{16,24},{20,28},{1,9},{5,13},{9,17},{1... | collective-permute-start | bytes 442376 | tf_op jit(solution)/shard_map/ppermute | solution.py:355
  93.8 9.0 %collective-permute-start.14 = (bf16[144,512]{1,0:T(8,128)(2,1)S(1)}, bf16[144,512]{1,0:T(8,128)(2,1)S(1)}, u32[]{:S(2)}, u32[]{:S(2)}) collective-permute-start(bf16[144,512]{1,0:T(8,128)(2,1)S(1)} %get-tuple-element.38), channel_id=1, source_target_pairs={{0,16},{4,20},{8,24},{12,28},{1,17},{5,21},{9,25},{13,29},{2,18},{... | collective-permute-start | bytes 442376 | tf_op jit(solution)/shard_map/ppermute | solution.py:355
  103.7 7.4 %collective-permute-start.15 = (bf16[256,512]{1,0:T(8,128)(2,1)S(1)}, bf16[256,512]{1,0:T(8,128)(2,1)S(1)}, u32[]{:S(2)}, u32[]{:S(2)}) collective-permute-start(bf16[256,512]{1,0:T(8,128)(2,1)S(1)} %shard_map.89), channel_id=1, source_target_pairs={{0,4},{4,0},{8,12},{12,8},{16,20},{20,16},{24,28},{28,24},{1,5},{5... | collective-permute-start | bytes 786440 | tf_op jit(solution)/shard_map/ppermute | solution.py:355

commit v4 on v3

--- a/solution.py
+++ b/solution.py
@@ -13,6 +13,7 @@
 DOC_MAX = 1024
 LANES = 2
 PLANES = 4
+SUBLANES = 8
 
 
 def passed_along(x, axis, by):
@@ -116,7 +117,7 @@
     return jnp.where(first, one, other)
 
 
-def call(body, outs, *operands, flops=0, scratch=()):
+def call(body, outs, *operands, flops=0, scratch=(), left=0, grant=16):
     single = not isinstance(outs, list)
     shapes = [outs] if single else outs
     size = sum(math.prod(o.shape) * o.dtype.itemsize for o in (*operands, *shapes))
@@ -124,10 +125,11 @@
         body,
         out_shape=shapes,
         in_specs=[pl.BlockSpec(memory_space=pltpu.SMEM)]
-        + [pl.BlockSpec(memory_space=pltpu.VMEM)] * (len(operands) - 1),
+        + [pl.BlockSpec(memory_space=pltpu.VMEM)] * (len(operands) - 1 - left)
+        + [pl.BlockSpec(memory_space=pl.ANY)] * left,
         out_specs=[pl.BlockSpec(memory_space=pltpu.VMEM)] * len(shapes),
         scratch_shapes=list(scratch),
-        compiler_params=pltpu.CompilerParams(vmem_limit_bytes=40 * 2**20),
+        compiler_params=pltpu.CompilerParams(vmem_limit_bytes=grant * 2**20),
         cost_estimate=pl.CostEstimate(flops=flops, bytes_accessed=size, transcendentals=0),
     )(*operands)
     return result[0] if single else result
@@ -150,32 +152,81 @@
     return own, jnp.where(is_near, near_ref[:, inside], far_ref[:, inside])
 
 
-def share_kernel(used, place, hidden, near, far, s0, s1, s2, s3, out):
+def split_kernel(place, x_weight, bc, dt, ids, hidden, own, sent, small, ahead, below, ids_in, done):
+    f32, bf16 = jnp.float32, jnp.bfloat16
+    plane, lane, core = place[0], place[1], place[2]
+    size, half = x_weight.shape[0], x_weight.shape[1] // 2
+    maps, heads, rows = bc.shape[0], dt.shape[0], ids.shape[1]
+    at = LANES * ((plane + 1) % PLANES) + core
+
+    def columns(ref, index, width):
+        return ref.at[:, pl.ds(pl.multiple_of(index * width, width), width)]
+
+    moves = [
+        (columns(hidden, at, size), ahead),
+        (columns(x_weight, lane, half), own.at[pl.ds(0, size), :]),
+        (columns(x_weight, 1 - lane, half), sent),
+        (bc, own.at[pl.ds(size, maps), :]),
+        (bc, small.at[pl.ds(0, maps), :]),
+        (dt, below),
+        (ids, ids_in),
+    ]
+    copies = [pltpu.make_async_copy(a, b, done.at[i]) for i, (a, b) in enumerate(moves)]
+    for copy in copies:
+        copy.start()
+    for copy in copies:
+        copy.wait()
+    row = lax.broadcasted_iota(jnp.int32, (heads, rows), 0)
+    notes = jnp.where(row == 0, ids_in[...].astype(f32), 0.0)
+    notes = jnp.concatenate([notes, jnp.zeros((heads, size - rows), f32)], axis=1)
+    last = jnp.concatenate([below[...].astype(f32), notes], axis=0).astype(bf16)
+    own[size + maps :, :] = last
+    small[maps:, :] = last
+
+
+def share_kernel(used, place, hidden, near, far, c0, c1, c2, s3, out, small, done):
     plane, lane = place[0], place[1]
     rows = hidden.shape[0]
-    size = s0.shape[1]
+    size = c0.shape[1]
+    below = pl.ds(size, c0.shape[0] - size)
+    copies = [
+        pltpu.make_async_copy(c.at[below, :], small.at[i], done.at[i])
+        for i, c in enumerate((c0, c1, c2))
+    ]
+    copies.append(pltpu.make_async_copy(s3, small.at[3], done.at[3]))
+    for copy in copies:
+        copy.start()
     totals = [None, None]
-    for back, s in enumerate((s0, s1, s2, s3)):
+    for back, copy in enumerate(copies):
         at = LANES * ((plane + PLANES - back) % PLANES) + lane
-        weights = s[...]
+        copy.wait()
+        weights = small[back]
         for r, tokens in enumerate(depth_blocks(place, (hidden, near, far), at, size)):
             product = contract_last(weights, tokens)
             totals[r] = product if totals[r] is None else totals[r] + product
-    row = lax.broadcasted_iota(jnp.int32, (s0.shape[0] - used, rows), 0)
-    ids = s0[used:, :rows].astype(jnp.float32)
-    ends = [s[used:, :rows].astype(jnp.float32)[0:1, rows - 1 : rows] for s in (s1, s2)]
-    notes = jnp.where(row == 1, ends[0], jnp.where(row == 2, ends[1], ids))
+    notes = [small[i, used:, :rows].astype(jnp.float32) for i in range(3)]
+    row = lax.broadcasted_iota(jnp.int32, notes[0].shape, 0)
+    ends = [n[0:1, rows - 1 : rows] for n in notes[1:]]
+    note = jnp.where(row == 1, ends[0], jnp.where(row == 2, ends[1], notes[0]))
     out[:used, :rows] = totals[0][:used]
     out[:used, rows:] = totals[1][:used]
-    out[used:, :rows] = notes
-    out[used:, rows:] = jnp.zeros_like(notes)
+    out[used:, :rows] = note
+    out[used:, rows:] = jnp.zeros_like(note)
 
 
 def decay_kernel(
-    map_cols, place, maps, total, bias, rate_of, mixing, loaded, c_out, fac, meta
+    map_cols, place, some, some_core, some_chip, some_both, total, bias, rate_of, mixing, loaded, c_out, fac, meta
 ):
     f32, bf16 = jnp.float32, jnp.bfloat16
     plane, lane = place[0], place[1]
+    first_core, first_chip = place[2] == 0, place[3] == 0
+    here = [pick(first_core, a[...], b[...]) for a, b in ((some, some_core), (some_core, some))]
+    there = [
+        pick(first_core, a[...], b[...])
+        for a, b in ((some_chip, some_both), (some_both, some_chip))
+    ]
+    here, there = jnp.concatenate(here, axis=0), jnp.concatenate(there, axis=0)
+    b_maps, c_maps = pick(first_chip, here, there), pick(first_chip, there, here)
     heads = bias.shape[0]
     mine = heads // 2
     rows = total.shape[1] // 2
@@ -231,7 +282,7 @@
         fac[b] = factor.T
         cols = jnp.concatenate([cum[:mine], jnp.broadcast_to(seg, (8 - mine, rows))], axis=0).T
         keep = causal & (cols[:, mine : mine + 1] == seg)
-        b_t, c_t = maps[:NS, cut], maps[NS:, cut]
+        b_t, c_t = b_maps[:, cut], c_maps[:, cut]
         c_rows = c_t.astype(f32).T.astype(bf16)
         c_out[b] = c_rows
         scores = mul(c_rows, b_t)
@@ -248,8 +299,9 @@
     plane, lane = place[0], place[1]
     for (back, is_own), w in zip(backs, weight_refs):
         at = LANES * ((plane + PLANES - back) % PLANES) + (lane if is_own else 1 - lane)
-        weights = w[...]
-        for r, tokens in enumerate(depth_blocks(place, token_refs, at, w.shape[0])):
+        size = w.shape[1]
+        weights = w[:size, :]
+        for r, tokens in enumerate(depth_blocks(place, token_refs, at, size)):
             product = mul(tokens, weights)
             totals[r] = product if totals[r] is None else totals[r] + product
 
@@ -265,12 +317,21 @@
     out[1] = totals[1]
 
 
-def input_kernel(place, hidden, near, far, acc, last_own, last_other, loaded, meta, x_out, ready, built_out):
+def neighbour_kernel(place, mine, far, own, other, out):
+    same = place[1] == place[2]
+    size = other.shape[0]
+    here, there = mine[...], far[...]
+    first, second = jnp.where(same, here, there), jnp.where(same, there, here)
+    out[...] = (mul(first, own[:size, :]) + mul(second, other[...])).astype(out.dtype)
+
+
+def input_kernel(backs, place, hidden, near, far, acc, back, *refs):
+    *chunks, loaded, meta, x_out, ready, built_out = refs
     f32, bf16 = jnp.float32, jnp.bfloat16
     lane = place[1]
-    totals = [acc[0], acc[1]]
-    backs = ((PLANES - 1, True), (PLANES - 1, False))
-    add_products(place, (hidden, near, far), backs, (last_own, last_other), totals)
+    rows = hidden.shape[0]
+    totals = [acc[0] + back[:rows, :].astype(f32), acc[1] + back[rows : 2 * rows, :].astype(f32)]
+    add_products(place, (hidden, near, far), backs, chunks, totals)
     x_out[lane] = totals[0].astype(bf16)
     x_out[1 - lane] = totals[1].astype(bf16)
     mine = loaded.shape[1]
@@ -327,7 +388,7 @@
     lane, plane = me % LANES, me // LANES
     even = lane == 0
     core = lax.axis_index("rep") % 2
-    place = jnp.stack([plane, lane, core]).astype(jnp.int32)
+    place = jnp.stack([plane, lane, core, lax.axis_index("rep") // 2]).astype(jnp.int32)
     rows, depth = hidden.shape
     k_rows, cols = x_weight.shape
     half = cols // 2
@@ -344,20 +405,89 @@
 
     swap = [(i, i ^ 1) for i in range(LANES * PLANES)]
     cores = [(i, i ^ 1) for i in range(lax.axis_size("rep"))]
+    chips = [(i, i ^ 2) for i in range(lax.axis_size("rep"))]
 
     def shift(by, sources):
         return [(at(p, l), at(p + by, l)) for p in sources for l in range(LANES)]
 
-    def ring(by):
-        return [(at(p, l), at((p + by) % PLANES, l)) for p in range(PLANES) for l in range(LANES)]
+    along = [(at(p, l), at((p + 1) % PLANES, l)) for p in range(PLANES) for l in range(LANES)]
+    back = [(b, a) for a, b in along]
 
     def send(x, pairs, axis="seq"):
         return lax.ppermute(x, axis, pairs)
 
     together = lax.optimization_barrier
-    along = ring(1)
-
-    def add_early(backs, *operands):
+
+    own, sent, small, ahead = call(
+        split_kernel,
+        [
+            shaped(bf16, k_rows + used + heads, half),
+            shaped(bf16, k_rows, half),
+            shaped(bf16, used + heads, k_rows),
+            shaped(bf16, rows, k_rows),
+        ],
+        place,
+        x_weight,
+        bc_weight.T,
+        dt_weight.T,
+        seg_ids[None],
+        hidden,
+        left=5,
+        grant=60,
+        scratch=[
+            pltpu.VMEM((heads, k_rows), bf16),
+            pltpu.VMEM((1, rows), jnp.int32),
+            pltpu.SemaphoreType.DMA((7,)),
+        ],
+    )
+    ahead = send(ahead, along)
+    other = send(sent, swap)
+    own_one = send(own, along)
+    small_next = send(small, back)
+    near = pick(core == 0, hidden[:, : depth // 2], hidden[:, depth // 2 :])
+    ahead_other = send(ahead, swap)
+    other, own_one, near, ahead, ahead_other = together((other, own_one, near, ahead, ahead_other))
+
+    other_one = send(other, along)
+    own_two = send(own_one, along)
+    near = send(near, swap)
+    ahead = jnp.concatenate([ahead, ahead_other], axis=0)
+    ahead_far = send(ahead, cores, "rep")
+    part = call(
+        neighbour_kernel,
+        shaped(bf16, LANES * rows, half),
+        place,
+        ahead,
+        ahead_far,
+        own,
+        other,
+        flops=4 * rows * LANES * k_rows * half,
+    )
+    other_one, own_two, near, part = together((other_one, own_two, near, part))
+
+    other_two = send(other_one, along)
+    from_next = send(part, back)
+    far = send(near, cores, "rep")
+    share = call(
+        functools.partial(share_kernel, used),
+        shaped(f32, used + heads, LANES * rows),
+        place,
+        hidden,
+        near,
+        far,
+        own,
+        own_one,
+        own_two,
+        small_next,
+        flops=4 * rows * depth * used,
+        left=PLANES,
+        scratch=[
+            pltpu.VMEM((PLANES, used + heads, k_rows), bf16),
+            pltpu.SemaphoreType.DMA((PLANES,)),
+        ],
+    )
+
+    def early_products(backs, chunks, *totals):
         return call(
             functools.partial(early_kernel, backs),
             shaped(f32, LANES, rows, half),
@@ -365,47 +495,21 @@
             hidden,
             near,
             far,
-            *operands,
+            *totals,
+            *chunks,
             flops=4 * rows * k_rows * half * len(backs),
         )
 
-    own = pick(even, x_weight[:, :half], x_weight[:, half:])
-    other = send(pick(even, x_weight[:, half:], x_weight[:, :half]), swap)
-    own_one = send(own, along)
-    other_one = send(other, along)
-    own_two = send(own_one, along)
-    other_two = send(other_one, along)
-    own_three = send(own_two, along)
-    other_three = send(other_two, along)
-
-    ids_row = jnp.pad(seg_ids.astype(bf16), (0, k_rows - rows))[None]
-    small = jnp.concatenate(
-        [bc_weight.T, dt_weight.T, ids_row, jnp.zeros((7, k_rows), bf16)], axis=0
-    )
-    near = pick(core == 0, hidden[:, : depth // 2], hidden[:, depth // 2 :])
-    from_ring = [send(small, ring(by)) for by in (1, 2, 3)]
-    near, from_ring, _ = together((near, from_ring, (other, own_one)))
-    near = send(near, swap)
-    near, from_ring, _ = together((near, from_ring, (own_two, other_one)))
-    far = send(near, cores, "rep")
-    share = call(
-        functools.partial(share_kernel, used),
-        shaped(f32, used + 8, LANES * rows),
-        place,
-        hidden,
-        near,
-        far,
-        small,
-        *from_ring,
-        flops=4 * rows * depth * used,
-    )
-    early = add_early(
-        ((0, True), (0, False), (1, True), (1, False)), own, other, own_one, other_one
-    )
+    early = early_products(
+        ((0, True), (0, False), (1, True), (1, False)), (own, other, own_one, other_one)
+    )
+    early = early_products(((2, True),), (own_two,), early)
     share_other = send(share, swap)
     total = share + jnp.concatenate([share_other[:, rows:], share_other[:, :rows]], axis=1)
-    total, _ = together((total, own_three))
-    maps = lax.all_gather(total[:map_cols].astype(bf16), "rep", axis=0, tiled=True)
+    some = total[:map_cols].astype(bf16)
+    some_core = send(some, cores, "rep")
+    some_chip = send(some, chips, "rep")
+    some_both = send(some_chip, cores, "rep")
     mixing, loaded, c_rows, fac, meta = call(
         functools.partial(decay_kernel, map_cols),
         [
@@ -416,15 +520,17 @@
             shaped(f32, 8, half),
         ],
         place,
-        maps,
+        some,
+        some_core,
+        some_chip,
+        some_both,
         total,
         dt_bias[:, None],
         decay_rate[:, None],
         flops=100 * mine * rows * rows,
     )
-    early = add_early(((2, True), (2, False)), early, own_two, other_two)
     inputs, ready, built = call(
-        input_kernel,
+        functools.partial(input_kernel, ((2, False),)),
         [
             shaped(bf16, LANES, rows, half),
             shaped(bf16, NS + 16, half),
@@ -435,8 +541,8 @@
         near,
         far,
         early,
-        own_three,
-        other_three,
+        from_next,
+        other_two,
         loaded,
         meta,
         flops=rows * depth * half,
@@ -479,6 +585,21 @@
     )
 
 
+def shards(hidden, seg_ids, x_weight, bc_weight, dt_weight, dt_bias, decay_rate, skip):
+    heads = dt_bias.shape[0]
+    by_planes = (
+        lax.axis_size("seq") == LANES * PLANES
+        and lax.axis_size("rep") == 4
+        and heads == SUBLANES
+        and 2 * x_weight.shape[0] == x_weight.shape[1] == heads * P_SIZE
+        and 2 * bc_weight.shape[1] == NS
+        and hidden.shape[0] <= x_weight.shape[0]
+        and 2 * LANES * hidden.shape[0] >= DOC_MAX
+    )
+    plan = plane_shards if by_planes else gathered_shards
+    return plan(hidden, seg_ids, x_weight, bc_weight, dt_weight, dt_bias, decay_rate, skip)
+
+
 def solution(mesh):
     placed = (
         P("seq", None),
@@ -490,9 +611,8 @@
         P("rep"),
         P("rep"),
     )
-    by_planes = mesh.shape["seq"] == LANES * PLANES and mesh.shape["rep"] % 2 == 0
     return jax.shard_map(
-        plane_shards if by_planes else gathered_shards,
+        shards,
         mesh=mesh,
         in_specs=placed,
         out_specs=P("seq", "rep"),

time: 114 us -> 112 us (0.982)
  blocking collectives: 5.79 us -> 0 us
  Pallas kernels: 13.6 us -> 17.6 us
  starting transfers between devices: 21.4 us -> 23.4 us
  waiting for transfers between devices: 60.9 us -> 58.9 us
  other arithmetic: 3.45 us -> 1.7 us
  local copies, waits for them, and re-layouts: 6.61 us -> 8.23 us
    all_gather x1 -> x0, blocking collectives: 5.79 us -> none  [plane_shards(): lax.all_gather(total[:map_cols].astype(bf16), 'rep', axis=0, tiled=True)]
    pallas_call x8 -> x10, Pallas kernels: 13.6 us -> 17.6 us  [call(): pl.pallas_call(body, out_shape=shapes, in_specs=[pl.BlockSpec(memory_spac...]
    select_n x3 -> x2, other arithmetic: 3.26 us -> 1.04 us  [pick(): return jnp.where(first, one, other)]
    ppermute x16 -> x19, waiting for transfers between devices: 60.9 us -> 58.9 us  [send(): return lax.ppermute(x, axis, pairs)]
    ppermute x16 -> x19, starting transfers between devices: 21.4 us -> 23.4 us  [send(): return lax.ppermute(x, axis, pairs)]
    unnamed x32 -> x53, local copies, waits for them, and re-layouts: 5.03 us -> 6.84 us
  transfers between devices with their start and end apart: 16 -> 19, of which waited for: 10 -> 12; matrix products, arithmetic and copies ran while one was open for 2% -> 1% of each run, Pallas kernels for 9% -> 8%
where the time goes in v4:
time: 112 us; the launch traced here: 110 us
  waiting for transfers between devices  58.9 us (53%)
  starting transfers between devices  23.4 us (21%)
  Pallas kernels  17.6 us (16%)
  local copies, waits for them, and re-layouts  8.23 us (7%)
  other arithmetic  1.7 us (2%)
    ppermute x19, waiting for transfers between devices, send(): return lax.ppermute(x, axis, pairs)  58.9 us
    ppermute x19, starting transfers between devices, send(): return lax.ppermute(x, axis, pairs)  23.4 us
    pallas_call x10, Pallas kernels, call(): pl.pallas_call(body, out_shape=shapes, in_specs=[pl.BlockSpec(memory_spac...  17.6 us
    unnamed x53, local copies, waits for them, and re-layouts  6.84 us
  transfers between devices with their start and end apart: 19, of which 12 were waited for; matrix products, arithmetic and copies ran while one was open for 1% of the time, Pallas kernels for 8%

profile of v4, /device:TPU:16, one launch (start us, length us, event | category | flops | bytes accessed | tf_op | source)
XLA Modules:
  0.0 110.1 jit_solution(17970102055643856623)
XLA Ops:
  0.0 0.6 pad_add_fusion.place
  0.6 3.3 %shard_map.82 = (bf16[592,512]{1,0:T(8,128)(2,1)}, bf16[512,512]{1,0:T(8,128)(2,1)}, bf16[80,512]{1,0:T(8,128)(2,1)}, bf16[256,512]{1,0:T(8,128)(2,1)}) custom-call(s32[4]{0:T(128)} %pad_add_fusion.place, bf16[512,1024]{1,0:T(8,128)(2,1)} %x_weight.1, bf16[64,512]{1,0:T(8,128)(2,1)} %bitcast.11, bf16[8,512]{1,0:T(8,128)(2,1)} %bitcast.12, ...), custom_call_target="tpu_custom_call" | custom-call | bytes 4695056 | tf_op jit(solution)/shard_map/pallas_call | solution.py:124
  3.9 1.6 %collective-permute-start.2 = (bf16[256,512]{1,0:T(8,128)(2,1)}, bf16[256,512]{1,0:T(8,128)(2,1)S(1)}, u32[]{:S(2)}, u32[]{:S(2)}) collective-permute-start(bf16[256,512]{1,0:T(8,128)(2,1)} %get-tuple-element.28), channel_id=1, source_target_pairs={{0,8},{4,12},{8,16},{12,20},{16,24},{20,28},{24,0},{28,4},{1,9},{5... | collective-permute-start | bytes 786440 | tf_op jit(solution)/shard_map/ppermute | solution.py:417
  5.5 0.1 collective-permute-start.1
  5.6 1.7 %collective-permute-start = (bf16[512,512]{1,0:T(8,128)(2,1)}, bf16[512,512]{1,0:T(8,128)(2,1)S(1)}, u32[]{:S(2)}, u32[]{:S(2)}) collective-permute-start(bf16[512,512]{1,0:T(8,128)(2,1)} %get-tuple-element.26), channel_id=1, source_target_pairs={{0,4},{4,0},{8,12},{12,8},{16,20},{20,16},{24,28},{28,24},{1,5},{5... | collective-permute-start | bytes 1572872 | tf_op jit(solution)/shard_map/ppermute | solution.py:417
  7.3 6.1 %collective-permute-done.2 = bf16[256,512]{1,0:T(8,128)(2,1)S(1)} collective-permute-done((bf16[256,512]{1,0:T(8,128)(2,1)}, bf16[256,512]{1,0:T(8,128)(2,1)S(1)}, u32[]{:S(2)}, u32[]{:S(2)}) %collective-permute-start.2) | collective-permute-done | bytes 262176 | tf_op jit(solution)/shard_map/ppermute | solution.py:417
  13.3 1.5 %collective-permute-start.3 = (bf16[256,512]{1,0:T(8,128)(2,1)S(1)}, bf16[256,512]{1,0:T(8,128)(2,1)S(1)}, u32[]{:S(2)}, u32[]{:S(2)}) collective-permute-start(bf16[256,512]{1,0:T(8,128)(2,1)S(1)} %collective-permute-done.2), channel_id=1, source_target_pairs={{0,4},{4,0},{8,12},{12,8},{16,20},{20,16},{24,28},{28,24},{1,5},{5... | collective-permute-start | bytes 786440 | tf_op jit(solution)/shard_map/ppermute | solution.py:417
  14.9 0.1 slice_select_fusion
  15.0 5.7 %collective-permute-done.other.refs_1_ = bf16[512,512]{1,0:T(8,128)(2,1)S(1)} collective-permute-done((bf16[512,512]{1,0:T(8,128)(2,1)}, bf16[512,512]{1,0:T(8,128)(2,1)S(1)}, u32[]{:S(2)}, u32[]{:S(2)}) %collective-permute-start) | collective-permute-done | bytes 524320 | tf_op jit(solution)/shard_map/ppermute | solution.py:417
  20.6 4.2 %collective-permute-done.3 = bf16[256,512]{1,0:T(8,128)(2,1)S(1)} collective-permute-done((bf16[256,512]{1,0:T(8,128)(2,1)S(1)}, bf16[256,512]{1,0:T(8,128)(2,1)S(1)}, u32[]{:S(2)}, u32[]{:S(2)}) %collective-permute-start.3) | collective-permute-done | bytes 262176 | tf_op jit(solution)/shard_map/ppermute | solution.py:417
  24.8 0.0 copy-done.8
  24.8 0.5 collective-permute-done.1.refs_2_.c1
  25.3 1.5 %collective-permute-start.6 = (bf16[256,2048]{1,0:T(8,128)(2,1)S(1)}, bf16[256,2048]{1,0:T(8,128)(2,1)S(1)}, u32[]{:S(2)}, u32[]{:S(2)}) collective-permute-start(bf16[256,2048]{1,0:T(8,128)(2,1)S(1)} %slice_select_fusion), channel_id=1, source_target_pairs={{0,4},{4,0},{8,12},{12,8},{16,20},{20,16},{24,28},{28,24},{1,5},{5... | collective-permute-start | bytes 3145736 | tf_op jit(solution)/shard_map/ppermute | solution.py:417
  26.8 1.6 %collective-permute-start.5 = (bf16[592,512]{1,0:T(8,128)(2,1)}, bf16[592,512]{1,0:T(8,128)(2,1)S(1)}, u32[]{:S(2)}, u32[]{:S(2)}) collective-permute-start(bf16[592,512]{1,0:T(8,128)(2,1)} %collective-permute-done.1.refs_2_.c1), channel_id=1, source_target_pairs={{0,8},{4,12},{8,16},{12,20},{16,24},{20,28},{24,0},{28,4},{1,9},{5... | collective-permute-start | bytes 1818632 | tf_op jit(solution)/shard_map/ppermute | solution.py:417
  28.4 0.1 collective-permute-start.7
  28.5 2.1 %collective-permute-start.4 = (bf16[512,512]{1,0:T(8,128)(2,1)}, bf16[512,512]{1,0:T(8,128)(2,1)}, u32[]{:S(2)}, u32[]{:S(2)}) collective-permute-start(bf16[512,512]{1,0:T(8,128)(2,1)} %copy-done.8), channel_id=1, source_target_pairs={{0,8},{4,12},{8,16},{12,20},{16,24},{20,28},{24,0},{28,4},{1,9},{5... | collective-permute-start | bytes 1572872 | tf_op jit(solution)/shard_map/ppermute | solution.py:417
  30.7 0.0 collective-permute-done.7.far
  30.7 0.0 copy-done.17
  30.7 1.1 copy-done.9
  31.7 2.0 %shard_map.83 = bf16[512,512]{1,0:T(8,128)(2,1)} custom-call(s32[4]{0:T(128)S(1)} %copy-done.17, bf16[512,512]{1,0:T(8,128)(2,1)S(1)} %constant_dynamic-update-slice_fusion.mine, bf16[512,512]{1,0:T(8,128)(2,1)S(1)} %collective-permute-done.7.far, bf16[592,512]{1,0:T(8,128)(2,1)S(1)} %copy-done.4, bf16[512,512]{1,0:T(8,128)(2,1)S(1)} %copy-done.9), custom_call_target="tpu_custom_call" | custom-call | flops 536870912 | bytes 2703376 | tf_op jit(solution)/shard_map/pallas_call | solution.py:124
  33.8 18.9 %collective-permute-done.4.refs_3_ = bf16[512,512]{1,0:T(8,128)(2,1)} collective-permute-done((bf16[512,512]{1,0:T(8,128)(2,1)}, bf16[512,512]{1,0:T(8,128)(2,1)}, u32[]{:S(2)}, u32[]{:S(2)}) %collective-permute-start.4) | collective-permute-done | bytes 524320 | tf_op jit(solution)/shard_map/ppermute | solution.py:417
  52.6 0.0 collective-permute-done.5.refs_1_.c2
  52.6 0.0 collective-permute-done.6.near
  52.6 0.1 collective-permute-start.8
  52.7 0.0 copy-start.23
  52.7 0.0 copy-start.24
  52.8 1.1 %collective-permute-start.11 = (bf16[80,512]{1,0:T(8,128)(2,1)S(1)}, bf16[80,512]{1,0:T(8,128)(2,1)S(1)}, u32[]{:S(2)}, u32[]{:S(2)}) collective-permute-start(bf16[80,512]{1,0:T(8,128)(2,1)S(1)} %copy-done.25), channel_id=1, source_target_pairs={{8,0},{12,4},{16,8},{20,12},{24,16},{28,20},{0,24},{4,28},{9,1},{1... | collective-permute-start | bytes 245768 | tf_op jit(solution)/shard_map/ppermute | solution.py:417
  53.9 3.7 %collective-permute-done.11.s3 = bf16[80,512]{1,0:T(8,128)(2,1)S(1)} collective-permute-done((bf16[80,512]{1,0:T(8,128)(2,1)S(1)}, bf16[80,512]{1,0:T(8,128)(2,1)S(1)}, u32[]{:S(2)}, u32[]{:S(2)}) %collective-permute-start.11) | collective-permute-done | bytes 81952 | tf_op jit(solution)/shard_map/ppermute | solution.py:417
  57.6 0.0 collective-permute-done.8.far
  57.6 2.4 %shard_map.86 = f32[80,512]{1,0:T(8,128)S(1)} custom-call(s32[4]{0:T(128)S(1)} %copy-done.17, bf16[256,4096]{1,0:T(8,128)(2,1)S(1)} %copy-done, bf16[256,2048]{1,0:T(8,128)(2,1)S(1)} %collective-permute-done.6.near, bf16[256,2048]{1,0:T(8,128)(2,1)S(1)} %collective-permute-done.8.far, bf16[592,512]{1,0:T(8,128)(2,1)S(1)} %copy-done.4, ...), custom_call_target="tpu_custom_call" | custom-call | flops 301989888 | bytes 6258704 | tf_op jit(solution)/shard_map/pallas_call | solution.py:124
  60.0 0.6 collective-permute-start.12
  60.6 2.4 %collective-permute-start.9 = (bf16[512,512]{1,0:T(8,128)(2,1)}, bf16[512,512]{1,0:T(8,128)(2,1)}, u32[]{:S(2)}, u32[]{:S(2)}) collective-permute-start(bf16[512,512]{1,0:T(8,128)(2,1)} %shard_map.83), channel_id=1, source_target_pairs={{8,0},{12,4},{16,8},{20,12},{24,16},{28,20},{0,24},{4,28},{9,1},{1... | collective-permute-start | bytes 1572872 | tf_op jit(solution)/shard_map/ppermute | solution.py:417
  63.0 1.6 %collective-permute-start.10 = (bf16[512,512]{1,0:T(8,128)(2,1)}, bf16[512,512]{1,0:T(8,128)(2,1)}, u32[]{:S(2)}, u32[]{:S(2)}) collective-permute-start(bf16[512,512]{1,0:T(8,128)(2,1)} %collective-permute-done.4.refs_3_), channel_id=1, source_target_pairs={{0,8},{4,12},{8,16},{12,20},{16,24},{20,28},{24,0},{28,4},{1,9},{5... | collective-permute-start | bytes 1572872 | tf_op jit(solution)/shard_map/ppermute | solution.py:417
  64.6 1.2 %collective-permute-done.12 = f32[80,512]{1,0:T(8,128)S(1)} collective-permute-done((f32[80,512]{1,0:T(8,128)S(1)}, f32[80,512]{1,0:T(8,128)S(1)}, u32[]{:S(2)}, u32[]{:S(2)}) %collective-permute-start.12) | collective-permute-done | bytes 163872 | tf_op jit(solution)/shard_map/ppermute | solution.py:417
  65.9 0.7 copy-done.11
  66.6 1.5 %collective-permute-start.14 = (bf16[64,512]{1,0:T(8,128)(2,1)S(1)}, bf16[64,512]{1,0:T(8,128)(2,1)S(1)}, u32[]{:S(2)}, u32[]{:S(2)}) collective-permute-start(bf16[64,512]{1,0:T(8,128)(2,1)S(1)} %slice.27.some), channel_id=1, source_target_pairs={{0,2},{1,3},{2,0},{3,1},{4,6},{5,7},{6,4},{7,5},{8,10},{9,11},{10,... | collective-permute-start | bytes 196616 | tf_op jit(solution)/shard_map/ppermute | solution.py:417
  68.1 0.7 copy.9.bias
  68.7 0.7 copy.10.rate_of
  69.4 0.0 collective-permute-start.13
  69.4 1.4 %collective-permute-done.14.some_chip = bf16[64,512]{1,0:T(8,128)(2,1)S(1)} collective-permute-done((bf16[64,512]{1,0:T(8,128)(2,1)S(1)}, bf16[64,512]{1,0:T(8,128)(2,1)S(1)}, u32[]{:S(2)}, u32[]{:S(2)}) %collective-permute-start.14) | collective-permute-done | bytes 65568 | tf_op jit(solution)/shard_map/ppermute | solution.py:417
  70.8 0.0 collective-permute-start.15
  70.8 1.2 %copy-done.2 = bf16[256,2048]{1,0:T(8,128)(2,1)S(1)} copy-done((bf16[256,2048]{1,0:T(8,128)(2,1)S(1)}, bf16[256,2048]{1,0:T(8,128)(2,1)}, u32[]{:S(2)}) %copy-start.2) | copy-done | bytes 1048600
  72.1 1.1 copy-done.5
  73.2 1.0 copy-done.10
  74.2 2.5 %shard_map.84.refs_0_ = f32[2,256,512]{2,1,0:T(8,128)S(1)} custom-call(s32[4]{0:T(128)S(1)} %copy-done.17, bf16[256,4096]{1,0:T(8,128)(2,1)S(1)} %copy-done, bf16[256,2048]{1,0:T(8,128)(2,1)S(1)} %collective-permute-done.6.near, bf16[256,2048]{1,0:T(8,128)(2,1)S(1)} %copy-done.2, bf16[592,512]{1,0:T(8,128)(2,1)S(1)} %copy-done.5, ...), custom_call_target="tpu_custom_call" | custom-call | flops 1073741824 | bytes 7503888 | tf_op jit(solution)/shard_map/pallas_call | solution.py:124
  76.8 1.0 shard_map.85.acc
  77.8 0.0 collective-permute-done.13.some_core
  77.8 0.0 collective-permute-done.15.some_both
  77.9 0.8 copy-done.14
  78.7 0.8 copy-done.16
  79.5 1.8 %shard_map.87 = (bf16[2,4,256,256]{3,2,1,0:T(8,128)(2,1)S(1)}, bf16[2,4,128,256]{3,2,1,0:T(8,128)(2,1)S(1)}, bf16[2,256,128]{2,1,0:T(8,128)(2,1)S(1)}, f32[2,256,8]{2,1,0:T(8,128)S(1)}, f32[8,512]{1,0:T(8,128)S(1)}) custom-call(s32[4]{0:T(128)S(1)} %copy-done.18, bf16[64,512]{1,0:T(8,128)(2,1)S(1)} %copy-done.14, ...), custom_call_target="tpu_custom_call" | custom-call | flops 26214400 | bytes 2162768 | tf_op jit(solution)/shard_map/pallas_call | solution.py:124
  81.3 0.0 collective-permute-done.9.back
  81.3 6.9 %collective-permute-done.10.refs_0_ = bf16[512,512]{1,0:T(8,128)(2,1)} collective-permute-done((bf16[512,512]{1,0:T(8,128)(2,1)}, bf16[512,512]{1,0:T(8,128)(2,1)}, u32[]{:S(2)}, u32[]{:S(2)}) %collective-permute-start.10) | collective-permute-done | bytes 524320 | tf_op jit(solution)/shard_map/ppermute | solution.py:417
  88.2 2.0 %shard_map.88 = (bf16[2,256,512]{2,1,0:T(8,128)(2,1)S(1)}, bf16[144,512]{1,0:T(8,128)(2,1)S(1)}, bf16[128,512]{1,0:T(8,128)(2,1)S(1)}) custom-call(s32[4]{0:T(128)S(1)} %copy-done.18, bf16[256,4096]{1,0:T(8,128)(2,1)S(1)} %copy-done, bf16[256,2048]{1,0:T(8,128)(2,1)S(1)} %collective-permute-done.6.near, bf16[256,2048]{1,0:T(8,128)(2,1)S(1)} %copy-done.3, ...), custom_call_target="tpu_custom_call" | custom-call | flops 536870912 | bytes 7634960 | tf_op jit(solution)/shard_map/pallas_call | solution.py:124
  90.2 3.3 %collective-permute-start.16 = (bf16[144,512]{1,0:T(8,128)(2,1)S(1)}, bf16[144,512]{1,0:T(8,128)(2,1)S(1)}, u32[]{:S(2)}, u32[]{:S(2)}) collective-permute-start(bf16[144,512]{1,0:T(8,128)(2,1)S(1)} %get-tuple-element.46), channel_id=1, source_target_pairs={{0,8},{4,12},{8,16},{12,20},{16,24},{20,28},{1,9},{5,13},{9,17},{1... | collective-permute-start | bytes 442376 | tf_op jit(solution)/shard_map/ppermute | solution.py:417
  93.4 1.3 %collective-permute-start.17 = (bf16[144,512]{1,0:T(8,128)(2,1)S(1)}, bf16[144,512]{1,0:T(8,128)(2,1)S(1)}, u32[]{:S(2)}, u32[]{:S(2)}) collective-permute-start(bf16[144,512]{1,0:T(8,128)(2,1)S(1)} %get-tuple-element.46), channel_id=1, source_target_pairs={{0,16},{4,20},{8,24},{12,28},{1,17},{5,21},{9,25},{13,29},{2,18},{... | collective-permute-start | bytes 442376 | tf_op jit(solution)/shard_map/ppermute | solution.py:417
  94.8 1.0 shard_map.89.local
  95.8 4.4 %collective-permute-done.16.one = bf16[144,512]{1,0:T(8,128)(2,1)S(1)} collective-permute-done((bf16[144,512]{1,0:T(8,128)(2,1)S(1)}, bf16[144,512]{1,0:T(8,128)(2,1)S(1)}, u32[]{:S(2)}, u32[]{:S(2)}) %collective-permute-start.16) | collective-permute-done | bytes 147488 | tf_op jit(solution)/shard_map/ppermute | solution.py:417
  100.2 1.7 %collective-permute-done.17.two = bf16[144,512]{1,0:T(8,128)(2,1)S(1)} collective-permute-done((bf16[144,512]{1,0:T(8,128)(2,1)S(1)}, bf16[144,512]{1,0:T(8,128)(2,1)S(1)}, u32[]{:S(2)}, u32[]{:S(2)}) %collective-permute-start.17) | collective-permute-done | bytes 147488 | tf_op jit(solution)/shard_map/ppermute | solution.py:417
  101.9 0.8 shard_map.91
  102.7 1.3 %collective-permute-start.18 = (bf16[256,512]{1,0:T(8,128)(2,1)S(1)}, bf16[256,512]{1,0:T(8,128)(2,1)S(1)}, u32[]{:S(2)}, u32[]{:S(2)}) collective-permute-start(bf16[256,512]{1,0:T(8,128)(2,1)S(1)} %shard_map.91), channel_id=1, source_target_pairs={{0,4},{4,0},{8,12},{12,8},{16,20},{20,16},{24,28},{28,24},{1,5},{5... | collective-permute-start | bytes 786440 | tf_op jit(solution)/shard_map/ppermute | solution.py:417
  104.1 0.8 shard_map.90
  104.9 4.3 %collective-permute-done.18 = bf16[256,512]{1,0:T(8,128)(2,1)S(1)} collective-permute-done((bf16[256,512]{1,0:T(8,128)(2,1)S(1)}, bf16[256,512]{1,0:T(8,128)(2,1)S(1)}, u32[]{:S(2)}, u32[]{:S(2)}) %collective-permute-start.18) | collective-permute-done | bytes 262176 | tf_op jit(solution)/shard_map/ppermute | solution.py:417
  109.2 0.9 maximum_select_fusion
  (46 shorter events, 0.2 us)
Async XLA Ops:
  0.0 14.9 %copy-start = (bf16[256,4096]{1,0:T(8,128)(2,1)S(1)}, bf16[256,4096]{1,0:T(8,128)(2,1)}, u32[]{:S(2)}) copy-start(bf16[256,4096]{1,0:T(8,128)(2,1)} %hidden.9) | copy-start | bytes 6291460
  3.9 9.5 %collective-permute-start.2 = (bf16[256,512]{1,0:T(8,128)(2,1)}, bf16[256,512]{1,0:T(8,128)(2,1)S(1)}, u32[]{:S(2)}, u32[]{:S(2)}) collective-permute-start(bf16[256,512]{1,0:T(8,128)(2,1)} %get-tuple-element.28), channel_id=1, source_target_pairs={{0,8},{4,12},{8,16},{12,20},{16,24},{20,28},{24,0},{28,4},{1,9},{5... | collective-permute-start | bytes 786440 | tf_op jit(solution)/shard_map/ppermute | solution.py:417
  5.5 19.8 %collective-permute-start.1 = (bf16[592,512]{1,0:T(8,128)(2,1)}, bf16[592,512]{1,0:T(8,128)(2,1)}, u32[]{:S(2)}, u32[]{:S(2)}) collective-permute-start(bf16[592,512]{1,0:T(8,128)(2,1)} %get-tuple-element.27.own.refs_0_.c0), channel_id=1, source_target_pairs={{0,8},{4,12},{8,16},{12,20},{16,24},{20,28},{24,0},{28,4},{1,9},{5... | collective-permute-start | bytes 1818632 | tf_op jit(solution)/shard_map/ppermute | solution.py:417
  5.6 15.1 %collective-permute-start = (bf16[512,512]{1,0:T(8,128)(2,1)}, bf16[512,512]{1,0:T(8,128)(2,1)S(1)}, u32[]{:S(2)}, u32[]{:S(2)}) collective-permute-start(bf16[512,512]{1,0:T(8,128)(2,1)} %get-tuple-element.26), channel_id=1, source_target_pairs={{0,4},{4,0},{8,12},{12,8},{16,20},{20,16},{24,28},{28,24},{1,5},{5... | collective-permute-start | bytes 1572872 | tf_op jit(solution)/shard_map/ppermute | solution.py:417
  7.3 23.4 %copy-start.4 = (bf16[592,512]{1,0:T(8,128)(2,1)S(1)}, bf16[592,512]{1,0:T(8,128)(2,1)}, u32[]{:S(2)}) copy-start(bf16[592,512]{1,0:T(8,128)(2,1)} %get-tuple-element.27.own.refs_0_.c0) | copy-start | bytes 1818628
  7.3 23.4 %copy-start.17 = (s32[4]{0:T(128)S(1)}, s32[4]{0:T(128)}, u32[]{:S(2)}) copy-start(s32[4]{0:T(128)} %pad_add_fusion.place) | copy-start | bytes 52
  13.3 11.5 %collective-permute-start.3 = (bf16[256,512]{1,0:T(8,128)(2,1)S(1)}, bf16[256,512]{1,0:T(8,128)(2,1)S(1)}, u32[]{:S(2)}, u32[]{:S(2)}) collective-permute-start(bf16[256,512]{1,0:T(8,128)(2,1)S(1)} %collective-permute-done.2), channel_id=1, source_target_pairs={{0,4},{4,0},{8,12},{12,8},{16,20},{20,16},{24,28},{28,24},{1,5},{5... | collective-permute-start | bytes 786440 | tf_op jit(solution)/shard_map/ppermute | solution.py:417
  15.0 37.7 %copy-start.25 = (bf16[80,512]{1,0:T(8,128)(2,1)S(1)}, bf16[80,512]{1,0:T(8,128)(2,1)}, u32[]{:S(2)}) copy-start(bf16[80,512]{1,0:T(8,128)(2,1)} %get-tuple-element.38) | copy-start | bytes 245764
  20.6 4.2 %copy-start.8 = (bf16[512,512]{1,0:T(8,128)(2,1)}, bf16[512,512]{1,0:T(8,128)(2,1)S(1)}, u32[]{:S(2)}) copy-start(bf16[512,512]{1,0:T(8,128)(2,1)S(1)} %collective-permute-done.other.refs_1_) | copy-start | bytes 1572868
  25.3 27.3 %collective-permute-start.6 = (bf16[256,2048]{1,0:T(8,128)(2,1)S(1)}, bf16[256,2048]{1,0:T(8,128)(2,1)S(1)}, u32[]{:S(2)}, u32[]{:S(2)}) collective-permute-start(bf16[256,2048]{1,0:T(8,128)(2,1)S(1)} %slice_select_fusion), channel_id=1, source_target_pairs={{0,4},{4,0},{8,12},{12,8},{16,20},{20,16},{24,28},{28,24},{1,5},{5... | collective-permute-start | bytes 3145736 | tf_op jit(solution)/shard_map/ppermute | solution.py:417
  26.8 25.8 %collective-permute-start.5 = (bf16[592,512]{1,0:T(8,128)(2,1)}, bf16[592,512]{1,0:T(8,128)(2,1)S(1)}, u32[]{:S(2)}, u32[]{:S(2)}) collective-permute-start(bf16[592,512]{1,0:T(8,128)(2,1)} %collective-permute-done.1.refs_2_.c1), channel_id=1, source_target_pairs={{0,8},{4,12},{8,16},{12,20},{16,24},{20,28},{24,0},{28,4},{1,9},{5... | collective-permute-start | bytes 1818632 | tf_op jit(solution)/shard_map/ppermute | solution.py:417
  28.4 2.2 %collective-permute-start.7 = (bf16[512,512]{1,0:T(8,128)(2,1)S(1)}, bf16[512,512]{1,0:T(8,128)(2,1)S(1)}, u32[]{:S(2)}, u32[]{:S(2)}) collective-permute-start(bf16[512,512]{1,0:T(8,128)(2,1)S(1)} %constant_dynamic-update-slice_fusion.mine), channel_id=1, source_target_pairs={{0,1},{1,0},{2,3},{3,2},{4,5},{5,4},{6,7},{7,6},{8,9},{9,8},{10,11... | collective-permute-start | bytes 1572872 | tf_op jit(solution)/shard_map/ppermute | solution.py:417
  28.5 24.1 %collective-permute-start.4 = (bf16[512,512]{1,0:T(8,128)(2,1)}, bf16[512,512]{1,0:T(8,128)(2,1)}, u32[]{:S(2)}, u32[]{:S(2)}) collective-permute-start(bf16[512,512]{1,0:T(8,128)(2,1)} %copy-done.8), channel_id=1, source_target_pairs={{0,8},{4,12},{8,16},{12,20},{16,24},{20,28},{24,0},{28,4},{1,9},{5... | collective-permute-start | bytes 1572872 | tf_op jit(solution)/shard_map/ppermute | solution.py:417
  30.7 1.1 copy-start.9
  52.6 7.4 %copy-start.6 = (bf16[592,512]{1,0:T(8,128)(2,1)}, bf16[592,512]{1,0:T(8,128)(2,1)S(1)}, u32[]{:S(2)}) copy-start(bf16[592,512]{1,0:T(8,128)(2,1)S(1)} %collective-permute-done.5.refs_1_.c2) | copy-start | bytes 1818628
  52.6 4.9 %collective-permute-start.8 = (bf16[256,2048]{1,0:T(8,128)(2,1)S(1)}, bf16[256,2048]{1,0:T(8,128)(2,1)S(1)}, u32[]{:S(2)}, u32[]{:S(2)}) collective-permute-start(bf16[256,2048]{1,0:T(8,128)(2,1)S(1)} %collective-permute-done.6.near), channel_id=1, source_target_pairs={{0,1},{1,0},{2,3},{3,2},{4,5},{5,4},{6,7},{7,6},{8,9},{9,8},{10,11... | collective-permute-start | bytes 3145736 | tf_op jit(solution)/shard_map/ppermute | solution.py:417
  52.7 15.3 %copy-start.23 = (f32[8]{0:T(128)S(1)}, f32[8]{0:T(128)}, u32[]{:S(2)}) copy-start(f32[8]{0:T(128)} %param.13) | copy-start | bytes 100
  52.7 16.0 %copy-start.24 = (f32[8]{0:T(128)S(1)}, f32[8]{0:T(128)}, u32[]{:S(2)}) copy-start(f32[8]{0:T(128)} %param.14) | copy-start | bytes 100
  52.8 4.8 %collective-permute-start.11 = (bf16[80,512]{1,0:T(8,128)(2,1)S(1)}, bf16[80,512]{1,0:T(8,128)(2,1)S(1)}, u32[]{:S(2)}, u32[]{:S(2)}) collective-permute-start(bf16[80,512]{1,0:T(8,128)(2,1)S(1)} %copy-done.25), channel_id=1, source_target_pairs={{8,0},{12,4},{16,8},{20,12},{24,16},{28,20},{0,24},{4,28},{9,1},{1... | collective-permute-start | bytes 245768 | tf_op jit(solution)/shard_map/ppermute | solution.py:417
  57.6 2.4 %copy-start.1 = (bf16[256,2048]{1,0:T(8,128)(2,1)}, bf16[256,2048]{1,0:T(8,128)(2,1)S(1)}, u32[]{:S(2)}) copy-start(bf16[256,2048]{1,0:T(8,128)(2,1)S(1)} %collective-permute-done.8.far) | copy-start | bytes 3145732
  60.0 5.8 %collective-permute-start.12 = (f32[80,512]{1,0:T(8,128)S(1)}, f32[80,512]{1,0:T(8,128)S(1)}, u32[]{:S(2)}, u32[]{:S(2)}) collective-permute-start(f32[80,512]{1,0:T(8,128)S(1)} %shard_map.86), channel_id=1, source_target_pairs={{0,4},{4,0},{8,12},{12,8},{16,20},{20,16},{24,28},{28,24},{1,5},{5... | collective-permute-start | bytes 491528 | tf_op jit(solution)/shard_map/ppermute | solution.py:417
  60.6 20.7 %collective-permute-start.9 = (bf16[512,512]{1,0:T(8,128)(2,1)}, bf16[512,512]{1,0:T(8,128)(2,1)}, u32[]{:S(2)}, u32[]{:S(2)}) collective-permute-start(bf16[512,512]{1,0:T(8,128)(2,1)} %shard_map.83), channel_id=1, source_target_pairs={{8,0},{12,4},{16,8},{20,12},{24,16},{28,20},{0,24},{4,28},{9,1},{1... | collective-permute-start | bytes 1572872 | tf_op jit(solution)/shard_map/ppermute | solution.py:417
  63.0 25.2 %collective-permute-start.10 = (bf16[512,512]{1,0:T(8,128)(2,1)}, bf16[512,512]{1,0:T(8,128)(2,1)}, u32[]{:S(2)}, u32[]{:S(2)}) collective-permute-start(bf16[512,512]{1,0:T(8,128)(2,1)} %collective-permute-done.4.refs_3_), channel_id=1, source_target_pairs={{0,8},{4,12},{8,16},{12,20},{16,24},{20,28},{24,0},{28,4},{1,9},{5... | collective-permute-start | bytes 1572872 | tf_op jit(solution)/shard_map/ppermute | solution.py:417
  65.9 0.7 copy-start.11
  66.6 10.2 %copy-start.13 = (bf16[64,512]{1,0:T(8,128)(2,1)}, bf16[64,512]{1,0:T(8,128)(2,1)S(1)}, u32[]{:S(2)}) copy-start(bf16[64,512]{1,0:T(8,128)(2,1)S(1)} %slice.27.some) | copy-start | bytes 196612
  66.6 4.3 %collective-permute-start.14 = (bf16[64,512]{1,0:T(8,128)(2,1)S(1)}, bf16[64,512]{1,0:T(8,128)(2,1)S(1)}, u32[]{:S(2)}, u32[]{:S(2)}) collective-permute-start(bf16[64,512]{1,0:T(8,128)(2,1)S(1)} %slice.27.some), channel_id=1, source_target_pairs={{0,2},{1,3},{2,0},{3,1},{4,6},{5,7},{6,4},{7,5},{8,10},{9,11},{10,... | collective-permute-start | bytes 196616 | tf_op jit(solution)/shard_map/ppermute | solution.py:417
  69.4 8.4 %collective-permute-start.13 = (bf16[64,512]{1,0:T(8,128)(2,1)S(1)}, bf16[64,512]{1,0:T(8,128)(2,1)S(1)}, u32[]{:S(2)}, u32[]{:S(2)}) collective-permute-start(bf16[64,512]{1,0:T(8,128)(2,1)S(1)} %slice.27.some), channel_id=1, source_target_pairs={{0,1},{1,0},{2,3},{3,2},{4,5},{5,4},{6,7},{7,6},{8,9},{9,8},{10,11... | collective-permute-start | bytes 196616 | tf_op jit(solution)/shard_map/ppermute | solution.py:417
  70.8 5.9 %copy-start.15 = (bf16[64,512]{1,0:T(8,128)(2,1)}, bf16[64,512]{1,0:T(8,128)(2,1)S(1)}, u32[]{:S(2)}) copy-start(bf16[64,512]{1,0:T(8,128)(2,1)S(1)} %collective-permute-done.14.some_chip) | copy-start | bytes 196612
  70.8 7.0 %collective-permute-start.15 = (bf16[64,512]{1,0:T(8,128)(2,1)S(1)}, bf16[64,512]{1,0:T(8,128)(2,1)S(1)}, u32[]{:S(2)}, u32[]{:S(2)}) collective-permute-start(bf16[64,512]{1,0:T(8,128)(2,1)S(1)} %collective-permute-done.14.some_chip), channel_id=1, source_target_pairs={{0,1},{1,0},{2,3},{3,2},{4,5},{5,4},{6,7},{7,6},{8,9},{9,8},{10,11... | collective-permute-start | bytes 196616 | tf_op jit(solution)/shard_map/ppermute | solution.py:417
  70.8 1.2 %copy-start.2 = (bf16[256,2048]{1,0:T(8,128)(2,1)S(1)}, bf16[256,2048]{1,0:T(8,128)(2,1)}, u32[]{:S(2)}) copy-start(bf16[256,2048]{1,0:T(8,128)(2,1)} %copy-done.1) | copy-start | bytes 3145732
  72.1 1.1 copy-start.5
  73.2 1.0 copy-start.10
  74.2 2.6 %copy-start.7 = (bf16[592,512]{1,0:T(8,128)(2,1)S(1)}, bf16[592,512]{1,0:T(8,128)(2,1)}, u32[]{:S(2)}) copy-start(bf16[592,512]{1,0:T(8,128)(2,1)} %copy-done.6) | copy-start | bytes 1818628
  76.8 1.1 copy-start.12
  76.8 1.1 copy-start.18
  76.8 1.1 copy-start.20
  76.8 1.1 copy-start.21
  76.8 11.4 %copy-start.3 = (bf16[256,2048]{1,0:T(8,128)(2,1)S(1)}, bf16[256,2048]{1,0:T(8,128)(2,1)}, u32[]{:S(2)}) copy-start(bf16[256,2048]{1,0:T(8,128)(2,1)} %copy-done.1) | copy-start | bytes 3145732
  77.9 0.8 copy-start.14
  78.7 0.8 copy-start.16
  88.2 6.6 %copy-start.22 = (f32[8]{0:T(128)S(1)}, f32[8]{0:T(128)}, u32[]{:S(2)}) copy-start(f32[8]{0:T(128)} %param.15) | copy-start | bytes 100
  90.2 10.1 %collective-permute-start.16 = (bf16[144,512]{1,0:T(8,128)(2,1)S(1)}, bf16[144,512]{1,0:T(8,128)(2,1)S(1)}, u32[]{:S(2)}, u32[]{:S(2)}) collective-permute-start(bf16[144,512]{1,0:T(8,128)(2,1)S(1)} %get-tuple-element.46), channel_id=1, source_target_pairs={{0,8},{4,12},{8,16},{12,20},{16,24},{20,28},{1,9},{5,13},{9,17},{1... | collective-permute-start | bytes 442376 | tf_op jit(solution)/shard_map/ppermute | solution.py:417
  93.4 8.5 %collective-permute-start.17 = (bf16[144,512]{1,0:T(8,128)(2,1)S(1)}, bf16[144,512]{1,0:T(8,128)(2,1)S(1)}, u32[]{:S(2)}, u32[]{:S(2)}) collective-permute-start(bf16[144,512]{1,0:T(8,128)(2,1)S(1)} %get-tuple-element.46), channel_id=1, source_target_pairs={{0,16},{4,20},{8,24},{12,28},{1,17},{5,21},{9,25},{13,29},{2,18},{... | collective-permute-start | bytes 442376 | tf_op jit(solution)/shard_map/ppermute | solution.py:417
  94.7 9.3 %copy-start.19 = (s32[4]{0:T(128)S(1)}, s32[4]{0:T(128)}, u32[]{:S(2)}) copy-start(s32[4]{0:T(128)} %pad_add_fusion.place) | copy-start | bytes 52
  102.7 6.4 %collective-permute-start.18 = (bf16[256,512]{1,0:T(8,128)(2,1)S(1)}, bf16[256,512]{1,0:T(8,128)(2,1)S(1)}, u32[]{:S(2)}, u32[]{:S(2)}) collective-permute-start(bf16[256,512]{1,0:T(8,128)(2,1)S(1)} %shard_map.91), channel_id=1, source_target_pairs={{0,4},{4,0},{8,12},{12,8},{16,20},{20,16},{24,28},{28,24},{1,5},{5... | collective-permute-start | bytes 786440 | tf_op jit(solution)/shard_map/ppermute | solution.py:417

commit v5 on v4

--- a/solution.py
+++ b/solution.py
@@ -152,20 +152,16 @@
     return own, jnp.where(is_near, near_ref[:, inside], far_ref[:, inside])
 
 
-def split_kernel(place, x_weight, bc, dt, ids, hidden, own, sent, small, ahead, below, ids_in, done):
+def split_kernel(place, x_weight, bc, dt, ids, own, small, below, ids_in, done):
     f32, bf16 = jnp.float32, jnp.bfloat16
-    plane, lane, core = place[0], place[1], place[2]
+    lane = place[1]
     size, half = x_weight.shape[0], x_weight.shape[1] // 2
     maps, heads, rows = bc.shape[0], dt.shape[0], ids.shape[1]
-    at = LANES * ((plane + 1) % PLANES) + core
-
     def columns(ref, index, width):
         return ref.at[:, pl.ds(pl.multiple_of(index * width, width), width)]
 
     moves = [
-        (columns(hidden, at, size), ahead),
         (columns(x_weight, lane, half), own.at[pl.ds(0, size), :]),
-        (columns(x_weight, 1 - lane, half), sent),
         (bc, own.at[pl.ds(size, maps), :]),
         (bc, small.at[pl.ds(0, maps), :]),
         (dt, below),
@@ -418,35 +414,34 @@
 
     together = lax.optimization_barrier
 
-    own, sent, small, ahead = call(
+    ahead_at = (LANES * ((plane + 1) % PLANES) + core) * k_rows
+    ahead = send(lax.dynamic_slice_in_dim(hidden, ahead_at, k_rows, 1), along)
+    sent = lax.dynamic_slice_in_dim(x_weight, (1 - lane) * half, half, 1)
+    other = send(sent, swap)
+    own, small = call(
         split_kernel,
         [
             shaped(bf16, k_rows + used + heads, half),
-            shaped(bf16, k_rows, half),
             shaped(bf16, used + heads, k_rows),
-            shaped(bf16, rows, k_rows),
         ],
         place,
         x_weight,
         bc_weight.T,
         dt_weight.T,
         seg_ids[None],
-        hidden,
-        left=5,
+        left=4,
         grant=60,
         scratch=[
             pltpu.VMEM((heads, k_rows), bf16),
             pltpu.VMEM((1, rows), jnp.int32),
-            pltpu.SemaphoreType.DMA((7,)),
+            pltpu.SemaphoreType.DMA((5,)),
         ],
     )
-    ahead = send(ahead, along)
-    other = send(sent, swap)
     own_one = send(own, along)
     small_next = send(small, back)
     near = pick(core == 0, hidden[:, : depth // 2], hidden[:, depth // 2 :])
     ahead_other = send(ahead, swap)
-    other, own_one, near, ahead, ahead_other = together((other, own_one, near, ahead, ahead_other))
+    other, own_one, ahead, ahead_other = together((other, own_one, ahead, ahead_other))
 
     other_one = send(other, along)
     own_two = send(own_one, along)

time: 112 us -> 109 us (0.973)
  starting transfers between devices: 23.4 us -> 21.4 us
  waiting for transfers between devices: 58.9 us -> 56.9 us
    dynamic_slice x0 -> x2, local copies, waits for them, and re-layouts: none -> 2.98 us  [the longest x1 1.87 us: plane_shards(): sent = lax.dynamic_slice_in_dim(x_weight, (1 - lane) * half, half, 1)]
    unnamed x53 -> x47, local copies, waits for them, and re-layouts: 6.84 us -> 4.75 us
    ppermute x19, starting transfers between devices: 23.4 us -> 21.4 us  [send(): return lax.ppermute(x, axis, pairs)]
    ppermute x19, waiting for transfers between devices: 58.9 us -> 56.9 us  [send(): return lax.ppermute(x, axis, pairs)]
  transfers between devices with their start and end apart: 19 -> 19, of which waited for: 12 -> 11; matrix products, arithmetic and copies ran while one was open for 1% -> 4% of each run, Pallas kernels for 8% -> 12%
where the time goes in v5:
time: 109 us; the launch traced here: 107 us
  waiting for transfers between devices  56.9 us (52%)
  starting transfers between devices  21.4 us (20%)
  Pallas kernels  17.7 us (16%)
  local copies, waits for them, and re-layouts  9.1 us (8%)
  other arithmetic  1.65 us (2%)
    ppermute x19, waiting for transfers between devices, send(): return lax.ppermute(x, axis, pairs)  56.9 us
    ppermute x19, starting transfers between devices, send(): return lax.ppermute(x, axis, pairs)  21.4 us
    pallas_call x10, Pallas kernels, call(): pl.pallas_call(body, out_shape=shapes, in_specs=[pl.BlockSpec(memory_spac...  17.7 us
    unnamed x47, local copies, waits for them, and re-layouts  4.75 us
  transfers between devices with their start and end apart: 19, of which 11 were waited for; matrix products, arithmetic and copies ran while one was open for 4% of the time, Pallas kernels for 12%

profile of v5, /device:TPU:16, one launch (start us, length us, event | category | flops | bytes accessed | tf_op | source)
XLA Modules:
  0.0 107.1 jit_solution(9310559463873284359)
XLA Ops:
  0.0 1.1 %constant_dynamic-slice_fusion = bf16[256,512]{1,0:T(8,128)(2,1)S(1)} fusion(bf16[256,4096]{1,0:T(8,128)(2,1)} %hidden.7, s32[]{:T(128)S(6)} %select_n.51), kind=kLoop, calls=%fused_computation.7 | loop fusion | bytes 524292 | tf_op jit(solution)/shard_map/dynamic_slice | solution.py:418
  1.1 1.6 %collective-permute-start.2 = (bf16[256,512]{1,0:T(8,128)(2,1)S(1)}, bf16[256,512]{1,0:T(8,128)(2,1)S(1)}, u32[]{:S(2)}, u32[]{:S(2)}) collective-permute-start(bf16[256,512]{1,0:T(8,128)(2,1)S(1)} %constant_dynamic-slice_fusion), channel_id=1, source_target_pairs={{0,8},{4,12},{8,16},{12,20},{16,24},{20,28},{24,0},{28,4},{1,9},{5... | collective-permute-start | bytes 786440 | tf_op jit(solution)/shard_map/ppermute | solution.py:413
  2.8 1.9 %constant_dynamic-slice_fusion.1 = bf16[512,512]{1,0:T(8,128)(2,1)} fusion(bf16[512,1024]{1,0:T(8,128)(2,1)} %x_weight.1, s32[]{:T(128)S(6)} %select_n.49), kind=kLoop, calls=%fused_computation.8 | loop fusion | bytes 1048580 | tf_op jit(solution)/shard_map/dynamic_slice | solution.py:419
  4.6 1.5 %collective-permute-start = (bf16[512,512]{1,0:T(8,128)(2,1)}, bf16[512,512]{1,0:T(8,128)(2,1)}, u32[]{:S(2)}, u32[]{:S(2)}) collective-permute-start(bf16[512,512]{1,0:T(8,128)(2,1)} %constant_dynamic-slice_fusion.1), channel_id=1, source_target_pairs={{0,4},{4,0},{8,12},{12,8},{16,20},{20,16},{24,28},{28,24},{1,5},{5... | collective-permute-start | bytes 1572872 | tf_op jit(solution)/shard_map/ppermute | solution.py:413
  6.1 0.6 pad_add_fusion.place
  6.7 2.6 %shard_map.82 = (bf16[592,512]{1,0:T(8,128)(2,1)}, bf16[80,512]{1,0:T(8,128)(2,1)}) custom-call(s32[4]{0:T(128)} %pad_add_fusion.place, bf16[512,1024]{1,0:T(8,128)(2,1)} %x_weight.1, bf16[64,512]{1,0:T(8,128)(2,1)} %bitcast.11, bf16[8,512]{1,0:T(8,128)(2,1)} %bitcast.12, s32[1,256]{1,0:T(1,128)} %bitcast.13), custom_call_target="tpu_custom_call" | custom-call | bytes 1811472 | tf_op jit(solution)/shard_map/pallas_call | solution.py:124
  9.3 0.3 collective-permute-start.1
  9.6 0.0 collective-permute-done.2
  9.6 1.1 %collective-permute-start.3 = (bf16[256,512]{1,0:T(8,128)(2,1)S(1)}, bf16[256,512]{1,0:T(8,128)(2,1)S(1)}, u32[]{:S(2)}, u32[]{:S(2)}) collective-permute-start(bf16[256,512]{1,0:T(8,128)(2,1)S(1)} %collective-permute-done.2), channel_id=1, source_target_pairs={{0,4},{4,0},{8,12},{12,8},{16,20},{20,16},{24,28},{28,24},{1,5},{5... | collective-permute-start | bytes 786440 | tf_op jit(solution)/shard_map/ppermute | solution.py:413
  10.7 0.1 slice_select_fusion
  10.9 1.0 collective-permute-start.6
  11.8 8.0 %collective-permute-done.other.refs_1_ = bf16[512,512]{1,0:T(8,128)(2,1)} collective-permute-done((bf16[512,512]{1,0:T(8,128)(2,1)}, bf16[512,512]{1,0:T(8,128)(2,1)}, u32[]{:S(2)}, u32[]{:S(2)}) %collective-permute-start) | collective-permute-done | bytes 524320 | tf_op jit(solution)/shard_map/ppermute | solution.py:413
  19.8 5.5 %collective-permute-done.3 = bf16[256,512]{1,0:T(8,128)(2,1)S(1)} collective-permute-done((bf16[256,512]{1,0:T(8,128)(2,1)S(1)}, bf16[256,512]{1,0:T(8,128)(2,1)S(1)}, u32[]{:S(2)}, u32[]{:S(2)}) %collective-permute-start.3) | collective-permute-done | bytes 262176 | tf_op jit(solution)/shard_map/ppermute | solution.py:413
  25.3 0.0 collective-permute-done.1.refs_2_.c1
  25.3 0.0 collective-permute-start.5
  25.4 0.1 collective-permute-start.7
  25.4 2.9 %collective-permute-start.4 = (bf16[512,512]{1,0:T(8,128)(2,1)}, bf16[512,512]{1,0:T(8,128)(2,1)}, u32[]{:S(2)}, u32[]{:S(2)}) collective-permute-start(bf16[512,512]{1,0:T(8,128)(2,1)} %collective-permute-done.other.refs_1_), channel_id=1, source_target_pairs={{0,8},{4,12},{8,16},{12,20},{16,24},{20,28},{24,0},{28,4},{1,9},{5... | collective-permute-start | bytes 1572872 | tf_op jit(solution)/shard_map/ppermute | solution.py:413
  28.3 0.0 collective-permute-done.7.far
  28.3 0.0 copy-done.4
  28.3 2.6 %shard_map.83 = bf16[512,512]{1,0:T(8,128)(2,1)} custom-call(s32[4]{0:T(128)S(1)} %copy-done.14, bf16[512,512]{1,0:T(8,128)(2,1)S(1)} %constant_dynamic-update-slice_fusion.mine, bf16[512,512]{1,0:T(8,128)(2,1)S(1)} %collective-permute-done.7.far, bf16[592,512]{1,0:T(8,128)(2,1)S(1)} %copy-done.4, bf16[512,512]{1,0:T(8,128)(2,1)} %collective-permute-done.other.refs_1_), custom_call_target="tpu_custom_call" | custom-call | flops 536870912 | bytes 2703376 | tf_op jit(solution)/shard_map/pallas_call | solution.py:124
  30.9 15.4 %collective-permute-done.6.near = bf16[256,2048]{1,0:T(8,128)(2,1)S(1)} collective-permute-done((bf16[256,2048]{1,0:T(8,128)(2,1)S(1)}, bf16[256,2048]{1,0:T(8,128)(2,1)S(1)}, u32[]{:S(2)}, u32[]{:S(2)}) %collective-permute-start.6) | collective-permute-done | bytes 1048608 | tf_op jit(solution)/shard_map/ppermute | solution.py:413
  46.3 3.7 %collective-permute-done.4.refs_3_ = bf16[512,512]{1,0:T(8,128)(2,1)} collective-permute-done((bf16[512,512]{1,0:T(8,128)(2,1)}, bf16[512,512]{1,0:T(8,128)(2,1)}, u32[]{:S(2)}, u32[]{:S(2)}) %collective-permute-start.4) | collective-permute-done | bytes 524320 | tf_op jit(solution)/shard_map/ppermute | solution.py:413
  50.0 0.0 collective-permute-done.5.refs_1_.c2
  50.0 0.0 collective-permute-start.8
  50.0 0.0 copy-done.22
  50.0 0.0 copy-start.20
  50.1 0.0 copy-start.21
  50.1 1.0 collective-permute-start.11
  51.1 3.8 %collective-permute-done.11.s3 = bf16[80,512]{1,0:T(8,128)(2,1)S(1)} collective-permute-done((bf16[80,512]{1,0:T(8,128)(2,1)S(1)}, bf16[80,512]{1,0:T(8,128)(2,1)S(1)}, u32[]{:S(2)}, u32[]{:S(2)}) %collective-permute-start.11) | collective-permute-done | bytes 81952 | tf_op jit(solution)/shard_map/ppermute | solution.py:413
  54.9 0.0 collective-permute-done.8.far
  54.9 2.4 %shard_map.86 = f32[80,512]{1,0:T(8,128)S(1)} custom-call(s32[4]{0:T(128)S(1)} %copy-done.14, bf16[256,4096]{1,0:T(8,128)(2,1)S(1)} %copy-done, bf16[256,2048]{1,0:T(8,128)(2,1)S(1)} %collective-permute-done.6.near, bf16[256,2048]{1,0:T(8,128)(2,1)S(1)} %collective-permute-done.8.far, bf16[592,512]{1,0:T(8,128)(2,1)S(1)} %copy-done.4, ...), custom_call_target="tpu_custom_call" | custom-call | flops 301989888 | bytes 6258704 | tf_op jit(solution)/shard_map/pallas_call | solution.py:124
  57.3 1.3 %collective-permute-start.12 = (f32[80,512]{1,0:T(8,128)S(1)}, f32[80,512]{1,0:T(8,128)S(1)}, u32[]{:S(2)}, u32[]{:S(2)}) collective-permute-start(f32[80,512]{1,0:T(8,128)S(1)} %shard_map.86), channel_id=1, source_target_pairs={{0,4},{4,0},{8,12},{12,8},{16,20},{20,16},{24,28},{28,24},{1,5},{5... | collective-permute-start | bytes 491528 | tf_op jit(solution)/shard_map/ppermute | solution.py:413
  58.6 1.3 %collective-permute-start.9 = (bf16[512,512]{1,0:T(8,128)(2,1)}, bf16[512,512]{1,0:T(8,128)(2,1)}, u32[]{:S(2)}, u32[]{:S(2)}) collective-permute-start(bf16[512,512]{1,0:T(8,128)(2,1)} %shard_map.83), channel_id=1, source_target_pairs={{8,0},{12,4},{16,8},{20,12},{24,16},{28,20},{0,24},{4,28},{9,1},{1... | collective-permute-start | bytes 1572872 | tf_op jit(solution)/shard_map/ppermute | solution.py:413
  59.9 1.6 %collective-permute-start.10 = (bf16[512,512]{1,0:T(8,128)(2,1)}, bf16[512,512]{1,0:T(8,128)(2,1)}, u32[]{:S(2)}, u32[]{:S(2)}) collective-permute-start(bf16[512,512]{1,0:T(8,128)(2,1)} %collective-permute-done.4.refs_3_), channel_id=1, source_target_pairs={{0,8},{4,12},{8,16},{12,20},{16,24},{20,28},{24,0},{28,4},{1,9},{5... | collective-permute-start | bytes 1572872 | tf_op jit(solution)/shard_map/ppermute | solution.py:413
  61.6 1.6 %collective-permute-done.12 = f32[80,512]{1,0:T(8,128)S(1)} collective-permute-done((f32[80,512]{1,0:T(8,128)S(1)}, f32[80,512]{1,0:T(8,128)S(1)}, u32[]{:S(2)}, u32[]{:S(2)}) %collective-permute-start.12) | collective-permute-done | bytes 163872 | tf_op jit(solution)/shard_map/ppermute | solution.py:413
  63.2 0.7 copy-done.8
  63.9 1.5 %collective-permute-start.14 = (bf16[64,512]{1,0:T(8,128)(2,1)S(1)}, bf16[64,512]{1,0:T(8,128)(2,1)S(1)}, u32[]{:S(2)}, u32[]{:S(2)}) collective-permute-start(bf16[64,512]{1,0:T(8,128)(2,1)S(1)} %slice.27.some), channel_id=1, source_target_pairs={{0,2},{1,3},{2,0},{3,1},{4,6},{5,7},{6,4},{7,5},{8,10},{9,11},{10,... | collective-permute-start | bytes 196616 | tf_op jit(solution)/shard_map/ppermute | solution.py:413
  65.4 0.7 copy.9.bias
  66.1 0.7 copy.10.rate_of
  66.7 0.0 collective-permute-start.13
  66.7 1.4 %collective-permute-done.14.some_chip = bf16[64,512]{1,0:T(8,128)(2,1)S(1)} collective-permute-done((bf16[64,512]{1,0:T(8,128)(2,1)S(1)}, bf16[64,512]{1,0:T(8,128)(2,1)S(1)}, u32[]{:S(2)}, u32[]{:S(2)}) %collective-permute-start.14) | collective-permute-done | bytes 65568 | tf_op jit(solution)/shard_map/ppermute | solution.py:413
  68.2 0.0 collective-permute-start.15
  68.2 1.2 %copy-done.2 = bf16[256,2048]{1,0:T(8,128)(2,1)S(1)} copy-done((bf16[256,2048]{1,0:T(8,128)(2,1)S(1)}, bf16[256,2048]{1,0:T(8,128)(2,1)}, u32[]{:S(2)}) %copy-start.2) | copy-done | bytes 1048600
  69.4 1.1 copy-done.5
  70.5 2.7 %shard_map.84.refs_0_ = f32[2,256,512]{2,1,0:T(8,128)S(1)} custom-call(s32[4]{0:T(128)S(1)} %copy-done.14, bf16[256,4096]{1,0:T(8,128)(2,1)S(1)} %copy-done, bf16[256,2048]{1,0:T(8,128)(2,1)S(1)} %collective-permute-done.6.near, bf16[256,2048]{1,0:T(8,128)(2,1)S(1)} %copy-done.2, bf16[592,512]{1,0:T(8,128)(2,1)S(1)} %copy-done.5, ...), custom_call_target="tpu_custom_call" | custom-call | flops 1073741824 | bytes 7503888 | tf_op jit(solution)/shard_map/pallas_call | solution.py:124
  73.3 1.0 shard_map.85.acc
  74.3 0.0 collective-permute-done.13.some_core
  74.3 0.0 collective-permute-done.15.some_both
  74.4 0.8 copy-done.11
  75.2 0.8 copy-done.13
  76.0 1.8 %shard_map.87 = (bf16[2,4,256,256]{3,2,1,0:T(8,128)(2,1)S(1)}, bf16[2,4,128,256]{3,2,1,0:T(8,128)(2,1)S(1)}, bf16[2,256,128]{2,1,0:T(8,128)(2,1)S(1)}, f32[2,256,8]{2,1,0:T(8,128)S(1)}, f32[8,512]{1,0:T(8,128)S(1)}) custom-call(s32[4]{0:T(128)S(1)} %copy-done.15, bf16[64,512]{1,0:T(8,128)(2,1)S(1)} %copy-done.11, ...), custom_call_target="tpu_custom_call" | custom-call | flops 26214400 | bytes 2162768 | tf_op jit(solution)/shard_map/pallas_call | solution.py:124
  77.8 0.0 collective-permute-done.9.back
  77.8 7.3 %collective-permute-done.10.refs_0_ = bf16[512,512]{1,0:T(8,128)(2,1)} collective-permute-done((bf16[512,512]{1,0:T(8,128)(2,1)}, bf16[512,512]{1,0:T(8,128)(2,1)}, u32[]{:S(2)}, u32[]{:S(2)}) %collective-permute-start.10) | collective-permute-done | bytes 524320 | tf_op jit(solution)/shard_map/ppermute | solution.py:413
  85.1 2.0 %shard_map.88 = (bf16[2,256,512]{2,1,0:T(8,128)(2,1)S(1)}, bf16[144,512]{1,0:T(8,128)(2,1)S(1)}, bf16[128,512]{1,0:T(8,128)(2,1)S(1)}) custom-call(s32[4]{0:T(128)S(1)} %copy-done.15, bf16[256,4096]{1,0:T(8,128)(2,1)S(1)} %copy-done, bf16[256,2048]{1,0:T(8,128)(2,1)S(1)} %collective-permute-done.6.near, bf16[256,2048]{1,0:T(8,128)(2,1)S(1)} %copy-done.3, ...), custom_call_target="tpu_custom_call" | custom-call | flops 536870912 | bytes 7634960 | tf_op jit(solution)/shard_map/pallas_call | solution.py:124
  87.1 3.3 %collective-permute-start.16 = (bf16[144,512]{1,0:T(8,128)(2,1)S(1)}, bf16[144,512]{1,0:T(8,128)(2,1)S(1)}, u32[]{:S(2)}, u32[]{:S(2)}) collective-permute-start(bf16[144,512]{1,0:T(8,128)(2,1)S(1)} %get-tuple-element.40), channel_id=1, source_target_pairs={{0,8},{4,12},{8,16},{12,20},{16,24},{20,28},{1,9},{5,13},{9,17},{1... | collective-permute-start | bytes 442376 | tf_op jit(solution)/shard_map/ppermute | solution.py:413
  90.4 1.3 %collective-permute-start.17 = (bf16[144,512]{1,0:T(8,128)(2,1)S(1)}, bf16[144,512]{1,0:T(8,128)(2,1)S(1)}, u32[]{:S(2)}, u32[]{:S(2)}) collective-permute-start(bf16[144,512]{1,0:T(8,128)(2,1)S(1)} %get-tuple-element.40), channel_id=1, source_target_pairs={{0,16},{4,20},{8,24},{12,28},{1,17},{5,21},{9,25},{13,29},{2,18},{... | collective-permute-start | bytes 442376 | tf_op jit(solution)/shard_map/ppermute | solution.py:413
  91.7 1.1 %shard_map.89.local = f32[2,256,512]{2,1,0:T(8,128)S(1)} custom-call(s32[4]{0:T(128)S(1)} %copy-done.15, bf16[2,256,512]{2,1,0:T(8,128)(2,1)S(1)} %get-tuple-element.35.x, bf16[2,4,256,256]{3,2,1,0:T(8,128)(2,1)S(1)} %get-tuple-element.36.mixing, f32[1,8]{1,0:T(1,128)S(1)} %bitcast.10, bf16[2,256,128]{2,1,0:T(8,128)(2,1)S(1)} %get-tuple-element.37.c_rows, ...), custom_call_target="tpu_custom_call" | custom-call | flops 134217728 | bytes 2900016 | tf_op jit(solution)/shard_map/pallas_call | solution.py:124
  92.8 4.4 %collective-permute-done.16.one = bf16[144,512]{1,0:T(8,128)(2,1)S(1)} collective-permute-done((bf16[144,512]{1,0:T(8,128)(2,1)S(1)}, bf16[144,512]{1,0:T(8,128)(2,1)S(1)}, u32[]{:S(2)}, u32[]{:S(2)}) %collective-permute-start.16) | collective-permute-done | bytes 147488 | tf_op jit(solution)/shard_map/ppermute | solution.py:413
  97.2 1.7 %collective-permute-done.17.two = bf16[144,512]{1,0:T(8,128)(2,1)S(1)} collective-permute-done((bf16[144,512]{1,0:T(8,128)(2,1)S(1)}, bf16[144,512]{1,0:T(8,128)(2,1)S(1)}, u32[]{:S(2)}, u32[]{:S(2)}) %collective-permute-start.17) | collective-permute-done | bytes 147488 | tf_op jit(solution)/shard_map/ppermute | solution.py:413
  98.9 0.8 shard_map.91
  99.7 1.6 %collective-permute-start.18 = (bf16[256,512]{1,0:T(8,128)(2,1)S(1)}, bf16[256,512]{1,0:T(8,128)(2,1)S(1)}, u32[]{:S(2)}, u32[]{:S(2)}) collective-permute-start(bf16[256,512]{1,0:T(8,128)(2,1)S(1)} %shard_map.91), channel_id=1, source_target_pairs={{0,4},{4,0},{8,12},{12,8},{16,20},{20,16},{24,28},{28,24},{1,5},{5... | collective-permute-start | bytes 786440 | tf_op jit(solution)/shard_map/ppermute | solution.py:413
  101.3 0.8 shard_map.90
  102.1 4.0 %collective-permute-done.18 = bf16[256,512]{1,0:T(8,128)(2,1)S(1)} collective-permute-done((bf16[256,512]{1,0:T(8,128)(2,1)S(1)}, bf16[256,512]{1,0:T(8,128)(2,1)S(1)}, u32[]{:S(2)}, u32[]{:S(2)}) %collective-permute-start.18) | collective-permute-done | bytes 262176 | tf_op jit(solution)/shard_map/ppermute | solution.py:413
  106.1 0.9 maximum_select_fusion
  (42 shorter events, 0.2 us)
Async XLA Ops:
  0.0 10.7 %copy-start = (bf16[256,4096]{1,0:T(8,128)(2,1)S(1)}, bf16[256,4096]{1,0:T(8,128)(2,1)}, u32[]{:S(2)}) copy-start(bf16[256,4096]{1,0:T(8,128)(2,1)} %hidden.7) | copy-start | bytes 6291460
  1.1 8.5 %collective-permute-start.2 = (bf16[256,512]{1,0:T(8,128)(2,1)S(1)}, bf16[256,512]{1,0:T(8,128)(2,1)S(1)}, u32[]{:S(2)}, u32[]{:S(2)}) collective-permute-start(bf16[256,512]{1,0:T(8,128)(2,1)S(1)} %constant_dynamic-slice_fusion), channel_id=1, source_target_pairs={{0,8},{4,12},{8,16},{12,20},{16,24},{20,28},{24,0},{28,4},{1,9},{5... | collective-permute-start | bytes 786440 | tf_op jit(solution)/shard_map/ppermute | solution.py:413
  4.6 15.2 %collective-permute-start = (bf16[512,512]{1,0:T(8,128)(2,1)}, bf16[512,512]{1,0:T(8,128)(2,1)}, u32[]{:S(2)}, u32[]{:S(2)}) collective-permute-start(bf16[512,512]{1,0:T(8,128)(2,1)} %constant_dynamic-slice_fusion.1), channel_id=1, source_target_pairs={{0,4},{4,0},{8,12},{12,8},{16,20},{20,16},{24,28},{28,24},{1,5},{5... | collective-permute-start | bytes 1572872 | tf_op jit(solution)/shard_map/ppermute | solution.py:413
  9.3 16.0 %collective-permute-start.1 = (bf16[592,512]{1,0:T(8,128)(2,1)}, bf16[592,512]{1,0:T(8,128)(2,1)}, u32[]{:S(2)}, u32[]{:S(2)}) collective-permute-start(bf16[592,512]{1,0:T(8,128)(2,1)} %get-tuple-element.23.own.refs_0_.c0), channel_id=1, source_target_pairs={{0,8},{4,12},{8,16},{12,20},{16,24},{20,28},{24,0},{28,4},{1,9},{5... | collective-permute-start | bytes 1818632 | tf_op jit(solution)/shard_map/ppermute | solution.py:413
  9.6 18.7 %copy-start.4 = (bf16[592,512]{1,0:T(8,128)(2,1)S(1)}, bf16[592,512]{1,0:T(8,128)(2,1)}, u32[]{:S(2)}) copy-start(bf16[592,512]{1,0:T(8,128)(2,1)} %get-tuple-element.23.own.refs_0_.c0) | copy-start | bytes 1818628
  9.6 18.7 %copy-start.14 = (s32[4]{0:T(128)S(1)}, s32[4]{0:T(128)}, u32[]{:S(2)}) copy-start(s32[4]{0:T(128)} %pad_add_fusion.place) | copy-start | bytes 52
  9.6 15.7 %collective-permute-start.3 = (bf16[256,512]{1,0:T(8,128)(2,1)S(1)}, bf16[256,512]{1,0:T(8,128)(2,1)S(1)}, u32[]{:S(2)}, u32[]{:S(2)}) collective-permute-start(bf16[256,512]{1,0:T(8,128)(2,1)S(1)} %collective-permute-done.2), channel_id=1, source_target_pairs={{0,4},{4,0},{8,12},{12,8},{16,20},{20,16},{24,28},{28,24},{1,5},{5... | collective-permute-start | bytes 786440 | tf_op jit(solution)/shard_map/ppermute | solution.py:413
  10.9 39.2 %copy-start.22 = (bf16[80,512]{1,0:T(8,128)(2,1)S(1)}, bf16[80,512]{1,0:T(8,128)(2,1)}, u32[]{:S(2)}) copy-start(bf16[80,512]{1,0:T(8,128)(2,1)} %get-tuple-element.32) | copy-start | bytes 245764
  10.9 35.4 %collective-permute-start.6 = (bf16[256,2048]{1,0:T(8,128)(2,1)S(1)}, bf16[256,2048]{1,0:T(8,128)(2,1)S(1)}, u32[]{:S(2)}, u32[]{:S(2)}) collective-permute-start(bf16[256,2048]{1,0:T(8,128)(2,1)S(1)} %slice_select_fusion), channel_id=1, source_target_pairs={{0,4},{4,0},{8,12},{12,8},{16,20},{20,16},{24,28},{28,24},{1,5},{5... | collective-permute-start | bytes 3145736 | tf_op jit(solution)/shard_map/ppermute | solution.py:413
  25.3 24.7 %collective-permute-start.5 = (bf16[592,512]{1,0:T(8,128)(2,1)}, bf16[592,512]{1,0:T(8,128)(2,1)S(1)}, u32[]{:S(2)}, u32[]{:S(2)}) collective-permute-start(bf16[592,512]{1,0:T(8,128)(2,1)} %collective-permute-done.1.refs_2_.c1), channel_id=1, source_target_pairs={{0,8},{4,12},{8,16},{12,20},{16,24},{20,28},{24,0},{28,4},{1,9},{5... | collective-permute-start | bytes 1818632 | tf_op jit(solution)/shard_map/ppermute | solution.py:413
  25.4 3.0 %collective-permute-start.7 = (bf16[512,512]{1,0:T(8,128)(2,1)S(1)}, bf16[512,512]{1,0:T(8,128)(2,1)S(1)}, u32[]{:S(2)}, u32[]{:S(2)}) collective-permute-start(bf16[512,512]{1,0:T(8,128)(2,1)S(1)} %constant_dynamic-update-slice_fusion.mine), channel_id=1, source_target_pairs={{0,1},{1,0},{2,3},{3,2},{4,5},{5,4},{6,7},{7,6},{8,9},{9,8},{10,11... | collective-permute-start | bytes 1572872 | tf_op jit(solution)/shard_map/ppermute | solution.py:413
  25.4 24.6 %collective-permute-start.4 = (bf16[512,512]{1,0:T(8,128)(2,1)}, bf16[512,512]{1,0:T(8,128)(2,1)}, u32[]{:S(2)}, u32[]{:S(2)}) collective-permute-start(bf16[512,512]{1,0:T(8,128)(2,1)} %collective-permute-done.other.refs_1_), channel_id=1, source_target_pairs={{0,8},{4,12},{8,16},{12,20},{16,24},{20,28},{24,0},{28,4},{1,9},{5... | collective-permute-start | bytes 1572872 | tf_op jit(solution)/shard_map/ppermute | solution.py:413
  50.0 7.3 %copy-start.6 = (bf16[592,512]{1,0:T(8,128)(2,1)}, bf16[592,512]{1,0:T(8,128)(2,1)S(1)}, u32[]{:S(2)}) copy-start(bf16[592,512]{1,0:T(8,128)(2,1)S(1)} %collective-permute-done.5.refs_1_.c2) | copy-start | bytes 1818628
  50.0 4.9 %collective-permute-start.8 = (bf16[256,2048]{1,0:T(8,128)(2,1)S(1)}, bf16[256,2048]{1,0:T(8,128)(2,1)S(1)}, u32[]{:S(2)}, u32[]{:S(2)}) collective-permute-start(bf16[256,2048]{1,0:T(8,128)(2,1)S(1)} %collective-permute-done.6.near), channel_id=1, source_target_pairs={{0,1},{1,0},{2,3},{3,2},{4,5},{5,4},{6,7},{7,6},{8,9},{9,8},{10,11... | collective-permute-start | bytes 3145736 | tf_op jit(solution)/shard_map/ppermute | solution.py:413
  50.0 15.4 %copy-start.20 = (f32[8]{0:T(128)S(1)}, f32[8]{0:T(128)}, u32[]{:S(2)}) copy-start(f32[8]{0:T(128)} %param.13) | copy-start | bytes 100
  50.1 16.0 %copy-start.21 = (f32[8]{0:T(128)S(1)}, f32[8]{0:T(128)}, u32[]{:S(2)}) copy-start(f32[8]{0:T(128)} %param.14) | copy-start | bytes 100
  50.1 4.8 %collective-permute-start.11 = (bf16[80,512]{1,0:T(8,128)(2,1)S(1)}, bf16[80,512]{1,0:T(8,128)(2,1)S(1)}, u32[]{:S(2)}, u32[]{:S(2)}) collective-permute-start(bf16[80,512]{1,0:T(8,128)(2,1)S(1)} %copy-done.22), channel_id=1, source_target_pairs={{8,0},{12,4},{16,8},{20,12},{24,16},{28,20},{0,24},{4,28},{9,1},{1... | collective-permute-start | bytes 245768 | tf_op jit(solution)/shard_map/ppermute | solution.py:413
  54.9 2.4 %copy-start.1 = (bf16[256,2048]{1,0:T(8,128)(2,1)}, bf16[256,2048]{1,0:T(8,128)(2,1)S(1)}, u32[]{:S(2)}) copy-start(bf16[256,2048]{1,0:T(8,128)(2,1)S(1)} %collective-permute-done.8.far) | copy-start | bytes 3145732
  57.3 5.8 %collective-permute-start.12 = (f32[80,512]{1,0:T(8,128)S(1)}, f32[80,512]{1,0:T(8,128)S(1)}, u32[]{:S(2)}, u32[]{:S(2)}) collective-permute-start(f32[80,512]{1,0:T(8,128)S(1)} %shard_map.86), channel_id=1, source_target_pairs={{0,4},{4,0},{8,12},{12,8},{16,20},{20,16},{24,28},{28,24},{1,5},{5... | collective-permute-start | bytes 491528 | tf_op jit(solution)/shard_map/ppermute | solution.py:413
  58.6 19.2 %collective-permute-start.9 = (bf16[512,512]{1,0:T(8,128)(2,1)}, bf16[512,512]{1,0:T(8,128)(2,1)}, u32[]{:S(2)}, u32[]{:S(2)}) collective-permute-start(bf16[512,512]{1,0:T(8,128)(2,1)} %shard_map.83), channel_id=1, source_target_pairs={{8,0},{12,4},{16,8},{20,12},{24,16},{28,20},{0,24},{4,28},{9,1},{1... | collective-permute-start | bytes 1572872 | tf_op jit(solution)/shard_map/ppermute | solution.py:413
  59.9 25.2 %collective-permute-start.10 = (bf16[512,512]{1,0:T(8,128)(2,1)}, bf16[512,512]{1,0:T(8,128)(2,1)}, u32[]{:S(2)}, u32[]{:S(2)}) collective-permute-start(bf16[512,512]{1,0:T(8,128)(2,1)} %collective-permute-done.4.refs_3_), channel_id=1, source_target_pairs={{0,8},{4,12},{8,16},{12,20},{16,24},{20,28},{24,0},{28,4},{1,9},{5... | collective-permute-start | bytes 1572872 | tf_op jit(solution)/shard_map/ppermute | solution.py:413
  63.2 0.7 copy-start.8
  63.9 9.3 %copy-start.10 = (bf16[64,512]{1,0:T(8,128)(2,1)}, bf16[64,512]{1,0:T(8,128)(2,1)S(1)}, u32[]{:S(2)}) copy-start(bf16[64,512]{1,0:T(8,128)(2,1)S(1)} %slice.27.some) | copy-start | bytes 196612
  63.9 4.3 %collective-permute-start.14 = (bf16[64,512]{1,0:T(8,128)(2,1)S(1)}, bf16[64,512]{1,0:T(8,128)(2,1)S(1)}, u32[]{:S(2)}, u32[]{:S(2)}) collective-permute-start(bf16[64,512]{1,0:T(8,128)(2,1)S(1)} %slice.27.some), channel_id=1, source_target_pairs={{0,2},{1,3},{2,0},{3,1},{4,6},{5,7},{6,4},{7,5},{8,10},{9,11},{10,... | collective-permute-start | bytes 196616 | tf_op jit(solution)/shard_map/ppermute | solution.py:413
  66.7 7.6 %collective-permute-start.13 = (bf16[64,512]{1,0:T(8,128)(2,1)S(1)}, bf16[64,512]{1,0:T(8,128)(2,1)S(1)}, u32[]{:S(2)}, u32[]{:S(2)}) collective-permute-start(bf16[64,512]{1,0:T(8,128)(2,1)S(1)} %slice.27.some), channel_id=1, source_target_pairs={{0,1},{1,0},{2,3},{3,2},{4,5},{5,4},{6,7},{7,6},{8,9},{9,8},{10,11... | collective-permute-start | bytes 196616 | tf_op jit(solution)/shard_map/ppermute | solution.py:413
  68.2 5.1 %copy-start.12 = (bf16[64,512]{1,0:T(8,128)(2,1)}, bf16[64,512]{1,0:T(8,128)(2,1)S(1)}, u32[]{:S(2)}) copy-start(bf16[64,512]{1,0:T(8,128)(2,1)S(1)} %collective-permute-done.14.some_chip) | copy-start | bytes 196612
  68.2 6.1 %collective-permute-start.15 = (bf16[64,512]{1,0:T(8,128)(2,1)S(1)}, bf16[64,512]{1,0:T(8,128)(2,1)S(1)}, u32[]{:S(2)}, u32[]{:S(2)}) collective-permute-start(bf16[64,512]{1,0:T(8,128)(2,1)S(1)} %collective-permute-done.14.some_chip), channel_id=1, source_target_pairs={{0,1},{1,0},{2,3},{3,2},{4,5},{5,4},{6,7},{7,6},{8,9},{9,8},{10,11... | collective-permute-start | bytes 196616 | tf_op jit(solution)/shard_map/ppermute | solution.py:413
  68.2 1.2 %copy-start.2 = (bf16[256,2048]{1,0:T(8,128)(2,1)S(1)}, bf16[256,2048]{1,0:T(8,128)(2,1)}, u32[]{:S(2)}) copy-start(bf16[256,2048]{1,0:T(8,128)(2,1)} %copy-done.1) | copy-start | bytes 3145732
  69.4 1.1 copy-start.5
  70.5 2.8 %copy-start.7 = (bf16[592,512]{1,0:T(8,128)(2,1)S(1)}, bf16[592,512]{1,0:T(8,128)(2,1)}, u32[]{:S(2)}) copy-start(bf16[592,512]{1,0:T(8,128)(2,1)} %copy-done.6) | copy-start | bytes 1818628
  73.3 1.1 copy-start.9
  73.3 1.1 copy-start.15
  73.3 1.1 copy-start.17
  73.3 1.1 copy-start.18
  73.3 11.8 %copy-start.3 = (bf16[256,2048]{1,0:T(8,128)(2,1)S(1)}, bf16[256,2048]{1,0:T(8,128)(2,1)}, u32[]{:S(2)}) copy-start(bf16[256,2048]{1,0:T(8,128)(2,1)} %copy-done.1) | copy-start | bytes 3145732
  74.4 0.8 copy-start.11
  75.2 0.8 copy-start.13
  85.1 6.6 %copy-start.19 = (f32[8]{0:T(128)S(1)}, f32[8]{0:T(128)}, u32[]{:S(2)}) copy-start(f32[8]{0:T(128)} %param.15) | copy-start | bytes 100
  87.1 10.1 %collective-permute-start.16 = (bf16[144,512]{1,0:T(8,128)(2,1)S(1)}, bf16[144,512]{1,0:T(8,128)(2,1)S(1)}, u32[]{:S(2)}, u32[]{:S(2)}) collective-permute-start(bf16[144,512]{1,0:T(8,128)(2,1)S(1)} %get-tuple-element.40), channel_id=1, source_target_pairs={{0,8},{4,12},{8,16},{12,20},{16,24},{20,28},{1,9},{5,13},{9,17},{1... | collective-permute-start | bytes 442376 | tf_op jit(solution)/shard_map/ppermute | solution.py:413
  90.4 8.5 %collective-permute-start.17 = (bf16[144,512]{1,0:T(8,128)(2,1)S(1)}, bf16[144,512]{1,0:T(8,128)(2,1)S(1)}, u32[]{:S(2)}, u32[]{:S(2)}) collective-permute-start(bf16[144,512]{1,0:T(8,128)(2,1)S(1)} %get-tuple-element.40), channel_id=1, source_target_pairs={{0,16},{4,20},{8,24},{12,28},{1,17},{5,21},{9,25},{13,29},{2,18},{... | collective-permute-start | bytes 442376 | tf_op jit(solution)/shard_map/ppermute | solution.py:413
  91.7 9.6 %copy-start.16 = (s32[4]{0:T(128)S(1)}, s32[4]{0:T(128)}, u32[]{:S(2)}) copy-start(s32[4]{0:T(128)} %pad_add_fusion.place) | copy-start | bytes 52
  99.7 6.4 %collective-permute-start.18 = (bf16[256,512]{1,0:T(8,128)(2,1)S(1)}, bf16[256,512]{1,0:T(8,128)(2,1)S(1)}, u32[]{:S(2)}, u32[]{:S(2)}) collective-permute-start(bf16[256,512]{1,0:T(8,128)(2,1)S(1)} %shard_map.91), channel_id=1, source_target_pairs={{0,4},{4,0},{8,12},{12,8},{16,20},{20,16},{24,28},{28,24},{1,5},{5... | collective-permute-start | bytes 786440 | tf_op jit(solution)/shard_map/ppermute | solution.py:413

commit v6 on v5

--- a/solution.py
+++ b/solution.py
@@ -211,7 +211,7 @@
 
 
 def decay_kernel(
-    map_cols, place, some, some_core, some_chip, some_both, total, bias, rate_of, mixing, loaded, c_out, fac, meta
+    map_cols, place, some, some_core, some_chip, some_both, total, bias, rate_of, mixing, loaded, c_out, fac, meta, passing
 ):
     f32, bf16 = jnp.float32, jnp.bfloat16
     plane, lane = place[0], place[1]
@@ -269,6 +269,12 @@
         meta[1:2, cut] = jnp.broadcast_to(enters[h : h + 1], (1, width))
         meta[2:3, cut] = jnp.broadcast_to(through[h : h + 1], (1, width))
         meta[3:4, cut] = jnp.broadcast_to(passes, (1, width))
+    whole = meta[2:3, :]
+    upper_part = whole.astype(bf16).astype(f32)
+    row = lax.broadcasted_iota(jnp.int32, passing.shape, 0)
+    passing[...] = jnp.where(
+        row == 0, upper_part, jnp.where(row == 1, whole - upper_part, 0.0)
+    ).astype(bf16)
     for r in range(2):
         b = lane if r == 0 else 1 - lane
         cut = slice(r * rows, (r + 1) * rows)
@@ -336,15 +342,8 @@
         cut = slice(h * width, (h + 1) * width)
         first = mul(loaded[0, h], x_out[0, :, cut])
         second = mul(loaded[1, h], x_out[1, :, cut])
-        ready[:NS, cut] = (second + meta[0:1, cut] * first).astype(bf16)
+        ready[:, cut] = (second + meta[0:1, cut] * first).astype(bf16)
         built_out[:, cut] = first.astype(bf16)
-    through = meta[2:3, :]
-    upper = through.astype(bf16)
-    lower = (through - upper.astype(f32)).astype(bf16)
-    row = lax.broadcasted_iota(jnp.int32, (ready.shape[0] - NS, ready.shape[1]), 0)
-    ready[NS:, :] = jnp.where(
-        row == 0, upper.astype(f32), jnp.where(row == 1, lower.astype(f32), 0.0)
-    ).astype(bf16)
 
 
 def local_kernel(place, x, mixing, skip, c_rows, built, fac, out):
@@ -363,12 +362,12 @@
             out[b, :, cut] = local
 
 
-def final_kernel(partner, mine, place, local, c_rows, fac, meta, one, two, out):
+def final_kernel(partner, mine, place, local, c_rows, fac, meta, passed, one, two, out):
     f32, bf16 = jnp.float32, jnp.bfloat16
     lane = place[1]
     b = 1 - lane if partner else lane
-    through = one[NS : NS + 1, :].astype(f32) + one[NS + 1 : NS + 2, :].astype(f32)
-    incoming = one[:NS, :].astype(f32) + (through * meta[3:4, :]) * two[:NS, :].astype(f32)
+    through = passed[0:1, :].astype(f32) + passed[1:2, :].astype(f32)
+    incoming = one[...].astype(f32) + (through * meta[3:4, :]) * two[...].astype(f32)
     entering = (incoming * jnp.where(b == 1, meta[1:2, :], 1.0)).astype(bf16)
     carried = mul(c_rows[b], entering)
     factor = fac[b]
@@ -440,6 +439,7 @@
     own_one = send(own, along)
     small_next = send(small, back)
     near = pick(core == 0, hidden[:, : depth // 2], hidden[:, depth // 2 :])
+    near, other = together((near, other))
     ahead_other = send(ahead, swap)
     other, own_one, ahead, ahead_other = together((other, own_one, ahead, ahead_other))
 
@@ -505,7 +505,7 @@
     some_core = send(some, cores, "rep")
     some_chip = send(some, chips, "rep")
     some_both = send(some_chip, cores, "rep")
-    mixing, loaded, c_rows, fac, meta = call(
+    mixing, loaded, c_rows, fac, meta, passing = call(
         functools.partial(decay_kernel, map_cols),
         [
             shaped(bf16, LANES, mine, rows, rows),
@@ -513,6 +513,7 @@
             shaped(bf16, LANES, rows, NS),
             shaped(f32, LANES, rows, 8),
             shaped(f32, 8, half),
+            shaped(bf16, 16, half),
         ],
         place,
         some,
@@ -528,7 +529,7 @@
         functools.partial(input_kernel, ((2, False),)),
         [
             shaped(bf16, LANES, rows, half),
-            shaped(bf16, NS + 16, half),
+            shaped(bf16, NS, half),
             shaped(bf16, NS, half),
         ],
         place,
@@ -542,6 +543,7 @@
         meta,
         flops=rows * depth * half,
     )
+    passed = send(passing, shift(1, (0, 1, 2)))
     from_one = send(ready, shift(1, (0, 1, 2)))
     from_two = send(ready, shift(2, (0, 1)))
     local = call(
@@ -566,6 +568,7 @@
             c_rows,
             fac,
             meta,
+            passed,
             from_one,
             from_two,
             flops=2 * rows * NS * half,

time: 109 us -> 108 us (level)
  starting transfers between devices: 21.4 us -> 24.9 us
  waiting for transfers between devices: 56.9 us -> 54.1 us
    ppermute x19 -> x20, starting transfers between devices: 21.4 us -> 24.9 us  [send(): return lax.ppermute(x, axis, pairs)]
    ppermute x19 -> x20, waiting for transfers between devices: 56.9 us -> 54.1 us  [send(): return lax.ppermute(x, axis, pairs)]
  transfers between devices with their start and end apart: 19 -> 20, of which waited for: 11 -> 10; matrix products, arithmetic and copies ran while one was open for 4% -> 3% of each run, Pallas kernels for 12% -> 12%
where the time goes in v6:
time: 108 us; the launch traced here: 107 us
  waiting for transfers between devices  54.1 us (50%)
  starting transfers between devices  24.9 us (23%)
  Pallas kernels  17.7 us (16%)
  local copies, waits for them, and re-layouts  8.32 us (8%)
  other arithmetic  1.74 us (2%)
    ppermute x20, waiting for transfers between devices, send(): return lax.ppermute(x, axis, pairs)  54.1 us
    ppermute x20, starting transfers between devices, send(): return lax.ppermute(x, axis, pairs)  24.9 us
    pallas_call x10, Pallas kernels, call(): pl.pallas_call(body, out_shape=shapes, in_specs=[pl.BlockSpec(memory_spac...  17.7 us
    unnamed x47, local copies, waits for them, and re-layouts  4.74 us
  transfers between devices with their start and end apart: 20, of which 10 were waited for; matrix products, arithmetic and copies ran while one was open for 3% of the time, Pallas kernels for 12%

profile of v6, /device:TPU:16, one launch (start us, length us, event | category | flops | bytes accessed | tf_op | source)
XLA Modules:
  0.0 107.1 jit_solution(16866040630012084203)
XLA Ops:
  0.0 1.1 %constant_dynamic-slice_fusion = bf16[256,512]{1,0:T(8,128)(2,1)S(1)} fusion(bf16[256,4096]{1,0:T(8,128)(2,1)} %hidden.7, s32[]{:T(128)S(6)} %select_n.53), kind=kLoop, calls=%fused_computation.7 | loop fusion | bytes 524292 | tf_op jit(solution)/shard_map/dynamic_slice | solution.py:417
  1.1 1.6 %collective-permute-start.2 = (bf16[256,512]{1,0:T(8,128)(2,1)S(1)}, bf16[256,512]{1,0:T(8,128)(2,1)S(1)}, u32[]{:S(2)}, u32[]{:S(2)}) collective-permute-start(bf16[256,512]{1,0:T(8,128)(2,1)S(1)} %constant_dynamic-slice_fusion), channel_id=1, source_target_pairs={{0,8},{4,12},{8,16},{12,20},{16,24},{20,28},{24,0},{28,4},{1,9},{5... | collective-permute-start | bytes 786440 | tf_op jit(solution)/shard_map/ppermute | solution.py:412
  2.8 1.1 %constant_dynamic-slice_fusion.1 = bf16[512,512]{1,0:T(8,128)(2,1)S(1)} fusion(bf16[512,1024]{1,0:T(8,128)(2,1)} %x_weight.1, s32[]{:T(128)S(6)} %select_n.51), kind=kLoop, calls=%fused_computation.8 | loop fusion | bytes 1048580 | tf_op jit(solution)/shard_map/dynamic_slice | solution.py:418
  3.8 1.6 %collective-permute-start = (bf16[512,512]{1,0:T(8,128)(2,1)S(1)}, bf16[512,512]{1,0:T(8,128)(2,1)}, u32[]{:S(2)}, u32[]{:S(2)}) collective-permute-start(bf16[512,512]{1,0:T(8,128)(2,1)S(1)} %constant_dynamic-slice_fusion.1), channel_id=1, source_target_pairs={{0,4},{4,0},{8,12},{12,8},{16,20},{20,16},{24,28},{28,24},{1,5},{5... | collective-permute-start | bytes 1572872 | tf_op jit(solution)/shard_map/ppermute | solution.py:412
  5.4 0.7 pad_add_fusion.place
  6.1 2.6 %shard_map.82 = (bf16[592,512]{1,0:T(8,128)(2,1)}, bf16[80,512]{1,0:T(8,128)(2,1)}) custom-call(s32[4]{0:T(128)} %pad_add_fusion.place, bf16[512,1024]{1,0:T(8,128)(2,1)} %x_weight.1, bf16[64,512]{1,0:T(8,128)(2,1)} %bitcast.11, bf16[8,512]{1,0:T(8,128)(2,1)} %bitcast.12, s32[1,256]{1,0:T(1,128)} %bitcast.13), custom_call_target="tpu_custom_call" | custom-call | bytes 1811472 | tf_op jit(solution)/shard_map/pallas_call | solution.py:124
  8.7 0.3 collective-permute-start.1
  9.0 0.2 collective-permute-done.2
  9.2 1.5 %collective-permute-start.3 = (bf16[256,512]{1,0:T(8,128)(2,1)S(1)}, bf16[256,512]{1,0:T(8,128)(2,1)S(1)}, u32[]{:S(2)}, u32[]{:S(2)}) collective-permute-start(bf16[256,512]{1,0:T(8,128)(2,1)S(1)} %collective-permute-done.2), channel_id=1, source_target_pairs={{0,4},{4,0},{8,12},{12,8},{16,20},{20,16},{24,28},{28,24},{1,5},{5... | collective-permute-start | bytes 786440 | tf_op jit(solution)/shard_map/ppermute | solution.py:412
  10.7 0.1 slice_select_fusion
  10.9 8.0 %collective-permute-done.other.refs_1_ = bf16[512,512]{1,0:T(8,128)(2,1)} collective-permute-done((bf16[512,512]{1,0:T(8,128)(2,1)S(1)}, bf16[512,512]{1,0:T(8,128)(2,1)}, u32[]{:S(2)}, u32[]{:S(2)}) %collective-permute-start) | collective-permute-done | bytes 524320 | tf_op jit(solution)/shard_map/ppermute | solution.py:412
  18.8 1.5 %collective-permute-start.6 = (bf16[256,2048]{1,0:T(8,128)(2,1)S(1)}, bf16[256,2048]{1,0:T(8,128)(2,1)S(1)}, u32[]{:S(2)}, u32[]{:S(2)}) collective-permute-start(bf16[256,2048]{1,0:T(8,128)(2,1)S(1)} %slice_select_fusion), channel_id=1, source_target_pairs={{0,4},{4,0},{8,12},{12,8},{16,20},{20,16},{24,28},{28,24},{1,5},{5... | collective-permute-start | bytes 3145736 | tf_op jit(solution)/shard_map/ppermute | solution.py:412
  20.4 4.0 %collective-permute-done.3 = bf16[256,512]{1,0:T(8,128)(2,1)S(1)} collective-permute-done((bf16[256,512]{1,0:T(8,128)(2,1)S(1)}, bf16[256,512]{1,0:T(8,128)(2,1)S(1)}, u32[]{:S(2)}, u32[]{:S(2)}) %collective-permute-start.3) | collective-permute-done | bytes 262176 | tf_op jit(solution)/shard_map/ppermute | solution.py:412
  24.4 0.0 collective-permute-done.1.refs_2_.c1
  24.4 0.0 collective-permute-start.5
  24.4 0.1 collective-permute-start.7
  24.5 3.2 %collective-permute-start.4 = (bf16[512,512]{1,0:T(8,128)(2,1)}, bf16[512,512]{1,0:T(8,128)(2,1)}, u32[]{:S(2)}, u32[]{:S(2)}) collective-permute-start(bf16[512,512]{1,0:T(8,128)(2,1)} %collective-permute-done.other.refs_1_), channel_id=1, source_target_pairs={{0,8},{4,12},{8,16},{12,20},{16,24},{20,28},{24,0},{28,4},{1,9},{5... | collective-permute-start | bytes 1572872 | tf_op jit(solution)/shard_map/ppermute | solution.py:412
  27.7 0.0 collective-permute-done.7.far
  27.7 2.6 %shard_map.83 = bf16[512,512]{1,0:T(8,128)(2,1)} custom-call(s32[4]{0:T(128)S(1)} %copy-done.14, bf16[512,512]{1,0:T(8,128)(2,1)S(1)} %constant_dynamic-update-slice_fusion.mine, bf16[512,512]{1,0:T(8,128)(2,1)S(1)} %collective-permute-done.7.far, bf16[592,512]{1,0:T(8,128)(2,1)S(1)} %copy-done.4, bf16[512,512]{1,0:T(8,128)(2,1)} %collective-permute-done.other.refs_1_), custom_call_target="tpu_custom_call" | custom-call | flops 536870912 | bytes 2703376 | tf_op jit(solution)/shard_map/pallas_call | solution.py:124
  30.3 19.1 %collective-permute-done.4.refs_3_ = bf16[512,512]{1,0:T(8,128)(2,1)} collective-permute-done((bf16[512,512]{1,0:T(8,128)(2,1)}, bf16[512,512]{1,0:T(8,128)(2,1)}, u32[]{:S(2)}, u32[]{:S(2)}) %collective-permute-start.4) | collective-permute-done | bytes 524320 | tf_op jit(solution)/shard_map/ppermute | solution.py:412
  49.4 0.0 collective-permute-done.5.refs_1_.c2
  49.4 0.0 collective-permute-done.6.near
  49.4 0.1 collective-permute-start.8
  49.5 0.0 copy-start.20
  49.5 0.0 copy-start.21
  49.6 1.0 collective-permute-start.11
  50.6 3.8 %collective-permute-done.11.s3 = bf16[80,512]{1,0:T(8,128)(2,1)S(1)} collective-permute-done((bf16[80,512]{1,0:T(8,128)(2,1)S(1)}, bf16[80,512]{1,0:T(8,128)(2,1)S(1)}, u32[]{:S(2)}, u32[]{:S(2)}) %collective-permute-start.11) | collective-permute-done | bytes 81952 | tf_op jit(solution)/shard_map/ppermute | solution.py:412
  54.4 0.0 collective-permute-done.8.far
  54.4 2.4 %shard_map.86 = f32[80,512]{1,0:T(8,128)S(1)} custom-call(s32[4]{0:T(128)S(1)} %copy-done.14, bf16[256,4096]{1,0:T(8,128)(2,1)S(1)} %copy-done, bf16[256,2048]{1,0:T(8,128)(2,1)S(1)} %collective-permute-done.6.near, bf16[256,2048]{1,0:T(8,128)(2,1)S(1)} %collective-permute-done.8.far, bf16[592,512]{1,0:T(8,128)(2,1)S(1)} %copy-done.4, ...), custom_call_target="tpu_custom_call" | custom-call | flops 301989888 | bytes 6258704 | tf_op jit(solution)/shard_map/pallas_call | solution.py:124
  56.8 0.9 collective-permute-start.12
  57.8 1.6 %collective-permute-start.9 = (bf16[512,512]{1,0:T(8,128)(2,1)}, bf16[512,512]{1,0:T(8,128)(2,1)}, u32[]{:S(2)}, u32[]{:S(2)}) collective-permute-start(bf16[512,512]{1,0:T(8,128)(2,1)} %shard_map.83), channel_id=1, source_target_pairs={{8,0},{12,4},{16,8},{20,12},{24,16},{28,20},{0,24},{4,28},{9,1},{1... | collective-permute-start | bytes 1572872 | tf_op jit(solution)/shard_map/ppermute | solution.py:412
  59.4 1.7 %collective-permute-start.10 = (bf16[512,512]{1,0:T(8,128)(2,1)}, bf16[512,512]{1,0:T(8,128)(2,1)}, u32[]{:S(2)}, u32[]{:S(2)}) collective-permute-start(bf16[512,512]{1,0:T(8,128)(2,1)} %collective-permute-done.4.refs_3_), channel_id=1, source_target_pairs={{0,8},{4,12},{8,16},{12,20},{16,24},{20,28},{24,0},{28,4},{1,9},{5... | collective-permute-start | bytes 1572872 | tf_op jit(solution)/shard_map/ppermute | solution.py:412
  61.1 1.5 %collective-permute-done.12 = f32[80,512]{1,0:T(8,128)S(1)} collective-permute-done((f32[80,512]{1,0:T(8,128)S(1)}, f32[80,512]{1,0:T(8,128)S(1)}, u32[]{:S(2)}, u32[]{:S(2)}) %collective-permute-start.12) | collective-permute-done | bytes 163872 | tf_op jit(solution)/shard_map/ppermute | solution.py:412
  62.7 0.7 copy-done.8
  63.4 1.5 %collective-permute-start.14 = (bf16[64,512]{1,0:T(8,128)(2,1)S(1)}, bf16[64,512]{1,0:T(8,128)(2,1)S(1)}, u32[]{:S(2)}, u32[]{:S(2)}) collective-permute-start(bf16[64,512]{1,0:T(8,128)(2,1)S(1)} %slice.27.some), channel_id=1, source_target_pairs={{0,2},{1,3},{2,0},{3,1},{4,6},{5,7},{6,4},{7,5},{8,10},{9,11},{10,... | collective-permute-start | bytes 196616 | tf_op jit(solution)/shard_map/ppermute | solution.py:412
  64.9 0.7 copy.9.bias
  65.5 0.7 copy.10.rate_of
  66.2 0.0 collective-permute-start.13
  66.2 1.4 %collective-permute-done.14.some_chip = bf16[64,512]{1,0:T(8,128)(2,1)S(1)} collective-permute-done((bf16[64,512]{1,0:T(8,128)(2,1)S(1)}, bf16[64,512]{1,0:T(8,128)(2,1)S(1)}, u32[]{:S(2)}, u32[]{:S(2)}) %collective-permute-start.14) | collective-permute-done | bytes 65568 | tf_op jit(solution)/shard_map/ppermute | solution.py:412
  67.6 0.0 collective-permute-start.15
  67.6 1.2 %copy-done.2 = bf16[256,2048]{1,0:T(8,128)(2,1)S(1)} copy-done((bf16[256,2048]{1,0:T(8,128)(2,1)S(1)}, bf16[256,2048]{1,0:T(8,128)(2,1)}, u32[]{:S(2)}) %copy-start.2) | copy-done | bytes 1048600
  68.9 1.1 copy-done.5
  70.0 2.7 %shard_map.84.refs_0_ = f32[2,256,512]{2,1,0:T(8,128)S(1)} custom-call(s32[4]{0:T(128)S(1)} %copy-done.14, bf16[256,4096]{1,0:T(8,128)(2,1)S(1)} %copy-done, bf16[256,2048]{1,0:T(8,128)(2,1)S(1)} %collective-permute-done.6.near, bf16[256,2048]{1,0:T(8,128)(2,1)S(1)} %copy-done.2, bf16[592,512]{1,0:T(8,128)(2,1)S(1)} %copy-done.5, ...), custom_call_target="tpu_custom_call" | custom-call | flops 1073741824 | bytes 7503888 | tf_op jit(solution)/shard_map/pallas_call | solution.py:124
  72.8 1.0 shard_map.85.acc
  73.7 0.0 collective-permute-done.13.some_core
  73.8 0.0 collective-permute-done.15.some_both
  73.8 0.8 copy-done.11
  74.6 0.8 copy-done.13
  75.5 1.8 %shard_map.87 = (bf16[2,4,256,256]{3,2,1,0:T(8,128)(2,1)S(1)}, bf16[2,4,128,256]{3,2,1,0:T(8,128)(2,1)S(1)}, bf16[2,256,128]{2,1,0:T(8,128)(2,1)S(1)}, f32[2,256...) custom-call(s32[4]{0:T(128)S(1)} %copy-done.15, bf16[64,512]{1,0:T(8,128)(2,1)S(1)} %copy-done.11, ...), custom_call_target="tpu_custom_call" | custom-call | flops 26214400 | bytes 2179152 | tf_op jit(solution)/shard_map/pallas_call | solution.py:124
  77.3 0.0 collective-permute-done.9.back
  77.3 7.3 %collective-permute-done.10.refs_0_ = bf16[512,512]{1,0:T(8,128)(2,1)} collective-permute-done((bf16[512,512]{1,0:T(8,128)(2,1)}, bf16[512,512]{1,0:T(8,128)(2,1)}, u32[]{:S(2)}, u32[]{:S(2)}) %collective-permute-start.10) | collective-permute-done | bytes 524320 | tf_op jit(solution)/shard_map/ppermute | solution.py:412
  84.6 2.0 %shard_map.88 = (bf16[2,256,512]{2,1,0:T(8,128)(2,1)S(1)}, bf16[128,512]{1,0:T(8,128)(2,1)S(1)}, bf16[128,512]{1,0:T(8,128)(2,1)S(1)}) custom-call(s32[4]{0:T(128)S(1)} %copy-done.15, bf16[256,4096]{1,0:T(8,128)(2,1)S(1)} %copy-done, bf16[256,2048]{1,0:T(8,128)(2,1)S(1)} %collective-permute-done.6.near, bf16[256,2048]{1,0:T(8,128)(2,1)S(1)} %copy-done.3, ...), custom_call_target="tpu_custom_call" | custom-call | flops 536870912 | bytes 7618576 | tf_op jit(solution)/shard_map/pallas_call | solution.py:124
  86.6 3.2 %collective-permute-start.17 = (bf16[128,512]{1,0:T(8,128)(2,1)S(1)}, bf16[128,512]{1,0:T(8,128)(2,1)S(1)}, u32[]{:S(2)}, u32[]{:S(2)}) collective-permute-start(bf16[128,512]{1,0:T(8,128)(2,1)S(1)} %get-tuple-element.46), channel_id=1, source_target_pairs={{0,8},{4,12},{8,16},{12,20},{16,24},{20,28},{1,9},{5,13},{9,17},{1... | collective-permute-start | bytes 393224 | tf_op jit(solution)/shard_map/ppermute | solution.py:412
  89.8 1.3 %collective-permute-start.18 = (bf16[128,512]{1,0:T(8,128)(2,1)S(1)}, bf16[128,512]{1,0:T(8,128)(2,1)S(1)}, u32[]{:S(2)}, u32[]{:S(2)}) collective-permute-start(bf16[128,512]{1,0:T(8,128)(2,1)S(1)} %get-tuple-element.46), channel_id=1, source_target_pairs={{0,16},{4,20},{8,24},{12,28},{1,17},{5,21},{9,25},{13,29},{2,18},{... | collective-permute-start | bytes 393224 | tf_op jit(solution)/shard_map/ppermute | solution.py:412
  91.1 1.9 %collective-permute-start.16 = (bf16[16,512]{1,0:T(8,128)(2,1)S(1)}, bf16[16,512]{1,0:T(8,128)(2,1)S(1)}, u32[]{:S(2)}, u32[]{:S(2)}) collective-permute-start(bf16[16,512]{1,0:T(8,128)(2,1)S(1)} %get-tuple-element.45), channel_id=1, source_target_pairs={{0,8},{4,12},{8,16},{12,20},{16,24},{20,28},{1,9},{5,13},{9,17},{1... | collective-permute-start | bytes 49160 | tf_op jit(solution)/shard_map/ppermute | solution.py:412
  93.0 1.1 %shard_map.89.local = f32[2,256,512]{2,1,0:T(8,128)S(1)} custom-call(s32[4]{0:T(128)S(1)} %copy-done.15, bf16[2,256,512]{2,1,0:T(8,128)(2,1)S(1)} %get-tuple-element.40.x, bf16[2,4,256,256]{3,2,1,0:T(8,128)(2,1)S(1)} %get-tuple-element.41.mixing, f32[1,8]{1,0:T(1,128)S(1)} %bitcast.10, bf16[2,256,128]{2,1,0:T(8,128)(2,1)S(1)} %get-tuple-element.42.c_rows, ...), custom_call_target="tpu_custom_call" | custom-call | flops 134217728 | bytes 2900016 | tf_op jit(solution)/shard_map/pallas_call | solution.py:124
  94.1 4.8 %collective-permute-done.16.passed = bf16[16,512]{1,0:T(8,128)(2,1)S(1)} collective-permute-done((bf16[16,512]{1,0:T(8,128)(2,1)S(1)}, bf16[16,512]{1,0:T(8,128)(2,1)S(1)}, u32[]{:S(2)}, u32[]{:S(2)}) %collective-permute-start.16) | collective-permute-done | bytes 16416 | tf_op jit(solution)/shard_map/ppermute | solution.py:412
  98.9 0.0 collective-permute-done.17.one
  98.9 0.0 collective-permute-done.18.two
  98.9 0.8 shard_map.91
  99.7 1.9 %collective-permute-start.19 = (bf16[256,512]{1,0:T(8,128)(2,1)S(1)}, bf16[256,512]{1,0:T(8,128)(2,1)S(1)}, u32[]{:S(2)}, u32[]{:S(2)}) collective-permute-start(bf16[256,512]{1,0:T(8,128)(2,1)S(1)} %shard_map.91), channel_id=1, source_target_pairs={{0,4},{4,0},{8,12},{12,8},{16,20},{20,16},{24,28},{28,24},{1,5},{5... | collective-permute-start | bytes 786440 | tf_op jit(solution)/shard_map/ppermute | solution.py:412
  101.6 0.8 shard_map.90
  102.4 3.8 %collective-permute-done.19 = bf16[256,512]{1,0:T(8,128)(2,1)S(1)} collective-permute-done((bf16[256,512]{1,0:T(8,128)(2,1)S(1)}, bf16[256,512]{1,0:T(8,128)(2,1)S(1)}, u32[]{:S(2)}, u32[]{:S(2)}) %collective-permute-start.19) | collective-permute-done | bytes 262176 | tf_op jit(solution)/shard_map/ppermute | solution.py:412
  106.2 0.9 maximum_select_fusion
  (44 shorter events, 0.2 us)
Async XLA Ops:
  0.0 10.7 %copy-start = (bf16[256,4096]{1,0:T(8,128)(2,1)S(1)}, bf16[256,4096]{1,0:T(8,128)(2,1)}, u32[]{:S(2)}) copy-start(bf16[256,4096]{1,0:T(8,128)(2,1)} %hidden.7) | copy-start | bytes 6291460
  1.1 8.1 %collective-permute-start.2 = (bf16[256,512]{1,0:T(8,128)(2,1)S(1)}, bf16[256,512]{1,0:T(8,128)(2,1)S(1)}, u32[]{:S(2)}, u32[]{:S(2)}) collective-permute-start(bf16[256,512]{1,0:T(8,128)(2,1)S(1)} %constant_dynamic-slice_fusion), channel_id=1, source_target_pairs={{0,8},{4,12},{8,16},{12,20},{16,24},{20,28},{24,0},{28,4},{1,9},{5... | collective-permute-start | bytes 786440 | tf_op jit(solution)/shard_map/ppermute | solution.py:412
  3.8 15.0 %collective-permute-start = (bf16[512,512]{1,0:T(8,128)(2,1)S(1)}, bf16[512,512]{1,0:T(8,128)(2,1)}, u32[]{:S(2)}, u32[]{:S(2)}) collective-permute-start(bf16[512,512]{1,0:T(8,128)(2,1)S(1)} %constant_dynamic-slice_fusion.1), channel_id=1, source_target_pairs={{0,4},{4,0},{8,12},{12,8},{16,20},{20,16},{24,28},{28,24},{1,5},{5... | collective-permute-start | bytes 1572872 | tf_op jit(solution)/shard_map/ppermute | solution.py:412
  8.7 15.7 %collective-permute-start.1 = (bf16[592,512]{1,0:T(8,128)(2,1)}, bf16[592,512]{1,0:T(8,128)(2,1)}, u32[]{:S(2)}, u32[]{:S(2)}) collective-permute-start(bf16[592,512]{1,0:T(8,128)(2,1)} %get-tuple-element.27.own.refs_0_.c0), channel_id=1, source_target_pairs={{0,8},{4,12},{8,16},{12,20},{16,24},{20,28},{24,0},{28,4},{1,9},{5... | collective-permute-start | bytes 1818632 | tf_op jit(solution)/shard_map/ppermute | solution.py:412
  9.0 18.7 %copy-start.4 = (bf16[592,512]{1,0:T(8,128)(2,1)S(1)}, bf16[592,512]{1,0:T(8,128)(2,1)}, u32[]{:S(2)}) copy-start(bf16[592,512]{1,0:T(8,128)(2,1)} %get-tuple-element.27.own.refs_0_.c0) | copy-start | bytes 1818628
  9.0 18.7 %copy-start.14 = (s32[4]{0:T(128)S(1)}, s32[4]{0:T(128)}, u32[]{:S(2)}) copy-start(s32[4]{0:T(128)} %pad_add_fusion.place) | copy-start | bytes 52
  9.2 15.1 %collective-permute-start.3 = (bf16[256,512]{1,0:T(8,128)(2,1)S(1)}, bf16[256,512]{1,0:T(8,128)(2,1)S(1)}, u32[]{:S(2)}, u32[]{:S(2)}) collective-permute-start(bf16[256,512]{1,0:T(8,128)(2,1)S(1)} %collective-permute-done.2), channel_id=1, source_target_pairs={{0,4},{4,0},{8,12},{12,8},{16,20},{20,16},{24,28},{28,24},{1,5},{5... | collective-permute-start | bytes 786440 | tf_op jit(solution)/shard_map/ppermute | solution.py:412
  10.9 38.7 %copy-start.22 = (bf16[80,512]{1,0:T(8,128)(2,1)S(1)}, bf16[80,512]{1,0:T(8,128)(2,1)}, u32[]{:S(2)}) copy-start(bf16[80,512]{1,0:T(8,128)(2,1)} %get-tuple-element.37) | copy-start | bytes 245764
  18.8 30.6 %collective-permute-start.6 = (bf16[256,2048]{1,0:T(8,128)(2,1)S(1)}, bf16[256,2048]{1,0:T(8,128)(2,1)S(1)}, u32[]{:S(2)}, u32[]{:S(2)}) collective-permute-start(bf16[256,2048]{1,0:T(8,128)(2,1)S(1)} %slice_select_fusion), channel_id=1, source_target_pairs={{0,4},{4,0},{8,12},{12,8},{16,20},{20,16},{24,28},{28,24},{1,5},{5... | collective-permute-start | bytes 3145736 | tf_op jit(solution)/shard_map/ppermute | solution.py:412
  24.4 25.1 %collective-permute-start.5 = (bf16[592,512]{1,0:T(8,128)(2,1)}, bf16[592,512]{1,0:T(8,128)(2,1)S(1)}, u32[]{:S(2)}, u32[]{:S(2)}) collective-permute-start(bf16[592,512]{1,0:T(8,128)(2,1)} %collective-permute-done.1.refs_2_.c1), channel_id=1, source_target_pairs={{0,8},{4,12},{8,16},{12,20},{16,24},{20,28},{24,0},{28,4},{1,9},{5... | collective-permute-start | bytes 1818632 | tf_op jit(solution)/shard_map/ppermute | solution.py:412
  24.4 3.3 %collective-permute-start.7 = (bf16[512,512]{1,0:T(8,128)(2,1)S(1)}, bf16[512,512]{1,0:T(8,128)(2,1)S(1)}, u32[]{:S(2)}, u32[]{:S(2)}) collective-permute-start(bf16[512,512]{1,0:T(8,128)(2,1)S(1)} %constant_dynamic-update-slice_fusion.mine), channel_id=1, source_target_pairs={{0,1},{1,0},{2,3},{3,2},{4,5},{5,4},{6,7},{7,6},{8,9},{9,8},{10,11... | collective-permute-start | bytes 1572872 | tf_op jit(solution)/shard_map/ppermute | solution.py:412
  24.5 24.9 %collective-permute-start.4 = (bf16[512,512]{1,0:T(8,128)(2,1)}, bf16[512,512]{1,0:T(8,128)(2,1)}, u32[]{:S(2)}, u32[]{:S(2)}) collective-permute-start(bf16[512,512]{1,0:T(8,128)(2,1)} %collective-permute-done.other.refs_1_), channel_id=1, source_target_pairs={{0,8},{4,12},{8,16},{12,20},{16,24},{20,28},{24,0},{28,4},{1,9},{5... | collective-permute-start | bytes 1572872 | tf_op jit(solution)/shard_map/ppermute | solution.py:412
  49.4 7.4 %copy-start.6 = (bf16[592,512]{1,0:T(8,128)(2,1)}, bf16[592,512]{1,0:T(8,128)(2,1)S(1)}, u32[]{:S(2)}) copy-start(bf16[592,512]{1,0:T(8,128)(2,1)S(1)} %collective-permute-done.5.refs_1_.c2) | copy-start | bytes 1818628
  49.4 4.9 %collective-permute-start.8 = (bf16[256,2048]{1,0:T(8,128)(2,1)S(1)}, bf16[256,2048]{1,0:T(8,128)(2,1)S(1)}, u32[]{:S(2)}, u32[]{:S(2)}) collective-permute-start(bf16[256,2048]{1,0:T(8,128)(2,1)S(1)} %collective-permute-done.6.near), channel_id=1, source_target_pairs={{0,1},{1,0},{2,3},{3,2},{4,5},{5,4},{6,7},{7,6},{8,9},{9,8},{10,11... | collective-permute-start | bytes 3145736 | tf_op jit(solution)/shard_map/ppermute | solution.py:412
  49.5 15.3 %copy-start.20 = (f32[8]{0:T(128)S(1)}, f32[8]{0:T(128)}, u32[]{:S(2)}) copy-start(f32[8]{0:T(128)} %param.13) | copy-start | bytes 100
  49.5 16.0 %copy-start.21 = (f32[8]{0:T(128)S(1)}, f32[8]{0:T(128)}, u32[]{:S(2)}) copy-start(f32[8]{0:T(128)} %param.14) | copy-start | bytes 100
  49.6 4.8 %collective-permute-start.11 = (bf16[80,512]{1,0:T(8,128)(2,1)S(1)}, bf16[80,512]{1,0:T(8,128)(2,1)S(1)}, u32[]{:S(2)}, u32[]{:S(2)}) collective-permute-start(bf16[80,512]{1,0:T(8,128)(2,1)S(1)} %copy-done.22), channel_id=1, source_target_pairs={{8,0},{12,4},{16,8},{20,12},{24,16},{28,20},{0,24},{4,28},{9,1},{1... | collective-permute-start | bytes 245768 | tf_op jit(solution)/shard_map/ppermute | solution.py:412
  54.4 2.4 %copy-start.1 = (bf16[256,2048]{1,0:T(8,128)(2,1)}, bf16[256,2048]{1,0:T(8,128)(2,1)S(1)}, u32[]{:S(2)}) copy-start(bf16[256,2048]{1,0:T(8,128)(2,1)S(1)} %collective-permute-done.8.far) | copy-start | bytes 3145732
  56.8 5.8 %collective-permute-start.12 = (f32[80,512]{1,0:T(8,128)S(1)}, f32[80,512]{1,0:T(8,128)S(1)}, u32[]{:S(2)}, u32[]{:S(2)}) collective-permute-start(f32[80,512]{1,0:T(8,128)S(1)} %shard_map.86), channel_id=1, source_target_pairs={{0,4},{4,0},{8,12},{12,8},{16,20},{20,16},{24,28},{28,24},{1,5},{5... | collective-permute-start | bytes 491528 | tf_op jit(solution)/shard_map/ppermute | solution.py:412
  57.8 19.5 %collective-permute-start.9 = (bf16[512,512]{1,0:T(8,128)(2,1)}, bf16[512,512]{1,0:T(8,128)(2,1)}, u32[]{:S(2)}, u32[]{:S(2)}) collective-permute-start(bf16[512,512]{1,0:T(8,128)(2,1)} %shard_map.83), channel_id=1, source_target_pairs={{8,0},{12,4},{16,8},{20,12},{24,16},{28,20},{0,24},{4,28},{9,1},{1... | collective-permute-start | bytes 1572872 | tf_op jit(solution)/shard_map/ppermute | solution.py:412
  59.4 25.2 %collective-permute-start.10 = (bf16[512,512]{1,0:T(8,128)(2,1)}, bf16[512,512]{1,0:T(8,128)(2,1)}, u32[]{:S(2)}, u32[]{:S(2)}) collective-permute-start(bf16[512,512]{1,0:T(8,128)(2,1)} %collective-permute-done.4.refs_3_), channel_id=1, source_target_pairs={{0,8},{4,12},{8,16},{12,20},{16,24},{20,28},{24,0},{28,4},{1,9},{5... | collective-permute-start | bytes 1572872 | tf_op jit(solution)/shard_map/ppermute | solution.py:412
  62.7 0.7 copy-start.8
  63.4 9.3 %copy-start.10 = (bf16[64,512]{1,0:T(8,128)(2,1)}, bf16[64,512]{1,0:T(8,128)(2,1)S(1)}, u32[]{:S(2)}) copy-start(bf16[64,512]{1,0:T(8,128)(2,1)S(1)} %slice.27.some) | copy-start | bytes 196612
  63.4 4.3 %collective-permute-start.14 = (bf16[64,512]{1,0:T(8,128)(2,1)S(1)}, bf16[64,512]{1,0:T(8,128)(2,1)S(1)}, u32[]{:S(2)}, u32[]{:S(2)}) collective-permute-start(bf16[64,512]{1,0:T(8,128)(2,1)S(1)} %slice.27.some), channel_id=1, source_target_pairs={{0,2},{1,3},{2,0},{3,1},{4,6},{5,7},{6,4},{7,5},{8,10},{9,11},{10,... | collective-permute-start | bytes 196616 | tf_op jit(solution)/shard_map/ppermute | solution.py:412
  66.2 7.5 %collective-permute-start.13 = (bf16[64,512]{1,0:T(8,128)(2,1)S(1)}, bf16[64,512]{1,0:T(8,128)(2,1)S(1)}, u32[]{:S(2)}, u32[]{:S(2)}) collective-permute-start(bf16[64,512]{1,0:T(8,128)(2,1)S(1)} %slice.27.some), channel_id=1, source_target_pairs={{0,1},{1,0},{2,3},{3,2},{4,5},{5,4},{6,7},{7,6},{8,9},{9,8},{10,11... | collective-permute-start | bytes 196616 | tf_op jit(solution)/shard_map/ppermute | solution.py:412
  67.6 5.1 %copy-start.12 = (bf16[64,512]{1,0:T(8,128)(2,1)}, bf16[64,512]{1,0:T(8,128)(2,1)S(1)}, u32[]{:S(2)}) copy-start(bf16[64,512]{1,0:T(8,128)(2,1)S(1)} %collective-permute-done.14.some_chip) | copy-start | bytes 196612
  67.6 6.1 %collective-permute-start.15 = (bf16[64,512]{1,0:T(8,128)(2,1)S(1)}, bf16[64,512]{1,0:T(8,128)(2,1)S(1)}, u32[]{:S(2)}, u32[]{:S(2)}) collective-permute-start(bf16[64,512]{1,0:T(8,128)(2,1)S(1)} %collective-permute-done.14.some_chip), channel_id=1, source_target_pairs={{0,1},{1,0},{2,3},{3,2},{4,5},{5,4},{6,7},{7,6},{8,9},{9,8},{10,11... | collective-permute-start | bytes 196616 | tf_op jit(solution)/shard_map/ppermute | solution.py:412
  67.6 1.2 %copy-start.2 = (bf16[256,2048]{1,0:T(8,128)(2,1)S(1)}, bf16[256,2048]{1,0:T(8,128)(2,1)}, u32[]{:S(2)}) copy-start(bf16[256,2048]{1,0:T(8,128)(2,1)} %copy-done.1) | copy-start | bytes 3145732
  68.9 1.1 copy-start.5
  70.0 2.7 %copy-start.7 = (bf16[592,512]{1,0:T(8,128)(2,1)S(1)}, bf16[592,512]{1,0:T(8,128)(2,1)}, u32[]{:S(2)}) copy-start(bf16[592,512]{1,0:T(8,128)(2,1)} %copy-done.6) | copy-start | bytes 1818628
  72.7 1.1 copy-start.9
  72.7 1.1 copy-start.15
  72.7 1.1 copy-start.17
  72.7 1.1 copy-start.18
  72.8 11.9 %copy-start.3 = (bf16[256,2048]{1,0:T(8,128)(2,1)S(1)}, bf16[256,2048]{1,0:T(8,128)(2,1)}, u32[]{:S(2)}) copy-start(bf16[256,2048]{1,0:T(8,128)(2,1)} %copy-done.1) | copy-start | bytes 3145732
  73.8 0.8 copy-start.11
  74.6 0.8 copy-start.13
  84.6 8.4 %copy-start.19 = (f32[8]{0:T(128)S(1)}, f32[8]{0:T(128)}, u32[]{:S(2)}) copy-start(f32[8]{0:T(128)} %param.15) | copy-start | bytes 100
  86.6 12.3 %collective-permute-start.17 = (bf16[128,512]{1,0:T(8,128)(2,1)S(1)}, bf16[128,512]{1,0:T(8,128)(2,1)S(1)}, u32[]{:S(2)}, u32[]{:S(2)}) collective-permute-start(bf16[128,512]{1,0:T(8,128)(2,1)S(1)} %get-tuple-element.46), channel_id=1, source_target_pairs={{0,8},{4,12},{8,16},{12,20},{16,24},{20,28},{1,9},{5,13},{9,17},{1... | collective-permute-start | bytes 393224 | tf_op jit(solution)/shard_map/ppermute | solution.py:412
  89.8 9.2 %collective-permute-start.18 = (bf16[128,512]{1,0:T(8,128)(2,1)S(1)}, bf16[128,512]{1,0:T(8,128)(2,1)S(1)}, u32[]{:S(2)}, u32[]{:S(2)}) collective-permute-start(bf16[128,512]{1,0:T(8,128)(2,1)S(1)} %get-tuple-element.46), channel_id=1, source_target_pairs={{0,16},{4,20},{8,24},{12,28},{1,17},{5,21},{9,25},{13,29},{2,18},{... | collective-permute-start | bytes 393224 | tf_op jit(solution)/shard_map/ppermute | solution.py:412
  91.1 7.8 %collective-permute-start.16 = (bf16[16,512]{1,0:T(8,128)(2,1)S(1)}, bf16[16,512]{1,0:T(8,128)(2,1)S(1)}, u32[]{:S(2)}, u32[]{:S(2)}) collective-permute-start(bf16[16,512]{1,0:T(8,128)(2,1)S(1)} %get-tuple-element.45), channel_id=1, source_target_pairs={{0,8},{4,12},{8,16},{12,20},{16,24},{20,28},{1,9},{5,13},{9,17},{1... | collective-permute-start | bytes 49160 | tf_op jit(solution)/shard_map/ppermute | solution.py:412
  93.0 8.6 %copy-start.16 = (s32[4]{0:T(128)S(1)}, s32[4]{0:T(128)}, u32[]{:S(2)}) copy-start(s32[4]{0:T(128)} %pad_add_fusion.place) | copy-start | bytes 52
  99.7 6.4 %collective-permute-start.19 = (bf16[256,512]{1,0:T(8,128)(2,1)S(1)}, bf16[256,512]{1,0:T(8,128)(2,1)S(1)}, u32[]{:S(2)}, u32[]{:S(2)}) collective-permute-start(bf16[256,512]{1,0:T(8,128)(2,1)S(1)} %shard_map.91), channel_id=1, source_target_pairs={{0,4},{4,0},{8,12},{12,8},{16,20},{20,16},{24,28},{28,24},{1,5},{5... | collective-permute-start | bytes 786440 | tf_op jit(solution)/shard_map/ppermute | solution.py:412

commit v7 on v6

--- a/solution.py
+++ b/solution.py
@@ -180,27 +180,18 @@
     small[maps:, :] = last
 
 
-def share_kernel(used, place, hidden, near, far, c0, c1, c2, s3, out, small, done):
+def share_kernel(used, place, hidden, near, far, c0, c1, c2, s3, out):
     plane, lane = place[0], place[1]
     rows = hidden.shape[0]
     size = c0.shape[1]
-    below = pl.ds(size, c0.shape[0] - size)
-    copies = [
-        pltpu.make_async_copy(c.at[below, :], small.at[i], done.at[i])
-        for i, c in enumerate((c0, c1, c2))
-    ]
-    copies.append(pltpu.make_async_copy(s3, small.at[3], done.at[3]))
-    for copy in copies:
-        copy.start()
     totals = [None, None]
-    for back, copy in enumerate(copies):
+    for back, s in enumerate((c0, c1, c2, s3)):
         at = LANES * ((plane + PLANES - back) % PLANES) + lane
-        copy.wait()
-        weights = small[back]
+        weights = s[...]
         for r, tokens in enumerate(depth_blocks(place, (hidden, near, far), at, size)):
             product = contract_last(weights, tokens)
             totals[r] = product if totals[r] is None else totals[r] + product
-    notes = [small[i, used:, :rows].astype(jnp.float32) for i in range(3)]
+    notes = [s[used:, :rows].astype(jnp.float32) for s in (c0, c1, c2)]
     row = lax.broadcasted_iota(jnp.int32, notes[0].shape, 0)
     ends = [n[0:1, rows - 1 : rows] for n in notes[1:]]
     note = jnp.where(row == 1, ends[0], jnp.where(row == 2, ends[1], notes[0]))
@@ -458,7 +449,10 @@
         other,
         flops=4 * rows * LANES * k_rows * half,
     )
-    other_one, own_two, near, part = together((other_one, own_two, near, part))
+    below_one = own_one[k_rows:]
+    other_one, own_two, near, part, below_one = together(
+        (other_one, own_two, near, part, below_one)
+    )
 
     other_two = send(other_one, along)
     from_next = send(part, back)
@@ -470,16 +464,11 @@
         hidden,
         near,
         far,
-        own,
-        own_one,
-        own_two,
+        small,
+        below_one,
+        own_two[k_rows:],
         small_next,
         flops=4 * rows * depth * used,
-        left=PLANES,
-        scratch=[
-            pltpu.VMEM((PLANES, used + heads, k_rows), bf16),
-            pltpu.SemaphoreType.DMA((PLANES,)),
-        ],
     )
 
     def early_products(backs, chunks, *totals):

time: 108 us -> 107 us (level)
  Pallas kernels: 17.7 us -> 16.6 us
  transfers between devices with their start and end apart: 20 -> 20, of which waited for: 10 -> 10; matrix products, arithmetic and copies ran while one was open for 3% -> 4% of each run, Pallas kernels for 12% -> 12%
where the time goes in v7:
time: 107 us; the launch traced here: 106 us
  waiting for transfers between devices  53.2 us (50%)
  starting transfers between devices  24.9 us (23%)
  Pallas kernels  16.6 us (16%)
  local copies, waits for them, and re-layouts  9.21 us (9%)
  other arithmetic  1.74 us (2%)
    ppermute x20, waiting for transfers between devices, send(): return lax.ppermute(x, axis, pairs)  53.2 us
    ppermute x20, starting transfers between devices, send(): return lax.ppermute(x, axis, pairs)  24.9 us
    pallas_call x10, Pallas kernels, call(): pl.pallas_call(body, out_shape=shapes, in_specs=[pl.BlockSpec(memory_spac...  16.6 us
    unnamed x47, local copies, waits for them, and re-layouts  4.74 us
  transfers between devices with their start and end apart: 20, of which 10 were waited for; matrix products, arithmetic and copies ran while one was open for 4% of the time, Pallas kernels for 12%

profile of v7, /device:TPU:16, one launch (start us, length us, event | category | flops | bytes accessed | tf_op | source)
XLA Modules:
  0.0 106.1 jit_solution(4026271639465472268)
XLA Ops:
  0.0 1.1 %constant_dynamic-slice_fusion = bf16[256,512]{1,0:T(8,128)(2,1)S(1)} fusion(bf16[256,4096]{1,0:T(8,128)(2,1)} %hidden.7, s32[]{:T(128)S(6)} %select_n.53), kind=kLoop, calls=%fused_computation.7 | loop fusion | bytes 524292 | tf_op jit(solution)/shard_map/dynamic_slice | solution.py:408
  1.1 1.6 %collective-permute-start.2 = (bf16[256,512]{1,0:T(8,128)(2,1)S(1)}, bf16[256,512]{1,0:T(8,128)(2,1)S(1)}, u32[]{:S(2)}, u32[]{:S(2)}) collective-permute-start(bf16[256,512]{1,0:T(8,128)(2,1)S(1)} %constant_dynamic-slice_fusion), channel_id=1, source_target_pairs={{0,8},{4,12},{8,16},{12,20},{16,24},{20,28},{24,0},{28,4},{1,9},{5... | collective-permute-start | bytes 786440 | tf_op jit(solution)/shard_map/ppermute | solution.py:403
  2.8 1.1 %constant_dynamic-slice_fusion.1 = bf16[512,512]{1,0:T(8,128)(2,1)S(1)} fusion(bf16[512,1024]{1,0:T(8,128)(2,1)} %x_weight.1, s32[]{:T(128)S(6)} %select_n.51), kind=kLoop, calls=%fused_computation.8 | loop fusion | bytes 1048580 | tf_op jit(solution)/shard_map/dynamic_slice | solution.py:409
  3.8 1.6 %collective-permute-start = (bf16[512,512]{1,0:T(8,128)(2,1)S(1)}, bf16[512,512]{1,0:T(8,128)(2,1)}, u32[]{:S(2)}, u32[]{:S(2)}) collective-permute-start(bf16[512,512]{1,0:T(8,128)(2,1)S(1)} %constant_dynamic-slice_fusion.1), channel_id=1, source_target_pairs={{0,4},{4,0},{8,12},{12,8},{16,20},{20,16},{24,28},{28,24},{1,5},{5... | collective-permute-start | bytes 1572872 | tf_op jit(solution)/shard_map/ppermute | solution.py:403
  5.4 0.7 pad_add_fusion.place
  6.1 2.6 %shard_map.82 = (bf16[592,512]{1,0:T(8,128)(2,1)}, bf16[80,512]{1,0:T(8,128)(2,1)}) custom-call(s32[4]{0:T(128)} %pad_add_fusion.place, bf16[512,1024]{1,0:T(8,128)(2,1)} %x_weight.1, bf16[64,512]{1,0:T(8,128)(2,1)} %bitcast.11, bf16[8,512]{1,0:T(8,128)(2,1)} %bitcast.12, s32[1,256]{1,0:T(1,128)} %bitcast.13), custom_call_target="tpu_custom_call" | custom-call | bytes 1811472 | tf_op jit(solution)/shard_map/pallas_call | solution.py:124
  8.7 0.3 collective-permute-start.1
  9.0 0.2 collective-permute-done.2
  9.2 1.5 %collective-permute-start.3 = (bf16[256,512]{1,0:T(8,128)(2,1)S(1)}, bf16[256,512]{1,0:T(8,128)(2,1)S(1)}, u32[]{:S(2)}, u32[]{:S(2)}) collective-permute-start(bf16[256,512]{1,0:T(8,128)(2,1)S(1)} %collective-permute-done.2), channel_id=1, source_target_pairs={{0,4},{4,0},{8,12},{12,8},{16,20},{20,16},{24,28},{28,24},{1,5},{5... | collective-permute-start | bytes 786440 | tf_op jit(solution)/shard_map/ppermute | solution.py:403
  10.7 0.1 slice_select_fusion
  10.9 8.0 %collective-permute-done.other.refs_1_ = bf16[512,512]{1,0:T(8,128)(2,1)} collective-permute-done((bf16[512,512]{1,0:T(8,128)(2,1)S(1)}, bf16[512,512]{1,0:T(8,128)(2,1)}, u32[]{:S(2)}, u32[]{:S(2)}) %collective-permute-start) | collective-permute-done | bytes 524320 | tf_op jit(solution)/shard_map/ppermute | solution.py:403
  18.8 1.5 %collective-permute-start.6 = (bf16[256,2048]{1,0:T(8,128)(2,1)S(1)}, bf16[256,2048]{1,0:T(8,128)(2,1)S(1)}, u32[]{:S(2)}, u32[]{:S(2)}) collective-permute-start(bf16[256,2048]{1,0:T(8,128)(2,1)S(1)} %slice_select_fusion), channel_id=1, source_target_pairs={{0,4},{4,0},{8,12},{12,8},{16,20},{20,16},{24,28},{28,24},{1,5},{5... | collective-permute-start | bytes 3145736 | tf_op jit(solution)/shard_map/ppermute | solution.py:403
  20.4 4.0 %collective-permute-done.3 = bf16[256,512]{1,0:T(8,128)(2,1)S(1)} collective-permute-done((bf16[256,512]{1,0:T(8,128)(2,1)S(1)}, bf16[256,512]{1,0:T(8,128)(2,1)S(1)}, u32[]{:S(2)}, u32[]{:S(2)}) %collective-permute-start.3) | collective-permute-done | bytes 262176 | tf_op jit(solution)/shard_map/ppermute | solution.py:403
  24.4 0.0 collective-permute-done.1.refs_2_
  24.4 0.0 collective-permute-start.5
  24.4 0.1 collective-permute-start.7
  24.5 3.2 %collective-permute-start.4 = (bf16[512,512]{1,0:T(8,128)(2,1)}, bf16[512,512]{1,0:T(8,128)(2,1)}, u32[]{:S(2)}, u32[]{:S(2)}) collective-permute-start(bf16[512,512]{1,0:T(8,128)(2,1)} %collective-permute-done.other.refs_1_), channel_id=1, source_target_pairs={{0,8},{4,12},{8,16},{12,20},{16,24},{20,28},{24,0},{28,4},{1,9},{5... | collective-permute-start | bytes 1572872 | tf_op jit(solution)/shard_map/ppermute | solution.py:403
  27.7 0.9 slice.24.c1
  28.6 0.0 collective-permute-done.7.far
  28.6 2.6 %shard_map.83 = bf16[512,512]{1,0:T(8,128)(2,1)} custom-call(s32[4]{0:T(128)S(1)} %copy-done.15, bf16[512,512]{1,0:T(8,128)(2,1)S(1)} %constant_dynamic-update-slice_fusion.mine, bf16[512,512]{1,0:T(8,128)(2,1)S(1)} %collective-permute-done.7.far, bf16[592,512]{1,0:T(8,128)(2,1)S(1)} %copy-done.4, bf16[512,512]{1,0:T(8,128)(2,1)} %collective-permute-done.other.refs_1_), custom_call_target="tpu_custom_call" | custom-call | flops 536870912 | bytes 2703376 | tf_op jit(solution)/shard_map/pallas_call | solution.py:124
  31.2 18.2 %collective-permute-done.4.refs_3_ = bf16[512,512]{1,0:T(8,128)(2,1)} collective-permute-done((bf16[512,512]{1,0:T(8,128)(2,1)}, bf16[512,512]{1,0:T(8,128)(2,1)}, u32[]{:S(2)}, u32[]{:S(2)}) %collective-permute-start.4) | collective-permute-done | bytes 524320 | tf_op jit(solution)/shard_map/ppermute | solution.py:403
  49.4 0.0 collective-permute-done.5.refs_1_
  49.4 0.0 collective-permute-done.6.near
  49.4 0.1 collective-permute-start.8
  49.5 1.0 collective-permute-start.11
  50.5 0.0 copy-start.22
  50.6 3.8 %collective-permute-done.11.s3 = bf16[80,512]{1,0:T(8,128)(2,1)S(1)} collective-permute-done((bf16[80,512]{1,0:T(8,128)(2,1)S(1)}, bf16[80,512]{1,0:T(8,128)(2,1)S(1)}, u32[]{:S(2)}, u32[]{:S(2)}) %collective-permute-start.11) | collective-permute-done | bytes 81952 | tf_op jit(solution)/shard_map/ppermute | solution.py:403
  54.4 0.0 collective-permute-done.8.far
  54.4 1.3 %shard_map.86 = f32[80,512]{1,0:T(8,128)S(1)} custom-call(s32[4]{0:T(128)S(1)} %copy-done.15, bf16[256,4096]{1,0:T(8,128)(2,1)S(1)} %copy-done, bf16[256,2048]{1,0:T(8,128)(2,1)S(1)} %collective-permute-done.6.near, bf16[256,2048]{1,0:T(8,128)(2,1)S(1)} %collective-permute-done.8.far, bf16[80,512]{1,0:T(8,128)(2,1)S(1)} %copy-done.12, ...), custom_call_target="tpu_custom_call" | custom-call | flops 301989888 | bytes 4685840 | tf_op jit(solution)/shard_map/pallas_call | solution.py:124
  55.7 0.9 collective-permute-start.12
  56.7 1.6 %collective-permute-start.9 = (bf16[512,512]{1,0:T(8,128)(2,1)}, bf16[512,512]{1,0:T(8,128)(2,1)}, u32[]{:S(2)}, u32[]{:S(2)}) collective-permute-start(bf16[512,512]{1,0:T(8,128)(2,1)} %shard_map.83), channel_id=1, source_target_pairs={{8,0},{12,4},{16,8},{20,12},{24,16},{28,20},{0,24},{4,28},{9,1},{1... | collective-permute-start | bytes 1572872 | tf_op jit(solution)/shard_map/ppermute | solution.py:403
  58.3 1.7 %collective-permute-start.10 = (bf16[512,512]{1,0:T(8,128)(2,1)}, bf16[512,512]{1,0:T(8,128)(2,1)}, u32[]{:S(2)}, u32[]{:S(2)}) collective-permute-start(bf16[512,512]{1,0:T(8,128)(2,1)} %collective-permute-done.4.refs_3_), channel_id=1, source_target_pairs={{0,8},{4,12},{8,16},{12,20},{16,24},{20,28},{24,0},{28,4},{1,9},{5... | collective-permute-start | bytes 1572872 | tf_op jit(solution)/shard_map/ppermute | solution.py:403
  60.0 1.5 %collective-permute-done.12 = f32[80,512]{1,0:T(8,128)S(1)} collective-permute-done((f32[80,512]{1,0:T(8,128)S(1)}, f32[80,512]{1,0:T(8,128)S(1)}, u32[]{:S(2)}, u32[]{:S(2)}) %collective-permute-start.12) | collective-permute-done | bytes 163872 | tf_op jit(solution)/shard_map/ppermute | solution.py:403
  61.6 0.7 copy-done.6
  62.3 1.5 %collective-permute-start.14 = (bf16[64,512]{1,0:T(8,128)(2,1)S(1)}, bf16[64,512]{1,0:T(8,128)(2,1)S(1)}, u32[]{:S(2)}, u32[]{:S(2)}) collective-permute-start(bf16[64,512]{1,0:T(8,128)(2,1)S(1)} %slice.35.some), channel_id=1, source_target_pairs={{0,2},{1,3},{2,0},{3,1},{4,6},{5,7},{6,4},{7,5},{8,10},{9,11},{10,... | collective-permute-start | bytes 196616 | tf_op jit(solution)/shard_map/ppermute | solution.py:403
  63.8 0.7 copy.9.bias
  64.4 0.7 copy.10.rate_of
  65.1 0.0 collective-permute-start.13
  65.1 1.4 %collective-permute-done.14.some_chip = bf16[64,512]{1,0:T(8,128)(2,1)S(1)} collective-permute-done((bf16[64,512]{1,0:T(8,128)(2,1)S(1)}, bf16[64,512]{1,0:T(8,128)(2,1)S(1)}, u32[]{:S(2)}, u32[]{:S(2)}) %collective-permute-start.14) | collective-permute-done | bytes 65568 | tf_op jit(solution)/shard_map/ppermute | solution.py:403
  66.5 0.0 collective-permute-start.15
  66.5 1.2 %copy-done.2 = bf16[256,2048]{1,0:T(8,128)(2,1)S(1)} copy-done((bf16[256,2048]{1,0:T(8,128)(2,1)S(1)}, bf16[256,2048]{1,0:T(8,128)(2,1)}, u32[]{:S(2)}) %copy-start.2) | copy-done | bytes 1048600
  67.8 1.1 %copy-done.5 = bf16[592,512]{1,0:T(8,128)(2,1)S(1)} copy-done((bf16[592,512]{1,0:T(8,128)(2,1)S(1)}, bf16[592,512]{1,0:T(8,128)(2,1)}, u32[]{:S(2)}) %copy-start.5) | copy-done | bytes 606232
  68.9 2.7 %shard_map.84.refs_0_ = f32[2,256,512]{2,1,0:T(8,128)S(1)} custom-call(s32[4]{0:T(128)S(1)} %copy-done.15, bf16[256,4096]{1,0:T(8,128)(2,1)S(1)} %copy-done, bf16[256,2048]{1,0:T(8,128)(2,1)S(1)} %collective-permute-done.6.near, bf16[256,2048]{1,0:T(8,128)(2,1)S(1)} %copy-done.2, bf16[592,512]{1,0:T(8,128)(2,1)S(1)} %copy-done.5, ...), custom_call_target="tpu_custom_call" | custom-call | flops 1073741824 | bytes 7503888 | tf_op jit(solution)/shard_map/pallas_call | solution.py:124
  71.7 1.0 shard_map.85.acc
  72.6 0.0 collective-permute-done.13.some_core
  72.7 0.0 collective-permute-done.15.some_both
  72.7 0.8 copy-done.11
  73.6 0.8 copy-done.14
  74.4 1.8 %shard_map.87 = (bf16[2,4,256,256]{3,2,1,0:T(8,128)(2,1)S(1)}, bf16[2,4,128,256]{3,2,1,0:T(8,128)(2,1)S(1)}, bf16[2,256,128]{2,1,0:T(8,128)(2,1)S(1)}, f32[2,256...) custom-call(s32[4]{0:T(128)S(1)} %copy-done.16, bf16[64,512]{1,0:T(8,128)(2,1)S(1)} %copy-done.11, ...), custom_call_target="tpu_custom_call" | custom-call | flops 26214400 | bytes 2179152 | tf_op jit(solution)/shard_map/pallas_call | solution.py:124
  76.2 0.0 collective-permute-done.9.back
  76.2 7.3 %collective-permute-done.10.refs_0_ = bf16[512,512]{1,0:T(8,128)(2,1)} collective-permute-done((bf16[512,512]{1,0:T(8,128)(2,1)}, bf16[512,512]{1,0:T(8,128)(2,1)}, u32[]{:S(2)}, u32[]{:S(2)}) %collective-permute-start.10) | collective-permute-done | bytes 524320 | tf_op jit(solution)/shard_map/ppermute | solution.py:403
  83.5 2.0 %shard_map.88 = (bf16[2,256,512]{2,1,0:T(8,128)(2,1)S(1)}, bf16[128,512]{1,0:T(8,128)(2,1)S(1)}, bf16[128,512]{1,0:T(8,128)(2,1)S(1)}) custom-call(s32[4]{0:T(128)S(1)} %copy-done.16, bf16[256,4096]{1,0:T(8,128)(2,1)S(1)} %copy-done, bf16[256,2048]{1,0:T(8,128)(2,1)S(1)} %collective-permute-done.6.near, bf16[256,2048]{1,0:T(8,128)(2,1)S(1)} %copy-done.3, ...), custom_call_target="tpu_custom_call" | custom-call | flops 536870912 | bytes 7618576 | tf_op jit(solution)/shard_map/pallas_call | solution.py:124
  85.5 3.2 %collective-permute-start.17 = (bf16[128,512]{1,0:T(8,128)(2,1)S(1)}, bf16[128,512]{1,0:T(8,128)(2,1)S(1)}, u32[]{:S(2)}, u32[]{:S(2)}) collective-permute-start(bf16[128,512]{1,0:T(8,128)(2,1)S(1)} %get-tuple-element.48), channel_id=1, source_target_pairs={{0,8},{4,12},{8,16},{12,20},{16,24},{20,28},{1,9},{5,13},{9,17},{1... | collective-permute-start | bytes 393224 | tf_op jit(solution)/shard_map/ppermute | solution.py:403
  88.7 1.3 %collective-permute-start.18 = (bf16[128,512]{1,0:T(8,128)(2,1)S(1)}, bf16[128,512]{1,0:T(8,128)(2,1)S(1)}, u32[]{:S(2)}, u32[]{:S(2)}) collective-permute-start(bf16[128,512]{1,0:T(8,128)(2,1)S(1)} %get-tuple-element.48), channel_id=1, source_target_pairs={{0,16},{4,20},{8,24},{12,28},{1,17},{5,21},{9,25},{13,29},{2,18},{... | collective-permute-start | bytes 393224 | tf_op jit(solution)/shard_map/ppermute | solution.py:403
  90.0 1.9 %collective-permute-start.16 = (bf16[16,512]{1,0:T(8,128)(2,1)S(1)}, bf16[16,512]{1,0:T(8,128)(2,1)S(1)}, u32[]{:S(2)}, u32[]{:S(2)}) collective-permute-start(bf16[16,512]{1,0:T(8,128)(2,1)S(1)} %get-tuple-element.47), channel_id=1, source_target_pairs={{0,8},{4,12},{8,16},{12,20},{16,24},{20,28},{1,9},{5,13},{9,17},{1... | collective-permute-start | bytes 49160 | tf_op jit(solution)/shard_map/ppermute | solution.py:403
  91.9 1.1 %shard_map.89.local = f32[2,256,512]{2,1,0:T(8,128)S(1)} custom-call(s32[4]{0:T(128)S(1)} %copy-done.16, bf16[2,256,512]{2,1,0:T(8,128)(2,1)S(1)} %get-tuple-element.42.x, bf16[2,4,256,256]{3,2,1,0:T(8,128)(2,1)S(1)} %get-tuple-element.43.mixing, f32[1,8]{1,0:T(1,128)S(1)} %bitcast.10, bf16[2,256,128]{2,1,0:T(8,128)(2,1)S(1)} %get-tuple-element.44.c_rows, ...), custom_call_target="tpu_custom_call" | custom-call | flops 134217728 | bytes 2900016 | tf_op jit(solution)/shard_map/pallas_call | solution.py:124
  93.0 4.9 %collective-permute-done.16.passed = bf16[16,512]{1,0:T(8,128)(2,1)S(1)} collective-permute-done((bf16[16,512]{1,0:T(8,128)(2,1)S(1)}, bf16[16,512]{1,0:T(8,128)(2,1)S(1)}, u32[]{:S(2)}, u32[]{:S(2)}) %collective-permute-start.16) | collective-permute-done | bytes 16416 | tf_op jit(solution)/shard_map/ppermute | solution.py:403
  97.9 0.0 collective-permute-done.17.one
  97.9 0.0 collective-permute-done.18.two
  97.9 0.8 shard_map.91
  98.7 1.8 %collective-permute-start.19 = (bf16[256,512]{1,0:T(8,128)(2,1)S(1)}, bf16[256,512]{1,0:T(8,128)(2,1)S(1)}, u32[]{:S(2)}, u32[]{:S(2)}) collective-permute-start(bf16[256,512]{1,0:T(8,128)(2,1)S(1)} %shard_map.91), channel_id=1, source_target_pairs={{0,4},{4,0},{8,12},{12,8},{16,20},{20,16},{24,28},{28,24},{1,5},{5... | collective-permute-start | bytes 786440 | tf_op jit(solution)/shard_map/ppermute | solution.py:403
  100.5 0.8 shard_map.90
  101.3 3.8 %collective-permute-done.19 = bf16[256,512]{1,0:T(8,128)(2,1)S(1)} collective-permute-done((bf16[256,512]{1,0:T(8,128)(2,1)S(1)}, bf16[256,512]{1,0:T(8,128)(2,1)S(1)}, u32[]{:S(2)}, u32[]{:S(2)}) %collective-permute-start.19) | collective-permute-done | bytes 262176 | tf_op jit(solution)/shard_map/ppermute | solution.py:403
  105.1 0.9 maximum_select_fusion
  (46 shorter events, 0.2 us)
Async XLA Ops:
  0.0 10.7 %copy-start = (bf16[256,4096]{1,0:T(8,128)(2,1)S(1)}, bf16[256,4096]{1,0:T(8,128)(2,1)}, u32[]{:S(2)}) copy-start(bf16[256,4096]{1,0:T(8,128)(2,1)} %hidden.7) | copy-start | bytes 6291460
  1.1 8.1 %collective-permute-start.2 = (bf16[256,512]{1,0:T(8,128)(2,1)S(1)}, bf16[256,512]{1,0:T(8,128)(2,1)S(1)}, u32[]{:S(2)}, u32[]{:S(2)}) collective-permute-start(bf16[256,512]{1,0:T(8,128)(2,1)S(1)} %constant_dynamic-slice_fusion), channel_id=1, source_target_pairs={{0,8},{4,12},{8,16},{12,20},{16,24},{20,28},{24,0},{28,4},{1,9},{5... | collective-permute-start | bytes 786440 | tf_op jit(solution)/shard_map/ppermute | solution.py:403
  3.8 15.0 %collective-permute-start = (bf16[512,512]{1,0:T(8,128)(2,1)S(1)}, bf16[512,512]{1,0:T(8,128)(2,1)}, u32[]{:S(2)}, u32[]{:S(2)}) collective-permute-start(bf16[512,512]{1,0:T(8,128)(2,1)S(1)} %constant_dynamic-slice_fusion.1), channel_id=1, source_target_pairs={{0,4},{4,0},{8,12},{12,8},{16,20},{20,16},{24,28},{28,24},{1,5},{5... | collective-permute-start | bytes 1572872 | tf_op jit(solution)/shard_map/ppermute | solution.py:403
  8.7 15.7 %collective-permute-start.1 = (bf16[592,512]{1,0:T(8,128)(2,1)}, bf16[592,512]{1,0:T(8,128)(2,1)}, u32[]{:S(2)}, u32[]{:S(2)}) collective-permute-start(bf16[592,512]{1,0:T(8,128)(2,1)} %get-tuple-element.28.own.refs_0_), channel_id=1, source_target_pairs={{0,8},{4,12},{8,16},{12,20},{16,24},{20,28},{24,0},{28,4},{1,9},{5... | collective-permute-start | bytes 1818632 | tf_op jit(solution)/shard_map/ppermute | solution.py:403
  9.0 19.6 %copy-start.4 = (bf16[592,512]{1,0:T(8,128)(2,1)S(1)}, bf16[592,512]{1,0:T(8,128)(2,1)}, u32[]{:S(2)}) copy-start(bf16[592,512]{1,0:T(8,128)(2,1)} %get-tuple-element.28.own.refs_0_) | copy-start | bytes 1818628
  9.0 19.6 %copy-start.15 = (s32[4]{0:T(128)S(1)}, s32[4]{0:T(128)}, u32[]{:S(2)}) copy-start(s32[4]{0:T(128)} %pad_add_fusion.place) | copy-start | bytes 52
  9.2 15.1 %collective-permute-start.3 = (bf16[256,512]{1,0:T(8,128)(2,1)S(1)}, bf16[256,512]{1,0:T(8,128)(2,1)S(1)}, u32[]{:S(2)}, u32[]{:S(2)}) collective-permute-start(bf16[256,512]{1,0:T(8,128)(2,1)S(1)} %collective-permute-done.2), channel_id=1, source_target_pairs={{0,4},{4,0},{8,12},{12,8},{16,20},{20,16},{24,28},{28,24},{1,5},{5... | collective-permute-start | bytes 786440 | tf_op jit(solution)/shard_map/ppermute | solution.py:403
  10.9 38.7 %copy-start.12 = (bf16[80,512]{1,0:T(8,128)(2,1)S(1)}, bf16[80,512]{1,0:T(8,128)(2,1)}, u32[]{:S(2)}) copy-start(bf16[80,512]{1,0:T(8,128)(2,1)} %get-tuple-element.38.c0) | copy-start | bytes 245764
  18.8 30.6 %collective-permute-start.6 = (bf16[256,2048]{1,0:T(8,128)(2,1)S(1)}, bf16[256,2048]{1,0:T(8,128)(2,1)S(1)}, u32[]{:S(2)}, u32[]{:S(2)}) collective-permute-start(bf16[256,2048]{1,0:T(8,128)(2,1)S(1)} %slice_select_fusion), channel_id=1, source_target_pairs={{0,4},{4,0},{8,12},{12,8},{16,20},{20,16},{24,28},{28,24},{1,5},{5... | collective-permute-start | bytes 3145736 | tf_op jit(solution)/shard_map/ppermute | solution.py:403
  24.4 25.1 %collective-permute-start.5 = (bf16[592,512]{1,0:T(8,128)(2,1)}, bf16[592,512]{1,0:T(8,128)(2,1)S(1)}, u32[]{:S(2)}, u32[]{:S(2)}) collective-permute-start(bf16[592,512]{1,0:T(8,128)(2,1)} %collective-permute-done.1.refs_2_), channel_id=1, source_target_pairs={{0,8},{4,12},{8,16},{12,20},{16,24},{20,28},{24,0},{28,4},{1,9},{5... | collective-permute-start | bytes 1818632 | tf_op jit(solution)/shard_map/ppermute | solution.py:403
  24.4 4.2 %collective-permute-start.7 = (bf16[512,512]{1,0:T(8,128)(2,1)S(1)}, bf16[512,512]{1,0:T(8,128)(2,1)S(1)}, u32[]{:S(2)}, u32[]{:S(2)}) collective-permute-start(bf16[512,512]{1,0:T(8,128)(2,1)S(1)} %constant_dynamic-update-slice_fusion.mine), channel_id=1, source_target_pairs={{0,1},{1,0},{2,3},{3,2},{4,5},{5,4},{6,7},{7,6},{8,9},{9,8},{10,11... | collective-permute-start | bytes 1572872 | tf_op jit(solution)/shard_map/ppermute | solution.py:403
  24.5 24.9 %collective-permute-start.4 = (bf16[512,512]{1,0:T(8,128)(2,1)}, bf16[512,512]{1,0:T(8,128)(2,1)}, u32[]{:S(2)}, u32[]{:S(2)}) collective-permute-start(bf16[512,512]{1,0:T(8,128)(2,1)} %collective-permute-done.other.refs_1_), channel_id=1, source_target_pairs={{0,8},{4,12},{8,16},{12,20},{16,24},{20,28},{24,0},{28,4},{1,9},{5... | collective-permute-start | bytes 1572872 | tf_op jit(solution)/shard_map/ppermute | solution.py:403
  49.4 6.3 %copy-start.8 = (bf16[592,512]{1,0:T(8,128)(2,1)}, bf16[592,512]{1,0:T(8,128)(2,1)S(1)}, u32[]{:S(2)}) copy-start(bf16[592,512]{1,0:T(8,128)(2,1)S(1)} %collective-permute-done.5.refs_1_) | copy-start | bytes 1818628
  49.4 4.9 %collective-permute-start.8 = (bf16[256,2048]{1,0:T(8,128)(2,1)S(1)}, bf16[256,2048]{1,0:T(8,128)(2,1)S(1)}, u32[]{:S(2)}, u32[]{:S(2)}) collective-permute-start(bf16[256,2048]{1,0:T(8,128)(2,1)S(1)} %collective-permute-done.6.near), channel_id=1, source_target_pairs={{0,1},{1,0},{2,3},{3,2},{4,5},{5,4},{6,7},{7,6},{8,9},{9,8},{10,11... | collective-permute-start | bytes 3145736 | tf_op jit(solution)/shard_map/ppermute | solution.py:403
  49.5 4.8 %collective-permute-start.11 = (bf16[80,512]{1,0:T(8,128)(2,1)S(1)}, bf16[80,512]{1,0:T(8,128)(2,1)S(1)}, u32[]{:S(2)}, u32[]{:S(2)}) collective-permute-start(bf16[80,512]{1,0:T(8,128)(2,1)S(1)} %copy-done.12), channel_id=1, source_target_pairs={{8,0},{12,4},{16,8},{20,12},{24,16},{28,20},{0,24},{4,28},{9,1},{1... | collective-permute-start | bytes 245768 | tf_op jit(solution)/shard_map/ppermute | solution.py:403
  50.5 13.2 %copy-start.21 = (f32[8]{0:T(128)S(1)}, f32[8]{0:T(128)}, u32[]{:S(2)}) copy-start(f32[8]{0:T(128)} %param.13) | copy-start | bytes 100
  50.5 13.9 %copy-start.22 = (f32[8]{0:T(128)S(1)}, f32[8]{0:T(128)}, u32[]{:S(2)}) copy-start(f32[8]{0:T(128)} %param.14) | copy-start | bytes 100
  54.4 1.3 %copy-start.1 = (bf16[256,2048]{1,0:T(8,128)(2,1)}, bf16[256,2048]{1,0:T(8,128)(2,1)S(1)}, u32[]{:S(2)}) copy-start(bf16[256,2048]{1,0:T(8,128)(2,1)S(1)} %collective-permute-done.8.far) | copy-start | bytes 3145732
  55.7 5.8 %collective-permute-start.12 = (f32[80,512]{1,0:T(8,128)S(1)}, f32[80,512]{1,0:T(8,128)S(1)}, u32[]{:S(2)}, u32[]{:S(2)}) collective-permute-start(f32[80,512]{1,0:T(8,128)S(1)} %shard_map.86), channel_id=1, source_target_pairs={{0,4},{4,0},{8,12},{12,8},{16,20},{20,16},{24,28},{28,24},{1,5},{5... | collective-permute-start | bytes 491528 | tf_op jit(solution)/shard_map/ppermute | solution.py:403
  56.7 19.5 %collective-permute-start.9 = (bf16[512,512]{1,0:T(8,128)(2,1)}, bf16[512,512]{1,0:T(8,128)(2,1)}, u32[]{:S(2)}, u32[]{:S(2)}) collective-permute-start(bf16[512,512]{1,0:T(8,128)(2,1)} %shard_map.83), channel_id=1, source_target_pairs={{8,0},{12,4},{16,8},{20,12},{24,16},{28,20},{0,24},{4,28},{9,1},{1... | collective-permute-start | bytes 1572872 | tf_op jit(solution)/shard_map/ppermute | solution.py:403
  58.3 25.2 %collective-permute-start.10 = (bf16[512,512]{1,0:T(8,128)(2,1)}, bf16[512,512]{1,0:T(8,128)(2,1)}, u32[]{:S(2)}, u32[]{:S(2)}) collective-permute-start(bf16[512,512]{1,0:T(8,128)(2,1)} %collective-permute-done.4.refs_3_), channel_id=1, source_target_pairs={{0,8},{4,12},{8,16},{12,20},{16,24},{20,28},{24,0},{28,4},{1,9},{5... | collective-permute-start | bytes 1572872 | tf_op jit(solution)/shard_map/ppermute | solution.py:403
  61.6 0.7 copy-start.6
  62.3 9.3 %copy-start.10 = (bf16[64,512]{1,0:T(8,128)(2,1)}, bf16[64,512]{1,0:T(8,128)(2,1)S(1)}, u32[]{:S(2)}) copy-start(bf16[64,512]{1,0:T(8,128)(2,1)S(1)} %slice.35.some) | copy-start | bytes 196612
  62.3 4.3 %collective-permute-start.14 = (bf16[64,512]{1,0:T(8,128)(2,1)S(1)}, bf16[64,512]{1,0:T(8,128)(2,1)S(1)}, u32[]{:S(2)}, u32[]{:S(2)}) collective-permute-start(bf16[64,512]{1,0:T(8,128)(2,1)S(1)} %slice.35.some), channel_id=1, source_target_pairs={{0,2},{1,3},{2,0},{3,1},{4,6},{5,7},{6,4},{7,5},{8,10},{9,11},{10,... | collective-permute-start | bytes 196616 | tf_op jit(solution)/shard_map/ppermute | solution.py:403
  65.1 7.6 %collective-permute-start.13 = (bf16[64,512]{1,0:T(8,128)(2,1)S(1)}, bf16[64,512]{1,0:T(8,128)(2,1)S(1)}, u32[]{:S(2)}, u32[]{:S(2)}) collective-permute-start(bf16[64,512]{1,0:T(8,128)(2,1)S(1)} %slice.35.some), channel_id=1, source_target_pairs={{0,1},{1,0},{2,3},{3,2},{4,5},{5,4},{6,7},{7,6},{8,9},{9,8},{10,11... | collective-permute-start | bytes 196616 | tf_op jit(solution)/shard_map/ppermute | solution.py:403
  66.5 5.1 %copy-start.13 = (bf16[64,512]{1,0:T(8,128)(2,1)}, bf16[64,512]{1,0:T(8,128)(2,1)S(1)}, u32[]{:S(2)}) copy-start(bf16[64,512]{1,0:T(8,128)(2,1)S(1)} %collective-permute-done.14.some_chip) | copy-start | bytes 196612
  66.5 6.1 %collective-permute-start.15 = (bf16[64,512]{1,0:T(8,128)(2,1)S(1)}, bf16[64,512]{1,0:T(8,128)(2,1)S(1)}, u32[]{:S(2)}, u32[]{:S(2)}) collective-permute-start(bf16[64,512]{1,0:T(8,128)(2,1)S(1)} %collective-permute-done.14.some_chip), channel_id=1, source_target_pairs={{0,1},{1,0},{2,3},{3,2},{4,5},{5,4},{6,7},{7,6},{8,9},{9,8},{10,11... | collective-permute-start | bytes 196616 | tf_op jit(solution)/shard_map/ppermute | solution.py:403
  66.5 1.2 %copy-start.2 = (bf16[256,2048]{1,0:T(8,128)(2,1)S(1)}, bf16[256,2048]{1,0:T(8,128)(2,1)}, u32[]{:S(2)}) copy-start(bf16[256,2048]{1,0:T(8,128)(2,1)} %copy-done.1) | copy-start | bytes 3145732
  67.8 1.1 %copy-start.5 = (bf16[592,512]{1,0:T(8,128)(2,1)S(1)}, bf16[592,512]{1,0:T(8,128)(2,1)}, u32[]{:S(2)}) copy-start(bf16[592,512]{1,0:T(8,128)(2,1)} %get-tuple-element.28.own.refs_0_) | copy-start | bytes 1818628
  68.9 2.8 %copy-start.9 = (bf16[592,512]{1,0:T(8,128)(2,1)S(1)}, bf16[592,512]{1,0:T(8,128)(2,1)}, u32[]{:S(2)}) copy-start(bf16[592,512]{1,0:T(8,128)(2,1)} %copy-done.8) | copy-start | bytes 1818628
  71.6 1.1 copy-start.7
  71.6 1.1 copy-start.16
  71.6 1.1 copy-start.18
  71.6 1.1 copy-start.19
  71.7 11.8 %copy-start.3 = (bf16[256,2048]{1,0:T(8,128)(2,1)S(1)}, bf16[256,2048]{1,0:T(8,128)(2,1)}, u32[]{:S(2)}) copy-start(bf16[256,2048]{1,0:T(8,128)(2,1)} %copy-done.1) | copy-start | bytes 3145732
  72.7 0.8 copy-start.11
  73.6 0.8 copy-start.14
  83.5 8.4 %copy-start.20 = (f32[8]{0:T(128)S(1)}, f32[8]{0:T(128)}, u32[]{:S(2)}) copy-start(f32[8]{0:T(128)} %param.15) | copy-start | bytes 100
  85.5 12.4 %collective-permute-start.17 = (bf16[128,512]{1,0:T(8,128)(2,1)S(1)}, bf16[128,512]{1,0:T(8,128)(2,1)S(1)}, u32[]{:S(2)}, u32[]{:S(2)}) collective-permute-start(bf16[128,512]{1,0:T(8,128)(2,1)S(1)} %get-tuple-element.48), channel_id=1, source_target_pairs={{0,8},{4,12},{8,16},{12,20},{16,24},{20,28},{1,9},{5,13},{9,17},{1... | collective-permute-start | bytes 393224 | tf_op jit(solution)/shard_map/ppermute | solution.py:403
  88.7 9.2 %collective-permute-start.18 = (bf16[128,512]{1,0:T(8,128)(2,1)S(1)}, bf16[128,512]{1,0:T(8,128)(2,1)S(1)}, u32[]{:S(2)}, u32[]{:S(2)}) collective-permute-start(bf16[128,512]{1,0:T(8,128)(2,1)S(1)} %get-tuple-element.48), channel_id=1, source_target_pairs={{0,16},{4,20},{8,24},{12,28},{1,17},{5,21},{9,25},{13,29},{2,18},{... | collective-permute-start | bytes 393224 | tf_op jit(solution)/shard_map/ppermute | solution.py:403
  90.0 7.9 %collective-permute-start.16 = (bf16[16,512]{1,0:T(8,128)(2,1)S(1)}, bf16[16,512]{1,0:T(8,128)(2,1)S(1)}, u32[]{:S(2)}, u32[]{:S(2)}) collective-permute-start(bf16[16,512]{1,0:T(8,128)(2,1)S(1)} %get-tuple-element.47), channel_id=1, source_target_pairs={{0,8},{4,12},{8,16},{12,20},{16,24},{20,28},{1,9},{5,13},{9,17},{1... | collective-permute-start | bytes 49160 | tf_op jit(solution)/shard_map/ppermute | solution.py:403
  91.9 8.6 %copy-start.17 = (s32[4]{0:T(128)S(1)}, s32[4]{0:T(128)}, u32[]{:S(2)}) copy-start(s32[4]{0:T(128)} %pad_add_fusion.place) | copy-start | bytes 52
  98.7 6.4 %collective-permute-start.19 = (bf16[256,512]{1,0:T(8,128)(2,1)S(1)}, bf16[256,512]{1,0:T(8,128)(2,1)S(1)}, u32[]{:S(2)}, u32[]{:S(2)}) collective-permute-start(bf16[256,512]{1,0:T(8,128)(2,1)S(1)} %shard_map.91), channel_id=1, source_target_pairs={{0,4},{4,0},{8,12},{12,8},{16,20},{20,16},{24,28},{28,24},{1,5},{5... | collective-permute-start | bytes 786440 | tf_op jit(solution)/shard_map/ppermute | solution.py:403
